TPU v7x, 512 devices: a whole 4x4x16 slice. The times are simulated.
512 devices in a mesh: grp: 2 (over y_hi), wide: 64 (over y_lo, z, core), narrow: 4 (over x).
Axes of the slice: x: 4, y: 4 (y_hi: 2, y_lo: 2; y = y_hi * 2 + y_lo), z: 16, core: 2. Of those that a mesh axis runs over, the one named last changes fastest.
Arguments:
- hidden: bfloat16 [2048, 3584], P('wide'), may hold values from -6 to 6
- routes: int32 [2048, 8], P('wide'), may hold values from 0 to 63, all different within a row; in each aligned block of 32 rows (0 to 31, 32 to 63, ...) at most 8 rows name the same one
- route_gates: float32 [2048, 8], P('wide'), may hold values from 0.05 to 1
- gate_proj: bfloat16 [64, 3584, 1024], P('wide', None, ('grp', 'narrow')), may hold values from -0.09375 to 0.09375
- up_proj: bfloat16 [64, 3584, 1024], P('wide', None, ('grp', 'narrow')), may hold values from -0.09375 to 0.09375
- down_proj: bfloat16 [64, 1024, 3584], P('wide', ('grp', 'narrow')), may hold values from -0.1875 to 0.1875
Outputs:
- mixed: bfloat16 [2048, 3584], P('wide', ('grp', 'narrow'))
Inputs may be any that keep to these rules, and one draw needn't show every extreme that they name: Each request names 8 different experts; among the routes of the 32 requests of one index of wide no expert is named more than 8 times, and that count is reached.
All inputs are finite; a program needn't handle non-finite values.
Results may differ from a plain program's by a relative error of at most 0.017.
Values may be sent and summed in bfloat16 or wider, within the bound.
No kernel may reach another device: no remote copies, remote signals or barrier semaphores. Data moves between devices by JAX's collectives and lax.ppermute only.
A program may use at most 192 MiB of HBM per device.

v0:
```python
import jax
import jax.numpy as jnp
from jax import lax
from jax.sharding import PartitionSpec as P

EXPERTS = 64
CAP = 8


def per_device(hidden, routes, route_gates, gate_proj, up_proj, down_proj):
    tok_count, top_count = routes.shape
    width = hidden.shape[1]
    local_experts = gate_proj.shape[0]
    capacity = CAP
    route_flat = routes.reshape(-1)
    expert_iota = lax.broadcasted_iota(jnp.int32, (1, EXPERTS), 1)
    one_hot = (route_flat[:, None] == expert_iota).astype(jnp.int32)
    earlier = jnp.cumsum(one_hot, axis=0) - one_hot
    position = jnp.sum(earlier * one_hot, axis=1)
    slot_index = route_flat * capacity + position
    slot_iota = lax.broadcasted_iota(jnp.int32, (EXPERTS * capacity, 1, 1), 0)
    picker = jnp.any(slot_index.reshape(1, tok_count, top_count) == slot_iota, axis=2).astype(
        jnp.bfloat16
    )
    outgoing = jnp.dot(picker, hidden, preferred_element_type=jnp.float32).astype(jnp.bfloat16)
    outgoing = outgoing.reshape(EXPERTS, capacity, width)
    arrived = lax.all_to_all(outgoing, "wide", split_axis=0, concat_axis=0, tiled=True)
    sources = arrived.shape[0] // local_experts
    slots = arrived.shape[1]
    blocks = arrived.reshape(sources, local_experts, slots, width)
    gate_act = jnp.einsum("sjcd,jdh->jsch", blocks, gate_proj, preferred_element_type=jnp.float32)
    up_act = jnp.einsum("sjcd,jdh->jsch", blocks, up_proj, preferred_element_type=jnp.float32)
    inner = (jax.nn.silu(gate_act) * up_act).astype(jnp.bfloat16)
    partial_out = jnp.einsum("jsch,jhd->sjcd", inner, down_proj, preferred_element_type=jnp.float32)
    partial_rows = partial_out.astype(jnp.bfloat16).reshape(sources * local_experts, slots, width)
    gate_column = route_gates.reshape(-1, 1)
    returned = lax.all_to_all(partial_rows, "wide", split_axis=0, concat_axis=0, tiled=True)
    picked = returned.reshape(EXPERTS * capacity, width)[slot_index].astype(jnp.float32)
    weighted = jnp.sum((picked * gate_column).reshape(tok_count, top_count, width), axis=1)
    mixed = lax.psum_scatter(
        weighted.astype(jnp.bfloat16), ("grp", "narrow"), scatter_dimension=1, tiled=True
    )
    return mixed


def solution(mesh):
    return jax.shard_map(
        per_device,
        mesh=mesh,
        in_specs=(
            P("wide", None),
            P("wide", None),
            P("wide", None),
            P("wide", None, ("grp", "narrow")),
            P("wide", None, ("grp", "narrow")),
            P("wide", ("grp", "narrow"), None),
        ),
        out_specs=P("wide", ("grp", "narrow")),
        check_vma=False,
    )
```

profile of v0, /device:TPU:2, one launch (start us, length us, event | category | flops | bytes accessed | tf_op | source)
XLA Modules:
  0.0 476.5 jit_solution(16891105581785389810)
XLA Ops:
  6.5 0.0 copy-start
  6.5 0.8 copy.19
  7.4 0.1 eq.42
  7.5 0.1 eq.38
  7.6 0.6 reduce-window.6
  8.2 0.2 slice_reduce_fusion
  8.4 0.1 fusion.17
  8.5 0.1 reduce_sum.23
  8.6 0.2 fusion.8
  8.9 2.1 fusion
  11.0 0.0 copy-start.3
  11.0 181.1 %all_to_all.10 = bf16[64,8,3584]{2,1,0:T(8,128)(2,1)S(1)} all-to-all(bf16[64,8,3584]{2,1,0:T(8,128)(2,1)S(1)} %fusion), channel_id=1, replica_groups=mesh['grp'=2,'wide'=64,'narrow'=4] {'wide'}, dimensions={0} | all-to-all | bytes 7340032 | tf_op jit(solution)/shard_map/all_to_all | solution.py:27
  192.1 0.0 copy-start.1
  192.1 1.8 copy-done.1
  193.9 0.0 copy-done.3
  193.9 0.0 copy-start.2
  193.9 1.1 fusion.6
  195.0 0.0 copy-done
  195.0 0.1 copy-done.2
  195.1 7.7 %convolution_convert_fusion = bf16[64,8,3584]{2,1,0:T(8,128)(2,1)} fusion(bf16[64,8,3584]{2,1,0:T(8,128)(2,1)} %copy-done.1, bf16[1,128,3584]{2,1,0:T(8,128)(2,1)S(1)} %copy-done, bf16[1,3584,128]{2,1,0:T(8,128)(2,1)S(1)} %copy-done.2, f32[64,8,128]{2,1,0:T(8,128)S(1)} %fusion.6), kind=kOutput, calls=%fused_computation.1 | convolution fusion | flops 941752320 | bytes 9437184 | tf_op jit(solution)/shard_map/jsch,jhd->sjcd/dot_general | solution.py:34
  202.8 0.0 copy-start.4
  202.8 8.7 %all-to-all-start.1 = ((bf16[64,8,3584]{2,1,0:T(8,128)(2,1)}), bf16[64,8,3584]{2,1,0:T(8,128)(2,1)}, u32[]{:S(2)}, u32[]{:S(2)}) async-start(bf16[64,8,3584]{2,1,0:T(8,128)(2,1)} %convolution_convert_fusion), calls=%async_computation.1 | async-start | bytes 7340032 | tf_op jit(solution)/shard_map/all_to_all | solution.py:37
  211.5 0.2 reduce-scatter.4.cloned.1.call-start
  211.7 0.1 mul.44
  211.8 0.0 copy-done.4
  211.8 0.1 copy.23
  211.9 164.8 %all-to-all-done.1 = bf16[64,8,3584]{2,1,0:T(8,128)(2,1)} async-done(((bf16[64,8,3584]{2,1,0:T(8,128)(2,1)}), bf16[64,8,3584]{2,1,0:T(8,128)(2,1)}, u32[]{:S(2)}, u32[]{:S(2)}) %all-to-all-start.1) | async-done | bytes 3670048 | tf_op jit(solution)/shard_map/all_to_all | solution.py:37
  376.8 6.0 %gather_fusion = bf16[256,3584]{1,0:T(8,128)(2,1)S(1)} fusion(bf16[512,3584]{1,0:T(8,128)(2,1)} %bitcast.8, s32[1024]{0:T(1024)S(1)} %pad_clamp_fusion), kind=kCustom, calls=%fused_computation | custom fusion | bytes 3671040 | tf_op jit(solution)/shard_map/gather | solution.py:38
  382.8 1.4 fusion.1
  384.3 1.2 copy.24
  385.5 0.0 reduce-scatter.4.cloned.1.call-update
  385.5 82.5 %reduce-scatter.4.cloned.1.call-done = bf16[448,32]{1,0:T(8,128)(2,1)} async-done(((bf16[3584,32]{1,0:T(8,128)(2,1)}), bf16[448,32]{1,0:T(8,128)(2,1)}) %reduce-scatter.4.cloned.1.call-update) | async-done | bytes 28688
  468.0 1.6 copy.25
  (6 shorter events, 0.1 us)
Async XLA Ops:
  6.5 188.5 %copy-start = (bf16[1,128,3584]{2,1,0:T(8,128)(2,1)S(1)}, bf16[1,128,3584]{2,1,0:T(8,128)(2,1)}, u32[]{:S(2)}) copy-start(bf16[1,128,3584]{2,1,0:T(8,128)(2,1)} %param.11) | copy-start | bytes 2752516
  11.0 182.9 %copy-start.3 = (bf16[1,3584,128]{2,1,0:T(8,128)(2,1)S(1)}, bf16[1,3584,128]{2,1,0:T(8,128)(2,1)}, u32[]{:S(2)}) copy-start(bf16[1,3584,128]{2,1,0:T(8,128)(2,1)} %param.9) | copy-start | bytes 2752516
  192.1 1.8 copy-start.1
  193.9 1.2 copy-start.2
  202.8 9.0 %copy-start.4 = (f32[32,8]{0,1:T(8,128)S(1)}, f32[32,8]{0,1:T(8,128)}, u32[]{:S(2)}) copy-start(f32[32,8]{0,1:T(8,128)} %param.8) | copy-start | bytes 3076
  202.8 173.9 %all-to-all-start.1 = ((bf16[64,8,3584]{2,1,0:T(8,128)(2,1)}), bf16[64,8,3584]{2,1,0:T(8,128)(2,1)}, u32[]{:S(2)}, u32[]{:S(2)}) async-start(bf16[64,8,3584]{2,1,0:T(8,128)(2,1)} %convolution_convert_fusion), calls=%async_computation.1 | async-start | bytes 7340032 | tf_op jit(solution)/shard_map/all_to_all | solution.py:37
  211.5 256.5 %reduce-scatter.4.cloned.1.call-start = ((), (), s32[]{:S(2)}) async-start(), calls=%async_computation.3 | async-start | bytes 1032192
Sparse Core Ops, SparseCore 0:
  385.7 82.3 reduce-scatter.3
where the time goes:
time: 477 us; the launch traced here: 476 us
  waiting for transfers between devices  247 us (52%)
  blocking collectives  181 us (38%)
  between operations  13.5 us (3%)
  local copies, waits for them, and re-layouts  12.2 us (3%)
  matrix products  11 us (2%)
  starting transfers between devices  8.89 us (2%)
    all_to_all x1, blocking collectives, per_device(): lax.all_to_all(outgoing, 'wide', split_axis=0, concat_axis=0, tiled=True)  181 us
    all_to_all x1, waiting for transfers between devices, per_device(): lax.all_to_all(partial_rows, 'wide', split_axis=0, concat_axis=0, tiled=T...  165 us
    unnamed x2, waiting for transfers between devices  82.5 us
  transfers between devices with their start and end apart: 2, of which 2 were waited for; matrix products, arithmetic and copies ran while one was open for 0% of the time, Pallas kernels for 0%

commit v1 on v0

v1 whole, which is shorter than its diff:
```python
import jax
import jax.numpy as jnp
from jax import lax
from jax.sharding import PartitionSpec as P

EXPERTS = 64
CAP = 8
F32 = jnp.float32
BF16 = jnp.bfloat16


def exchange(x, axis):
    return lax.all_to_all(x, axis, split_axis=0, concat_axis=0, tiled=True)


def per_device(hidden, routes, route_gates, gate_proj, up_proj, down_proj):
    tok, width = hidden.shape
    n_grp, n_nar = lax.axis_size("grp"), lax.axis_size("narrow")
    g, n = lax.axis_index("grp"), lax.axis_index("narrow")
    units = gate_proj.shape[2]
    part = width // (n_grp * n_nar)
    slots = EXPERTS * CAP

    gate_up = jnp.concatenate([gate_proj[0], up_proj[0]], axis=1).reshape(n_nar, n_grp, part, 2 * units)
    down = down_proj[0].reshape(units, n_grp, n_nar, part)
    gu_parts, down_parts = [], []
    for k in range(n_nar):
        to = lax.rem(n + k, n_nar)
        gu = lax.dynamic_index_in_dim(gate_up, to, 0, keepdims=False)
        dn = lax.dynamic_index_in_dim(down, to, 2, keepdims=False)
        if k:
            pairs = [(i, (i + k) % n_nar) for i in range(n_nar)]
            gu = lax.ppermute(gu, "narrow", pairs)
            dn = lax.ppermute(dn, "narrow", pairs)
        gu_parts.append(gu)
        down_parts.append(dn)

    experts = lax.broadcasted_iota(jnp.int32, (EXPERTS, 1, 1), 0)
    match = routes.T[None] == experts
    chosen = jnp.any(match, axis=1)
    gates = jnp.sum(jnp.where(match, route_gates.T[None], 0.0), axis=1)
    before = (
        lax.broadcasted_iota(jnp.int32, (tok, tok), 0) < lax.broadcasted_iota(jnp.int32, (tok, tok), 1)
    ).astype(BF16)
    place = jnp.dot(chosen.astype(BF16), before, preferred_element_type=F32)
    slot = lax.broadcasted_iota(jnp.int32, (1, CAP, 1), 1).astype(F32)
    picked = (place[:, None] == slot) & chosen[:, None]
    picker = picked.astype(BF16).reshape(slots, tok)
    weight = jnp.where(picked, gates[:, None], 0.0).reshape(slots, tok)
    weight_hi = weight.astype(BF16)
    weight_lo = (weight - weight_hi.astype(F32)).astype(BF16)
    weights = jnp.concatenate([weight_hi, weight_lo], axis=1)

    mine = lax.dynamic_slice_in_dim(hidden, (n * n_grp + g) * part, part, 1)
    outgoing = jnp.dot(picker, mine, preferred_element_type=F32).astype(BF16)
    rows = exchange(outgoing.reshape(EXPERTS, CAP, part), "wide").reshape(1, slots, part)
    rows = exchange(jnp.broadcast_to(rows, (n_grp, slots, part)), "grp")

    acts = jnp.zeros((n_nar, slots, 2 * units), BF16)
    for k in range(n_nar):
        act = sum(jnp.dot(rows[i], gu_parts[k][i], preferred_element_type=F32) for i in range(n_grp))
        acts = lax.dynamic_update_index_in_dim(acts, act.astype(BF16), lax.rem(n - k + n_nar, n_nar), 0)
    act = jnp.sum(exchange(acts, "narrow").astype(F32), axis=0)
    inner = (jax.nn.silu(act[:, :units]) * act[:, units:]).astype(BF16)
    inners = exchange(jnp.broadcast_to(inner[None], (n_nar, slots, units)), "narrow")

    outs = []
    for i in range(n_grp):
        out = 0.0
        for k in range(n_nar):
            left = lax.dynamic_index_in_dim(inners, lax.rem(n - k + n_nar, n_nar), 0, keepdims=False)
            out = out + jnp.dot(left, down_parts[k][:, i], preferred_element_type=F32)
        outs.append(out.astype(BF16))
    out = jnp.sum(exchange(jnp.stack(outs), "grp").astype(F32), axis=0).astype(BF16)
    back = exchange(out.reshape(EXPERTS, CAP, part), "wide").reshape(slots, part)
    mixed = lax.dot_general(weights, back, (((0,), (0,)), ((), ())), preferred_element_type=F32)
    return (mixed[:tok] + mixed[tok:]).astype(BF16)


def solution(mesh):
    return jax.shard_map(
        per_device,
        mesh=mesh,
        in_specs=(
            P("wide", None),
            P("wide", None),
            P("wide", None),
            P("wide", None, ("grp", "narrow")),
            P("wide", None, ("grp", "narrow")),
            P("wide", ("grp", "narrow"), None),
        ),
        out_specs=P("wide", ("grp", "narrow")),
        check_vma=False,
    )
```

time: 477 us -> 189 us (0.40)
  the two profiles are of different devices: /device:TPU:2 before, /device:TPU:1 now
where the time goes in v1:
time: 189 us; the launch traced here: 188 us
  blocking collectives  83.8 us (44%)
  waiting for transfers between devices  53.3 us (28%)
  starting transfers between devices  36.1 us (19%)
  matrix products  5.89 us (3%)
  local copies, waits for them, and re-layouts  4.71 us (2%)
  other arithmetic  4.23 us (2%)
    all_to_all x3, blocking collectives, exchange(): return lax.all_to_all(x, axis, split_axis=0, concat_axis=0, tiled=True)  83.8 us
    all_to_all x3, waiting for transfers between devices, exchange(): return lax.all_to_all(x, axis, split_axis=0, concat_axis=0, tiled=True)  33.3 us
    all_to_all x3, starting transfers between devices, exchange(): return lax.all_to_all(x, axis, split_axis=0, concat_axis=0, tiled=True)  15.4 us
    ppermute x3, waiting for transfers between devices, per_device(): gu = lax.ppermute(gu, 'narrow', pairs)  14.3 us
    ppermute x3, starting transfers between devices, per_device(): gu = lax.ppermute(gu, 'narrow', pairs)  10.5 us
    ppermute x3, starting transfers between devices, per_device(): dn = lax.ppermute(dn, 'narrow', pairs)  10.1 us
    ppermute x3, waiting for transfers between devices, per_device(): dn = lax.ppermute(dn, 'narrow', pairs)  5.7 us
  transfers between devices with their start and end apart: 9, of which 7 were waited for; matrix products, arithmetic and copies ran while one was open for 2% of the time, Pallas kernels for 0%

profile of v1, /device:TPU:1, one launch (start us, length us, event | category | flops | bytes accessed | tf_op | source)
XLA Modules:
  0.0 188.4 jit_solution(1974748749809358159)
XLA Ops:
  0.0 0.8 fusion.44
  0.8 0.2 fusion.58
  1.2 0.8 select_reduce_fusion
  2.7 0.4 convolution_convert_fusion
  3.1 0.2 copy.38
  3.3 49.6 %all_to_all.30 = bf16[64,8,448]{2,1,0:T(8,128)(2,1)S(1)} all-to-all(bf16[64,8,448]{2,1,0:T(8,128)(2,1)S(1)} %bitcast.134), channel_id=1, replica_groups=mesh['grp'=2,'wide'=64,'narrow'=4] {'wide'}, dimensions={0} | all-to-all | bytes 917504 | tf_op jit(solution)/shard_map/all_to_all | solution.py:13
  53.1 1.0 broadcast_in_dim.67
  54.1 4.0 %all-to-all-start.1 = ((bf16[2,512,448]{1,2,0:T(8,128)(2,1)}), bf16[2,512,448]{1,2,0:T(8,128)(2,1)S(1)}, u32[]{:S(2)}, u32[]{:S(2)}) async-start(bf16[2,512,448]{1,2,0:T(8,128)(2,1)} %broadcast_in_dim.67), calls=%async_computation.1 | async-start | bytes 1835008 | tf_op jit(solution)/shard_map/all_to_all | solution.py:13
  58.2 1.2 fusion.21
  59.3 3.1 %collective-permute-start = (bf16[2,448,256]{2,1,0:T(8,128)(2,1)}, bf16[2,448,256]{2,1,0:T(8,128)(2,1)S(1)}, u32[]{:S(2)}, u32[]{:S(2)}) collective-permute-start(bf16[2,448,256]{2,1,0:T(8,128)(2,1)} %get-tuple-element.9), channel_id=1, source_target_pairs={{0,1},{1,2},{2,3},{3,0},{4,5},{5,6},{6,7},{7,4},{8,9},{9,10},{10,1... | collective-permute-start | bytes 1376264 | tf_op jit(solution)/shard_map/ppermute | solution.py:33
  62.4 4.4 %collective-permute-start.1 = (bf16[2,448,256]{2,1,0:T(8,128)(2,1)}, bf16[2,448,256]{2,1,0:T(8,128)(2,1)S(1)}, u32[]{:S(2)}, u32[]{:S(2)}) collective-permute-start(bf16[2,448,256]{2,1,0:T(8,128)(2,1)} %get-tuple-element.10), channel_id=1, source_target_pairs={{0,2},{1,3},{2,0},{3,1},{4,6},{5,7},{6,4},{7,5},{8,10},{9,11},{10,... | collective-permute-start | bytes 1376264 | tf_op jit(solution)/shard_map/ppermute | solution.py:33
  66.8 3.1 %collective-permute-start.2 = (bf16[2,448,256]{2,1,0:T(8,128)(2,1)}, bf16[2,448,256]{2,1,0:T(8,128)(2,1)S(1)}, u32[]{:S(2)}, u32[]{:S(2)}) collective-permute-start(bf16[2,448,256]{2,1,0:T(8,128)(2,1)} %get-tuple-element.7), channel_id=1, source_target_pairs={{0,3},{1,0},{2,1},{3,2},{4,7},{5,4},{6,5},{7,6},{8,11},{9,8},{10,9... | collective-permute-start | bytes 1376264 | tf_op jit(solution)/shard_map/ppermute | solution.py:33
  69.9 1.6 all-to-all-done.1
  71.5 0.3 fusion.27
  71.9 2.4 %collective-permute-done = bf16[2,448,256]{2,1,0:T(8,128)(2,1)S(1)} collective-permute-done((bf16[2,448,256]{2,1,0:T(8,128)(2,1)}, bf16[2,448,256]{2,1,0:T(8,128)(2,1)S(1)}, u32[]{:S(2)}, u32[]{:S(2)}) %collective-permute-start) | collective-permute-done | bytes 458784 | tf_op jit(solution)/shard_map/ppermute | solution.py:33
  74.3 0.3 fusion.30
  74.6 10.5 %collective-permute-done.1 = bf16[2,448,256]{2,1,0:T(8,128)(2,1)S(1)} collective-permute-done((bf16[2,448,256]{2,1,0:T(8,128)(2,1)}, bf16[2,448,256]{2,1,0:T(8,128)(2,1)S(1)}, u32[]{:S(2)}, u32[]{:S(2)}) %collective-permute-start.1) | collective-permute-done | bytes 458784 | tf_op jit(solution)/shard_map/ppermute | solution.py:33
  85.1 0.3 fusion.29
  85.5 1.5 collective-permute-done.2
  86.9 0.3 fusion.28
  87.4 0.4 fusion.17
  87.7 0.4 fusion.15
  88.1 0.4 fusion.13
  88.4 0.4 fusion.11
  88.8 18.0 %all_to_all.31 = bf16[4,512,256]{2,1,0:T(8,128)(2,1)S(1)} all-to-all(bf16[4,512,256]{2,1,0:T(8,128)(2,1)S(1)} %fusion.11), channel_id=1, replica_groups=mesh['grp'=2,'wide'=64,'narrow'=4] {'narrow'}, dimensions={0} | all-to-all | bytes 2097152 | tf_op jit(solution)/shard_map/all_to_all | solution.py:13
  107.1 0.9 broadcast_in_dim.72
  107.9 3.5 %all-to-all-start.3 = ((bf16[4,512,128]{2,1,0:T(8,128)(2,1)}), bf16[4,512,128]{2,1,0:T(8,128)(2,1)S(1)}, u32[]{:S(2)}, u32[]{:S(2)}) async-start(bf16[4,512,128]{2,1,0:T(8,128)(2,1)} %broadcast_in_dim.72), calls=%async_computation.3 | async-start | bytes 1048576 | tf_op jit(solution)/shard_map/all_to_all | solution.py:13
  111.4 0.6 copy.40
  112.1 3.3 %collective-permute-start.3 = (bf16[128,2,448]{0,2,1:T(8,128)(2,1)S(1)}, bf16[128,2,448]{0,2,1:T(8,128)(2,1)S(1)}, u32[]{:S(2)}, u32[]{:S(2)}) collective-permute-start(bf16[128,2,448]{0,2,1:T(8,128)(2,1)S(1)} %get-tuple-element.13), channel_id=1, source_target_pairs={{0,1},{1,2},{2,3},{3,0},{4,5},{5,6},{6,7},{7,4},{8,9},{9,10},{10,1... | collective-permute-start | bytes 688136 | tf_op jit(solution)/shard_map/ppermute | solution.py:34
  115.4 3.2 %collective-permute-start.5 = (bf16[128,2,448]{0,2,1:T(8,128)(2,1)S(1)}, bf16[128,2,448]{0,2,1:T(8,128)(2,1)S(1)}, u32[]{:S(2)}, u32[]{:S(2)}) collective-permute-start(bf16[128,2,448]{0,2,1:T(8,128)(2,1)S(1)} %get-tuple-element.12), channel_id=1, source_target_pairs={{0,3},{1,0},{2,1},{3,2},{4,7},{5,4},{6,5},{7,6},{8,11},{9,8},{10,9... | collective-permute-start | bytes 688136 | tf_op jit(solution)/shard_map/ppermute | solution.py:34
  118.6 3.6 %collective-permute-start.4 = (bf16[128,2,448]{0,2,1:T(8,128)(2,1)S(1)}, bf16[128,2,448]{0,2,1:T(8,128)(2,1)S(1)}, u32[]{:S(2)}, u32[]{:S(2)}) collective-permute-start(bf16[128,2,448]{0,2,1:T(8,128)(2,1)S(1)} %get-tuple-element.11), channel_id=1, source_target_pairs={{0,2},{1,3},{2,0},{3,1},{4,6},{5,7},{6,4},{7,5},{8,10},{9,11},{10,... | collective-permute-start | bytes 688136 | tf_op jit(solution)/shard_map/ppermute | solution.py:34
  122.3 0.3 fusion.42
  122.6 0.3 fusion.40
  122.8 0.3 fusion.34
  123.1 1.9 %collective-permute-done.3 = bf16[128,2,448]{0,2,1:T(8,128)(2,1)S(1)} collective-permute-done((bf16[128,2,448]{0,2,1:T(8,128)(2,1)S(1)}, bf16[128,2,448]{0,2,1:T(8,128)(2,1)S(1)}, u32[]{:S(2)}, u32[]{:S(2)}) %collective-permute-start.3) | collective-permute-done | bytes 229408 | tf_op jit(solution)/shard_map/ppermute | solution.py:34
  125.0 0.3 convolution_add_fusion.3
  125.3 0.3 convolution_add_fusion.1
  125.6 0.3 fusion.32
  125.9 3.8 %collective-permute-done.4 = bf16[128,2,448]{0,2,1:T(8,128)(2,1)S(1)} collective-permute-done((bf16[128,2,448]{0,2,1:T(8,128)(2,1)S(1)}, bf16[128,2,448]{0,2,1:T(8,128)(2,1)S(1)}, u32[]{:S(2)}, u32[]{:S(2)}) %collective-permute-start.4) | collective-permute-done | bytes 229408 | tf_op jit(solution)/shard_map/ppermute | solution.py:34
  129.7 0.3 fusion.5
  130.0 0.3 fusion.4
  130.4 16.1 %all_to_all.32 = bf16[2,512,448]{1,2,0:T(8,128)(2,1)S(1)} all-to-all(bf16[2,512,448]{1,2,0:T(8,128)(2,1)S(1)} %pad_maximum_fusion), channel_id=1, replica_groups=mesh['grp'=2,'wide'=64,'narrow'=4] {'grp'}, dimensions={0} | all-to-all | bytes 1835008 | tf_op jit(solution)/shard_map/all_to_all | solution.py:13
  146.5 0.4 reduce_sum.32
  146.9 1.0 copy.41
  147.9 7.9 %all-to-all-start.5 = ((bf16[64,8,448]{2,1,0:T(8,128)(2,1)}), bf16[64,8,448]{2,1,0:T(8,128)(2,1)S(1)}, u32[]{:S(2)}, u32[]{:S(2)}) async-start(bf16[64,8,448]{2,1,0:T(8,128)(2,1)} %bitcast.45), calls=%async_computation.5 | async-start | bytes 1048576 | tf_op jit(solution)/shard_map/all_to_all | solution.py:13
  155.9 31.7 %all-to-all-done.5 = bf16[64,8,448]{2,1,0:T(8,128)(2,1)S(1)} async-done(((bf16[64,8,448]{2,1,0:T(8,128)(2,1)}), bf16[64,8,448]{2,1,0:T(8,128)(2,1)S(1)}, u32[]{:S(2)}, u32[]{:S(2)}) %all-to-all-start.5) | async-done | bytes 458784 | tf_op jit(solution)/shard_map/all_to_all | solution.py:13
  187.5 0.2 fusion.18
  187.7 0.6 fusion.53
  (29 shorter events, 1.4 us)
Async XLA Ops:
  0.0 2.6 %copy-start = (bf16[32,3584]{1,0:T(8,128)(2,1)S(1)}, bf16[32,3584]{1,0:T(8,128)(2,1)}, u32[]{:S(2)}) copy-start(bf16[32,3584]{1,0:T(8,128)(2,1)} %param.6) | copy-start | bytes 688132
  54.1 4.0 %copy-start.2 = (bf16[1,3584,128]{2,1,0:T(8,128)(2,1)S(1)}, bf16[1,3584,128]{2,1,0:T(8,128)(2,1)}, u32[]{:S(2)}) copy-start(bf16[1,3584,128]{2,1,0:T(8,128)(2,1)} %param.9) | copy-start | bytes 2752516
  54.1 4.0 %copy-start.3 = (bf16[1,3584,128]{2,1,0:T(8,128)(2,1)S(1)}, bf16[1,3584,128]{2,1,0:T(8,128)(2,1)}, u32[]{:S(2)}) copy-start(bf16[1,3584,128]{2,1,0:T(8,128)(2,1)} %param.10) | copy-start | bytes 2752516
  54.1 17.4 %all-to-all-start.1 = ((bf16[2,512,448]{1,2,0:T(8,128)(2,1)}), bf16[2,512,448]{1,2,0:T(8,128)(2,1)S(1)}, u32[]{:S(2)}, u32[]{:S(2)}) async-start(bf16[2,512,448]{1,2,0:T(8,128)(2,1)} %broadcast_in_dim.67), calls=%async_computation.1 | async-start | bytes 1835008 | tf_op jit(solution)/shard_map/all_to_all | solution.py:13
  59.3 15.0 %collective-permute-start = (bf16[2,448,256]{2,1,0:T(8,128)(2,1)}, bf16[2,448,256]{2,1,0:T(8,128)(2,1)S(1)}, u32[]{:S(2)}, u32[]{:S(2)}) collective-permute-start(bf16[2,448,256]{2,1,0:T(8,128)(2,1)} %get-tuple-element.9), channel_id=1, source_target_pairs={{0,1},{1,2},{2,3},{3,0},{4,5},{5,6},{6,7},{7,4},{8,9},{9,10},{10,1... | collective-permute-start | bytes 1376264 | tf_op jit(solution)/shard_map/ppermute | solution.py:33
  62.4 22.7 %collective-permute-start.1 = (bf16[2,448,256]{2,1,0:T(8,128)(2,1)}, bf16[2,448,256]{2,1,0:T(8,128)(2,1)S(1)}, u32[]{:S(2)}, u32[]{:S(2)}) collective-permute-start(bf16[2,448,256]{2,1,0:T(8,128)(2,1)} %get-tuple-element.10), channel_id=1, source_target_pairs={{0,2},{1,3},{2,0},{3,1},{4,6},{5,7},{6,4},{7,5},{8,10},{9,11},{10,... | collective-permute-start | bytes 1376264 | tf_op jit(solution)/shard_map/ppermute | solution.py:33
  66.8 20.1 %collective-permute-start.2 = (bf16[2,448,256]{2,1,0:T(8,128)(2,1)}, bf16[2,448,256]{2,1,0:T(8,128)(2,1)S(1)}, u32[]{:S(2)}, u32[]{:S(2)}) collective-permute-start(bf16[2,448,256]{2,1,0:T(8,128)(2,1)} %get-tuple-element.7), channel_id=1, source_target_pairs={{0,3},{1,0},{2,1},{3,2},{4,7},{5,4},{6,5},{7,6},{8,11},{9,8},{10,9... | collective-permute-start | bytes 1376264 | tf_op jit(solution)/shard_map/ppermute | solution.py:33
  107.0 4.4 %copy-start.1 = (bf16[1,128,3584]{2,1,0:T(8,128)(2,1)S(1)}, bf16[1,128,3584]{2,1,0:T(8,128)(2,1)}, u32[]{:S(2)}) copy-start(bf16[1,128,3584]{2,1,0:T(8,128)(2,1)} %param.11) | copy-start | bytes 2752516
  107.9 14.3 %all-to-all-start.3 = ((bf16[4,512,128]{2,1,0:T(8,128)(2,1)}), bf16[4,512,128]{2,1,0:T(8,128)(2,1)S(1)}, u32[]{:S(2)}, u32[]{:S(2)}) async-start(bf16[4,512,128]{2,1,0:T(8,128)(2,1)} %broadcast_in_dim.72), calls=%async_computation.3 | async-start | bytes 1048576 | tf_op jit(solution)/shard_map/all_to_all | solution.py:13
  112.1 12.9 %collective-permute-start.3 = (bf16[128,2,448]{0,2,1:T(8,128)(2,1)S(1)}, bf16[128,2,448]{0,2,1:T(8,128)(2,1)S(1)}, u32[]{:S(2)}, u32[]{:S(2)}) collective-permute-start(bf16[128,2,448]{0,2,1:T(8,128)(2,1)S(1)} %get-tuple-element.13), channel_id=1, source_target_pairs={{0,1},{1,2},{2,3},{3,0},{4,5},{5,6},{6,7},{7,4},{8,9},{9,10},{10,1... | collective-permute-start | bytes 688136 | tf_op jit(solution)/shard_map/ppermute | solution.py:34
  115.4 7.4 %collective-permute-start.5 = (bf16[128,2,448]{0,2,1:T(8,128)(2,1)S(1)}, bf16[128,2,448]{0,2,1:T(8,128)(2,1)S(1)}, u32[]{:S(2)}, u32[]{:S(2)}) collective-permute-start(bf16[128,2,448]{0,2,1:T(8,128)(2,1)S(1)} %get-tuple-element.12), channel_id=1, source_target_pairs={{0,3},{1,0},{2,1},{3,2},{4,7},{5,4},{6,5},{7,6},{8,11},{9,8},{10,9... | collective-permute-start | bytes 688136 | tf_op jit(solution)/shard_map/ppermute | solution.py:34
  118.6 11.1 %collective-permute-start.4 = (bf16[128,2,448]{0,2,1:T(8,128)(2,1)S(1)}, bf16[128,2,448]{0,2,1:T(8,128)(2,1)S(1)}, u32[]{:S(2)}, u32[]{:S(2)}) collective-permute-start(bf16[128,2,448]{0,2,1:T(8,128)(2,1)S(1)} %get-tuple-element.11), channel_id=1, source_target_pairs={{0,2},{1,3},{2,0},{3,1},{4,6},{5,7},{6,4},{7,5},{8,10},{9,11},{10,... | collective-permute-start | bytes 688136 | tf_op jit(solution)/shard_map/ppermute | solution.py:34
  147.9 39.6 %all-to-all-start.5 = ((bf16[64,8,448]{2,1,0:T(8,128)(2,1)}), bf16[64,8,448]{2,1,0:T(8,128)(2,1)S(1)}, u32[]{:S(2)}, u32[]{:S(2)}) async-start(bf16[64,8,448]{2,1,0:T(8,128)(2,1)} %bitcast.45), calls=%async_computation.5 | async-start | bytes 1048576 | tf_op jit(solution)/shard_map/all_to_all | solution.py:13

commit v2 on v1

v2 whole, which is shorter than its diff:
```python
import functools

import jax
import jax.numpy as jnp
from jax import lax
from jax.experimental import pallas as pl
from jax.experimental.pallas import tpu as pltpu
from jax.sharding import Mesh, PartitionSpec as P

CAP = 8
F32 = jnp.float32
BF16 = jnp.bfloat16
I32 = jnp.int32
FAR = "zfar"
NEAR = ("grp", "ylo", "znear", "core")
AXES = ("grp", "ylo", "zfar", "znear", "core", "narrow")
WIDE = ("ylo", "zfar", "znear", "core")
LANES = 512

VMEM = pl.BlockSpec(memory_space=pltpu.VMEM)
SMEM = pl.BlockSpec(memory_space=pltpu.SMEM)
ANY = pl.BlockSpec(memory_space=pl.ANY)


def call(body, outs, specs, args, flops=0):
    single = not isinstance(outs, list)
    outs = [outs] if single else outs
    nbytes = sum(a.size * a.dtype.itemsize for a in args) + sum(o.size * o.dtype.itemsize for o in outs)
    got = pl.pallas_call(
        body,
        out_shape=outs,
        in_specs=specs,
        out_specs=[VMEM] * len(outs),
        compiler_params=pltpu.CompilerParams(vmem_limit_bytes=40 * 1024 * 1024),
        cost_estimate=pl.CostEstimate(flops=flops, bytes_accessed=nbytes, transcendentals=0),
    )(*args)
    return got[0] if single else got


def exchange(x, axis):
    return lax.all_to_all(x, axis, split_axis=0, concat_axis=0, tiled=True)


def pick_body(part, top, far_ref, rows_ref, *rest):
    out_ref, weight_ref = rest[-2:]
    blocks, tok, _ = rows_ref.shape
    count = blocks * tok
    rows = rows_ref[...].reshape(count, LANES)
    extra = rows[:, part : part + 3 * top]
    eye = (
        lax.broadcasted_iota(I32, (3 * top, 3 * top), 0) == lax.broadcasted_iota(I32, (3 * top, 3 * top), 1)
    ).astype(BF16)
    extra = lax.dot_general(eye, extra, (((1,), (1,)), ((), ())), preferred_element_type=F32)
    j = lax.broadcasted_iota(I32, (8, count), 0)
    z_count = 2 * lax.axis_size(FAR)
    expert = (((j // 4) * z_count + far_ref[0] * 2 + (j // 2) % 2) * 2 + j % 2).astype(F32)
    chosen = jnp.zeros((8, count), F32)
    gate = jnp.zeros((8, count), F32)
    for k in range(top):
        same = extra[k : k + 1] == expert
        chosen = jnp.where(same, 1.0, chosen)
        value = extra[top + k : top + k + 1] + extra[2 * top + k : 2 * top + k + 1]
        gate = gate + jnp.where(same, value, 0.0)
    first = lax.broadcasted_iota(I32, (count, count), 0)
    second = lax.broadcasted_iota(I32, (count, count), 1)
    before = ((first < second) & (first // tok == second // tok)).astype(BF16)
    place = jnp.dot(chosen.astype(BF16), before, preferred_element_type=F32)
    block = (lax.broadcasted_iota(I32, (8, count), 1) // tok).astype(F32)
    slot = jnp.where(chosen > 0.0, place + block * CAP, -1.0)
    want = lax.broadcasted_iota(I32, (8, blocks * CAP, count), 1).astype(F32)
    hit = slot[:, None, :] == want
    picker = jnp.where(hit, 1.0, 0.0).astype(BF16).reshape(8 * blocks * CAP, count)
    weight = jnp.where(hit, gate[:, None, :], 0.0).reshape(8 * blocks * CAP, count)
    high = weight.astype(BF16)
    weight_ref[:, :count] = high
    weight_ref[:, count:] = (weight - high.astype(F32)).astype(BF16)
    got = jnp.dot(picker, rows[:, :part], preferred_element_type=F32).astype(BF16)
    got = got.reshape(8, blocks * CAP, part)
    out_ref[:8] = got
    out_ref[8:] = got


def gate_up_body(n_nar, me_ref, rows_ref, *rest):
    parts, out_ref = rest[:n_nar], rest[-1]
    slots, part = out_ref.shape[1], rows_ref.shape[2]
    half = rows_ref.shape[0] // 2
    left = rows_ref[:half].reshape(slots, part)
    right = rows_ref[half:].reshape(slots, part)
    for k in range(n_nar):
        act = jnp.dot(left, parts[k][0], preferred_element_type=F32)
        act = act + jnp.dot(right, parts[k][1], preferred_element_type=F32)
        out_ref[lax.rem(me_ref[0] - k + n_nar, n_nar)] = act.astype(BF16)


def inner_body(acts_ref, out_ref):
    count, _, units = out_ref.shape
    act = sum(acts_ref[i].astype(F32) for i in range(count))
    gate, up = act[:, :units], act[:, units:]
    inner = (gate / (1.0 + jnp.exp(-gate)) * up).astype(BF16)
    for i in range(count):
        out_ref[i] = inner


def down_body(n_nar, me_ref, inner_ref, *rest):
    parts, out_ref = rest[:n_nar], rest[-1]
    half = out_ref.shape[0] // 2
    for i in range(2):
        out = 0.0
        for k in range(n_nar):
            left = inner_ref[lax.rem(me_ref[0] - k + n_nar, n_nar)]
            out = out + jnp.dot(left, parts[k][i], preferred_element_type=F32)
        out = out.astype(BF16)
        out_ref[i * half : (i + 1) * half] = out.reshape(half, -1, out.shape[1])


def combine_body(rows_ref, weight_ref, out_ref):
    blocks, tok, part = out_ref.shape
    half = rows_ref.shape[0] // 2
    weight = weight_ref[...]
    total = 0.0
    for i in range(2):
        rows = rows_ref[i * half : (i + 1) * half].reshape(weight.shape[0], part)
        total = total + lax.dot_general(weight, rows, (((0,), (0,)), ((), ())), preferred_element_type=F32)
    count = blocks * tok
    out_ref[...] = (total[:count] + total[count:]).astype(BF16).reshape(blocks, tok, part)


def per_device(hidden, routes, route_gates, gate_proj, up_proj, down_proj):
    tok, width = hidden.shape
    top = routes.shape[1]
    n_grp, n_nar, n_far = lax.axis_size("grp"), lax.axis_size("narrow"), lax.axis_size(FAR)
    g, n = lax.axis_index("grp"), lax.axis_index("narrow")
    me = n.astype(I32).reshape(1)
    far = lax.axis_index(FAR).astype(I32).reshape(1)
    units = gate_proj.shape[2]
    part = width // (n_grp * n_nar)
    near = 16
    slots = 8 * n_far * CAP

    mine = lax.dynamic_slice_in_dim(hidden, (n * n_grp + g) * part, part, 1)
    gate_hi = route_gates.astype(BF16)
    gate_lo = (route_gates - gate_hi.astype(F32)).astype(BF16)
    spare = jnp.zeros((tok, LANES - part - 3 * top), BF16)
    rows = jnp.concatenate([mine, routes.astype(BF16), gate_hi, gate_lo, spare], axis=1)
    rows = exchange(jnp.broadcast_to(rows[None], (n_far, tok, LANES)), FAR)

    gate_up = jnp.concatenate([gate_proj[0], up_proj[0]], axis=1).reshape(n_nar, n_grp, part, 2 * units)
    down = down_proj[0].reshape(units, n_grp, n_nar, part).transpose(2, 1, 0, 3)
    gu_parts, down_parts = [], []
    for k in range(n_nar):
        to = lax.rem(n + k, n_nar)
        gu = lax.dynamic_index_in_dim(gate_up, to, 0, keepdims=False)
        dn = lax.dynamic_index_in_dim(down, to, 0, keepdims=False)
        if k:
            pairs = [(i, (i + k) % n_nar) for i in range(n_nar)]
            gu = lax.ppermute(gu, "narrow", pairs)
            dn = lax.ppermute(dn, "narrow", pairs)
        gu_parts.append(gu)
        down_parts.append(dn)

    picked, weight = call(
        functools.partial(pick_body, part, top),
        [
            jax.ShapeDtypeStruct((near, n_far * CAP, part), BF16),
            jax.ShapeDtypeStruct((slots, 2 * n_far * tok), BF16),
        ],
        [SMEM, VMEM] + [ANY] * (n_nar - 1),
        [far, rows] + gu_parts[1:],
        flops=2 * slots * n_far * tok * part,
    )
    rows = exchange(picked, NEAR)

    acts = call(
        functools.partial(gate_up_body, n_nar),
        jax.ShapeDtypeStruct((n_nar, slots, 2 * units), BF16),
        [SMEM, VMEM] + [VMEM] * n_nar + [ANY] * (n_nar - 1),
        [me, rows] + gu_parts + down_parts[1:],
        flops=2 * slots * part * 2 * units * 2 * n_nar,
    )
    acts = exchange(acts, "narrow")
    inner = call(inner_body, jax.ShapeDtypeStruct((n_nar, slots, units), BF16), [VMEM], [acts])
    inner = exchange(inner, "narrow")
    outs = call(
        functools.partial(down_body, n_nar),
        jax.ShapeDtypeStruct((near, n_far * CAP, part), BF16),
        [SMEM, VMEM] + [VMEM] * n_nar,
        [me, inner] + down_parts,
        flops=2 * slots * units * n_nar * 2 * part,
    )
    outs = exchange(outs, NEAR)
    sums = call(
        combine_body,
        jax.ShapeDtypeStruct((n_far, tok, part), BF16),
        [VMEM, VMEM],
        [outs, weight],
        flops=2 * slots * 2 * 2 * n_far * tok * part,
    )
    sums = exchange(sums, FAR)
    return jnp.sum(sums.astype(F32), axis=0).astype(BF16)


def solution(mesh):
    n_grp, n_wide, n_nar = mesh.devices.shape
    fine = Mesh(mesh.devices.reshape(n_grp, 2, n_wide // 8, 2, 2, n_nar), AXES)
    return jax.shard_map(
        per_device,
        mesh=fine,
        in_specs=(
            P(WIDE, None),
            P(WIDE, None),
            P(WIDE, None),
            P(WIDE, None, ("grp", "narrow")),
            P(WIDE, None, ("grp", "narrow")),
            P(WIDE, ("grp", "narrow"), None),
        ),
        out_specs=P(WIDE, ("grp", "narrow")),
        check_vma=False,
    )
```

time: 189 us -> 174 us (0.921)
  the two profiles are of different devices: /device:TPU:1 before, /device:TPU:2 now
where the time goes in v2:
time: 174 us
  blocking collectives  71.5 us (41%)
  starting transfers between devices  45 us (26%)
  waiting for transfers between devices  33.1 us (19%)
  local copies, waits for them, and re-layouts  13.6 us (8%)
  Pallas kernels  5.79 us (3%)
  other arithmetic  4.44 us (3%)
    all_to_all x3, blocking collectives, exchange(): return lax.all_to_all(x, axis, split_axis=0, concat_axis=0, tiled=True)  71.5 us
    all_to_all x3, starting transfers between devices, exchange(): return lax.all_to_all(x, axis, split_axis=0, concat_axis=0, tiled=True)  25.1 us
    ppermute x3, waiting for transfers between devices, per_device(): gu = lax.ppermute(gu, 'narrow', pairs)  17.8 us
    ppermute x3, starting transfers between devices, per_device(): gu = lax.ppermute(gu, 'narrow', pairs)  10.5 us
    unnamed x23, local copies, waits for them, and re-layouts  10.2 us
    ppermute x3, starting transfers between devices, per_device(): dn = lax.ppermute(dn, 'narrow', pairs)  9.43 us
    ppermute x3, waiting for transfers between devices, per_device(): dn = lax.ppermute(dn, 'narrow', pairs)  8.84 us
    all_to_all x3, waiting for transfers between devices, exchange(): return lax.all_to_all(x, axis, split_axis=0, concat_axis=0, tiled=True)  6.48 us
  transfers between devices with their start and end apart: 9, of which 6 were waited for; matrix products, arithmetic and copies ran while one was open for 6% of the time, Pallas kernels for 0%

profile of v2, /device:TPU:2, one launch (start us, length us, event | category | flops | bytes accessed | tf_op | source)
XLA Modules:
  0.0 173.6 jit_solution(15024110682426295126)
XLA Ops:
  0.0 0.8 subtract_convert_fusion
  0.8 0.1 copy.11
  0.9 0.1 copy.12
  1.0 0.7 convert_element_type.14
  1.7 0.1 copy.10
  1.8 0.1 constant_dynamic-slice_fusion.4
  1.9 0.1 concatenate.11
  2.0 0.7 broadcast_in_dim.10
  2.7 15.1 %all-to-all-start = ((bf16[8,32,512]{2,1,0:T(8,128)(2,1)}), bf16[8,32,512]{2,1,0:T(8,128)(2,1)S(1)}, u32[]{:S(2)}, u32[]{:S(2)}) async-start(bf16[8,32,512]{2,1,0:T(8,128)(2,1)} %broadcast_in_dim.10), calls=%async_computation | async-start | bytes 524288 | tf_op jit(solution)/shard_map/all_to_all | solution.py:41
  17.8 2.3 %fusion.1 = (bf16[2,448,256]{2,1,0:T(8,128)(2,1)S(1)}, bf16[2,448,256]{2,1,0:T(8,128)(2,1)}, bf16[2,448,256]{2,1,0:T(8,128)(2,1)S(1)}, bf16[2,448,256]{2,1,0:T(8,128)(2,1)S(1)}) fusion(s32[]{:T(128)S(6)} %select_n.25, bf16[4,2,448,128]{3,2,1,0:T(8,128)(2,1)S(1)} %bitcast.27, bf16[4,2,448,128]{3,2,1,0:T(8,128)(2,1)} %bitcast.28, s32[]{:T(128)S(6)} %select_n.22, ...), kind=kLoop, calls=%fused_computation.9 | loop fusion | flops 3670016 | bytes 3670032 | tf_op jit(solution)/shard_map/jit(dynamic_index_in_dim)/squeeze | solution.py:152
  20.1 3.4 %collective-permute-start = (bf16[2,448,256]{2,1,0:T(8,128)(2,1)}, bf16[2,448,256]{2,1,0:T(8,128)(2,1)S(1)}, u32[]{:S(2)}, u32[]{:S(2)}) collective-permute-start(bf16[2,448,256]{2,1,0:T(8,128)(2,1)} %get-tuple-element.12), channel_id=1, source_target_pairs={{0,1},{1,2},{2,3},{3,0},{4,5},{5,6},{6,7},{7,4},{8,9},{9,10},{10,1... | collective-permute-start | bytes 1376264 | tf_op jit(solution)/shard_map/ppermute | solution.py:156
  23.5 3.0 %collective-permute-start.1 = (bf16[2,448,256]{2,1,0:T(8,128)(2,1)S(1)}, bf16[2,448,256]{2,1,0:T(8,128)(2,1)S(1)}, u32[]{:S(2)}, u32[]{:S(2)}) collective-permute-start(bf16[2,448,256]{2,1,0:T(8,128)(2,1)S(1)} %get-tuple-element.13), channel_id=1, source_target_pairs={{0,2},{1,3},{2,0},{3,1},{4,6},{5,7},{6,4},{7,5},{8,10},{9,11},{10,... | collective-permute-start | bytes 1376264 | tf_op jit(solution)/shard_map/ppermute | solution.py:156
  26.5 4.1 %collective-permute-start.2 = (bf16[2,448,256]{2,1,0:T(8,128)(2,1)S(1)}, bf16[2,448,256]{2,1,0:T(8,128)(2,1)S(1)}, u32[]{:S(2)}, u32[]{:S(2)}) collective-permute-start(bf16[2,448,256]{2,1,0:T(8,128)(2,1)S(1)} %get-tuple-element.14), channel_id=1, source_target_pairs={{0,3},{1,0},{2,1},{3,2},{4,7},{5,4},{6,5},{7,6},{8,11},{9,8},{10,9... | collective-permute-start | bytes 1376264 | tf_op jit(solution)/shard_map/ppermute | solution.py:156
  30.6 5.0 %collective-permute-done.rest_0_.rest_1_ = bf16[2,448,256]{2,1,0:T(8,128)(2,1)S(1)} collective-permute-done((bf16[2,448,256]{2,1,0:T(8,128)(2,1)}, bf16[2,448,256]{2,1,0:T(8,128)(2,1)S(1)}, u32[]{:S(2)}, u32[]{:S(2)}) %collective-permute-start) | collective-permute-done | bytes 458784 | tf_op jit(solution)/shard_map/ppermute | solution.py:156
  35.6 4.8 %collective-permute-done.1.rest_1_.rest_2_ = bf16[2,448,256]{2,1,0:T(8,128)(2,1)S(1)} collective-permute-done((bf16[2,448,256]{2,1,0:T(8,128)(2,1)S(1)}, bf16[2,448,256]{2,1,0:T(8,128)(2,1)S(1)}, u32[]{:S(2)}, u32[]{:S(2)}) %collective-permute-start.1) | collective-permute-done | bytes 458784 | tf_op jit(solution)/shard_map/ppermute | solution.py:156
  40.4 8.0 %collective-permute-done.2.rest_2_.rest_3_ = bf16[2,448,256]{2,1,0:T(8,128)(2,1)S(1)} collective-permute-done((bf16[2,448,256]{2,1,0:T(8,128)(2,1)S(1)}, bf16[2,448,256]{2,1,0:T(8,128)(2,1)S(1)}, u32[]{:S(2)}, u32[]{:S(2)}) %collective-permute-start.2) | collective-permute-done | bytes 458784 | tf_op jit(solution)/shard_map/ppermute | solution.py:156
  48.4 0.0 all-to-all-done.rows_ref
  48.4 0.6 shard_map.64
  49.1 1.0 copy-done.1
  50.0 0.8 copy-done.5
  50.8 5.0 %all-to-all-start.1 = ((bf16[16,64,448]{2,1,0:T(8,128)(2,1)}), bf16[16,64,448]{2,1,0:T(8,128)(2,1)S(1)}, u32[]{:S(2)}, u32[]{:S(2)}) async-start(bf16[16,64,448]{2,1,0:T(8,128)(2,1)} %copy-done.1), calls=%async_computation.1 | async-start | bytes 2097152 | tf_op jit(solution)/shard_map/all_to_all | solution.py:41
  55.9 2.2 %copy.13 = bf16[1,128,3584]{1,2,0:T(8,128)(2,1)} copy(bf16[1,128,3584]{2,1,0:T(8,128)(2,1)} %param.11) | data formatting | bytes 1835008 | tf_op args[5]
  58.1 2.2 %constant_dynamic-slice_fusion = (bf16[128,2,1,448]{0,3,2,1:T(8,128)(2,1)}, bf16[128,2,1,448]{0,3,2,1:T(8,128)(2,1)}, bf16[128,2,1,448]{0,3,2,1:T(8,128)(2,1)}, bf16[128,2,1,448]{0,3,2,1:T(8,128)(2,1)S(1)}) fusion(bf16[128,2,4,448]{0,3,2,1:T(8,128)(2,1)} %bitcast.26, s32[]{:T(128)S(6)} %select_n.25, s32[]{:T(128)S(6)} %select_n.24, s32[]{:T(128)S(6)} %select_n.23, ...), kind=kLoop, calls=%fused_computation.17 | loop fusion | bytes 1835024 | tf_op jit(solution)/shard_map/dynamic-slice.3
  60.3 0.8 copy.18
  61.1 2.5 %collective-permute-start.3 = (bf16[2,128,448]{2,1,0:T(8,128)(2,1)}, bf16[2,128,448]{2,1,0:T(8,128)(2,1)S(1)}, u32[]{:S(2)}, u32[]{:S(2)}) collective-permute-start(bf16[2,128,448]{2,1,0:T(8,128)(2,1)} %bitcast.29), channel_id=1, source_target_pairs={{0,1},{1,2},{2,3},{3,0},{4,5},{5,6},{6,7},{7,4},{8,9},{9,10},{10,1... | collective-permute-start | bytes 688136 | tf_op jit(solution)/shard_map/ppermute | solution.py:157
  63.6 1.8 %copy.19 = bf16[128,2,1,448]{3,0,1,2:T(8,128)(2,1)} copy(bf16[128,2,1,448]{0,3,2,1:T(8,128)(2,1)} %get-tuple-element.17) | data formatting | bytes 458752
  65.4 3.0 %collective-permute-start.4 = (bf16[2,128,448]{2,1,0:T(8,128)(2,1)}, bf16[2,128,448]{2,1,0:T(8,128)(2,1)}, u32[]{:S(2)}, u32[]{:S(2)}) collective-permute-start(bf16[2,128,448]{2,1,0:T(8,128)(2,1)} %bitcast.30), channel_id=1, source_target_pairs={{0,2},{1,3},{2,0},{3,1},{4,6},{5,7},{6,4},{7,5},{8,10},{9,11},{10,... | collective-permute-start | bytes 688136 | tf_op jit(solution)/shard_map/ppermute | solution.py:157
  68.4 1.8 %copy.20 = bf16[128,2,1,448]{3,0,1,2:T(8,128)(2,1)} copy(bf16[128,2,1,448]{0,3,2,1:T(8,128)(2,1)} %get-tuple-element.16) | data formatting | bytes 458752
  70.2 3.9 %collective-permute-start.5 = (bf16[2,128,448]{2,1,0:T(8,128)(2,1)}, bf16[2,128,448]{2,1,0:T(8,128)(2,1)S(1)}, u32[]{:S(2)}, u32[]{:S(2)}) collective-permute-start(bf16[2,128,448]{2,1,0:T(8,128)(2,1)} %bitcast.31), channel_id=1, source_target_pairs={{0,3},{1,0},{2,1},{3,2},{4,7},{5,4},{6,5},{7,6},{8,11},{9,8},{10,9... | collective-permute-start | bytes 688136 | tf_op jit(solution)/shard_map/ppermute | solution.py:157
  74.1 0.0 collective-permute-done.3.rest_4_.rest_1_
  74.1 4.1 %collective-permute-done.4.rest_5_.rest_2_ = bf16[2,128,448]{2,1,0:T(8,128)(2,1)} collective-permute-done((bf16[2,128,448]{2,1,0:T(8,128)(2,1)}, bf16[2,128,448]{2,1,0:T(8,128)(2,1)}, u32[]{:S(2)}, u32[]{:S(2)}) %collective-permute-start.4) | collective-permute-done | bytes 229408 | tf_op jit(solution)/shard_map/ppermute | solution.py:157
  78.3 4.7 %collective-permute-done.5.rest_6_.rest_3_ = bf16[2,128,448]{2,1,0:T(8,128)(2,1)S(1)} collective-permute-done((bf16[2,128,448]{2,1,0:T(8,128)(2,1)}, bf16[2,128,448]{2,1,0:T(8,128)(2,1)S(1)}, u32[]{:S(2)}, u32[]{:S(2)}) %collective-permute-start.5) | collective-permute-done | bytes 229408 | tf_op jit(solution)/shard_map/ppermute | solution.py:157
  83.0 0.7 copy-done.2
  83.7 0.0 all-to-all-done.1.rows_ref
  83.7 0.9 copy-done.3
  84.6 1.2 shard_map.65
  85.9 16.9 %all_to_all.30.acts_ref = bf16[4,512,256]{2,1,0:T(8,128)(2,1)S(1)} all-to-all(bf16[4,512,256]{2,1,0:T(8,128)(2,1)S(1)} %shard_map.65), channel_id=1, replica_groups=mesh['grp'=2,'ylo'=2,'zfar'=8,'znear'=2,'core'=2,'narrow'=4] {'narrow'}, dimensions={0} | all-to-all | bytes 2097152 | tf_op jit(solution)/shard_map/all_to_all | solution.py:41
  102.8 1.0 shard_map.66
  103.8 5.0 %all-to-all-start.3 = ((bf16[4,512,128]{2,1,0:T(8,128)(2,1)}), bf16[4,512,128]{2,1,0:T(8,128)(2,1)S(1)}, u32[]{:S(2)}, u32[]{:S(2)}) async-start(bf16[4,512,128]{2,1,0:T(8,128)(2,1)} %shard_map.66), calls=%async_computation.3 | async-start | bytes 1048576 | tf_op jit(solution)/shard_map/all_to_all | solution.py:41
  108.8 0.1 copy.21
  109.0 6.5 %all-to-all-done.3.inner_ref = bf16[4,512,128]{2,1,0:T(8,128)(2,1)S(1)} async-done(((bf16[4,512,128]{2,1,0:T(8,128)(2,1)}), bf16[4,512,128]{2,1,0:T(8,128)(2,1)S(1)}, u32[]{:S(2)}, u32[]{:S(2)}) %all-to-all-start.3) | async-done | bytes 524320 | tf_op jit(solution)/shard_map/all_to_all | solution.py:41
  115.5 0.0 copy-done.4
  115.5 2.2 %shard_map.67 = bf16[16,64,448]{2,1,0:T(8,128)(2,1)S(1)} custom-call(s32[1]{0:T(128)} %bitcast.me_ref, bf16[4,512,128]{2,1,0:T(8,128)(2,1)S(1)} %all-to-all-done.3.inner_ref, bf16[2,128,448]{2,1,0:T(8,128)(2,1)S(1)} %bitcast.25, bf16[2,128,448]{2,1,0:T(8,128)(2,1)S(1)} %collective-permute-done.3.rest_4_.rest_1_, ...), custom_call_target="tpu_custom_call" | custom-call | flops 469762048 | bytes 2359300 | tf_op jit(solution)/shard_map/pallas_call | solution.py:29
  117.6 0.0 copy-start.6
  117.6 21.8 %all_to_all.31.rows_ref = bf16[16,64,448]{2,1,0:T(8,128)(2,1)S(1)} all-to-all(bf16[16,64,448]{2,1,0:T(8,128)(2,1)S(1)} %shard_map.67), channel_id=1, replica_groups=mesh['grp'=2,'ylo'=2,'zfar'=8,'znear'=2,'core'=2,'narrow'=4] {'grp','ylo..., dimensions={0} | all-to-all | bytes 1835008 | tf_op jit(solution)/shard_map/all_to_all | solution.py:41
  139.5 0.7 shard_map.68
  140.2 32.7 %all_to_all.32 = bf16[8,32,448]{2,1,0:T(8,128)(2,1)S(1)} all-to-all(bf16[8,32,448]{2,1,0:T(8,128)(2,1)S(1)} %shard_map.68), channel_id=1, replica_groups=mesh['grp'=2,'ylo'=2,'zfar'=8,'znear'=2,'core'=2,'narrow'=4] {'zfar'}, dimensions={0} | all-to-all | bytes 458752 | tf_op jit(solution)/shard_map/all_to_all | solution.py:41
  173.0 0.7 reduce_sum.12
  (13 shorter events, 0.0 us)
Async XLA Ops:
  0.0 1.8 %copy-start = (bf16[32,3584]{1,0:T(8,128)(2,1)S(1)}, bf16[32,3584]{1,0:T(8,128)(2,1)}, u32[]{:S(2)}) copy-start(bf16[32,3584]{1,0:T(8,128)(2,1)} %param.6) | copy-start | bytes 688132
  0.0 17.8 %copy-start.7 = (bf16[1,3584,128]{2,1,0:T(8,128)(2,1)S(1)}, bf16[1,3584,128]{2,1,0:T(8,128)(2,1)}, u32[]{:S(2)}) copy-start(bf16[1,3584,128]{2,1,0:T(8,128)(2,1)} %param.9) | copy-start | bytes 2752516
  2.7 45.7 %all-to-all-start = ((bf16[8,32,512]{2,1,0:T(8,128)(2,1)}), bf16[8,32,512]{2,1,0:T(8,128)(2,1)S(1)}, u32[]{:S(2)}, u32[]{:S(2)}) async-start(bf16[8,32,512]{2,1,0:T(8,128)(2,1)} %broadcast_in_dim.10), calls=%async_computation | async-start | bytes 524288 | tf_op jit(solution)/shard_map/all_to_all | solution.py:41
  20.1 15.5 %collective-permute-start = (bf16[2,448,256]{2,1,0:T(8,128)(2,1)}, bf16[2,448,256]{2,1,0:T(8,128)(2,1)S(1)}, u32[]{:S(2)}, u32[]{:S(2)}) collective-permute-start(bf16[2,448,256]{2,1,0:T(8,128)(2,1)} %get-tuple-element.12), channel_id=1, source_target_pairs={{0,1},{1,2},{2,3},{3,0},{4,5},{5,6},{6,7},{7,4},{8,9},{9,10},{10,1... | collective-permute-start | bytes 1376264 | tf_op jit(solution)/shard_map/ppermute | solution.py:156
  23.5 16.9 %collective-permute-start.1 = (bf16[2,448,256]{2,1,0:T(8,128)(2,1)S(1)}, bf16[2,448,256]{2,1,0:T(8,128)(2,1)S(1)}, u32[]{:S(2)}, u32[]{:S(2)}) collective-permute-start(bf16[2,448,256]{2,1,0:T(8,128)(2,1)S(1)} %get-tuple-element.13), channel_id=1, source_target_pairs={{0,2},{1,3},{2,0},{3,1},{4,6},{5,7},{6,4},{7,5},{8,10},{9,11},{10,... | collective-permute-start | bytes 1376264 | tf_op jit(solution)/shard_map/ppermute | solution.py:156
  26.5 21.9 %collective-permute-start.2 = (bf16[2,448,256]{2,1,0:T(8,128)(2,1)S(1)}, bf16[2,448,256]{2,1,0:T(8,128)(2,1)S(1)}, u32[]{:S(2)}, u32[]{:S(2)}) collective-permute-start(bf16[2,448,256]{2,1,0:T(8,128)(2,1)S(1)} %get-tuple-element.14), channel_id=1, source_target_pairs={{0,3},{1,0},{2,1},{3,2},{4,7},{5,4},{6,5},{7,6},{8,11},{9,8},{10,9... | collective-permute-start | bytes 1376264 | tf_op jit(solution)/shard_map/ppermute | solution.py:156
  49.0 1.0 copy-start.1
  50.0 0.8 copy-start.5
  50.8 32.8 %all-to-all-start.1 = ((bf16[16,64,448]{2,1,0:T(8,128)(2,1)}), bf16[16,64,448]{2,1,0:T(8,128)(2,1)S(1)}, u32[]{:S(2)}, u32[]{:S(2)}) async-start(bf16[16,64,448]{2,1,0:T(8,128)(2,1)} %copy-done.1), calls=%async_computation.1 | async-start | bytes 2097152 | tf_op jit(solution)/shard_map/all_to_all | solution.py:41
  61.1 13.0 %collective-permute-start.3 = (bf16[2,128,448]{2,1,0:T(8,128)(2,1)}, bf16[2,128,448]{2,1,0:T(8,128)(2,1)S(1)}, u32[]{:S(2)}, u32[]{:S(2)}) collective-permute-start(bf16[2,128,448]{2,1,0:T(8,128)(2,1)} %bitcast.29), channel_id=1, source_target_pairs={{0,1},{1,2},{2,3},{3,0},{4,5},{5,6},{6,7},{7,4},{8,9},{9,10},{10,1... | collective-permute-start | bytes 688136 | tf_op jit(solution)/shard_map/ppermute | solution.py:157
  65.4 12.9 %collective-permute-start.4 = (bf16[2,128,448]{2,1,0:T(8,128)(2,1)}, bf16[2,128,448]{2,1,0:T(8,128)(2,1)}, u32[]{:S(2)}, u32[]{:S(2)}) collective-permute-start(bf16[2,128,448]{2,1,0:T(8,128)(2,1)} %bitcast.30), channel_id=1, source_target_pairs={{0,2},{1,3},{2,0},{3,1},{4,6},{5,7},{6,4},{7,5},{8,10},{9,11},{10,... | collective-permute-start | bytes 688136 | tf_op jit(solution)/shard_map/ppermute | solution.py:157
  70.2 12.8 %collective-permute-start.5 = (bf16[2,128,448]{2,1,0:T(8,128)(2,1)}, bf16[2,128,448]{2,1,0:T(8,128)(2,1)S(1)}, u32[]{:S(2)}, u32[]{:S(2)}) collective-permute-start(bf16[2,128,448]{2,1,0:T(8,128)(2,1)} %bitcast.31), channel_id=1, source_target_pairs={{0,3},{1,0},{2,1},{3,2},{4,7},{5,4},{6,5},{7,6},{8,11},{9,8},{10,9... | collective-permute-start | bytes 688136 | tf_op jit(solution)/shard_map/ppermute | solution.py:157
  83.0 0.7 copy-start.2
  83.7 1.0 copy-start.3
  102.8 6.0 %copy-start.8 = (bf16[128,2,1,448]{0,3,2,1:T(8,128)(2,1)S(1)}, bf16[128,2,1,448]{0,3,2,1:T(8,128)(2,1)}, u32[]{:S(2)}) copy-start(bf16[128,2,1,448]{0,3,2,1:T(8,128)(2,1)} %get-tuple-element.15) | copy-start | bytes 688132
  103.8 11.7 %copy-start.4 = (bf16[2,128,448]{2,1,0:T(8,128)(2,1)S(1)}, bf16[2,128,448]{2,1,0:T(8,128)(2,1)}, u32[]{:S(2)}) copy-start(bf16[2,128,448]{2,1,0:T(8,128)(2,1)} %copy-done.2) | copy-start | bytes 688132
  103.8 11.7 %all-to-all-start.3 = ((bf16[4,512,128]{2,1,0:T(8,128)(2,1)}), bf16[4,512,128]{2,1,0:T(8,128)(2,1)S(1)}, u32[]{:S(2)}, u32[]{:S(2)}) async-start(bf16[4,512,128]{2,1,0:T(8,128)(2,1)} %shard_map.66), calls=%async_computation.3 | async-start | bytes 1048576 | tf_op jit(solution)/shard_map/all_to_all | solution.py:41
  117.6 21.9 %copy-start.6 = (bf16[512,512]{1,0:T(8,128)(2,1)S(1)}, bf16[512,512]{1,0:T(8,128)(2,1)}, u32[]{:S(2)}) copy-start(bf16[512,512]{1,0:T(8,128)(2,1)} %copy-done.5) | copy-start | bytes 1572868

commit v3 on v2

--- a/solution.py
+++ b/solution.py
@@ -22,7 +22,7 @@
 ANY = pl.BlockSpec(memory_space=pl.ANY)
 
 
-def call(body, outs, specs, args, flops=0):
+def call(body, outs, specs, args, flops=0, scratch=()):
     single = not isinstance(outs, list)
     outs = [outs] if single else outs
     nbytes = sum(a.size * a.dtype.itemsize for a in args) + sum(o.size * o.dtype.itemsize for o in outs)
@@ -31,7 +31,8 @@
         out_shape=outs,
         in_specs=specs,
         out_specs=[VMEM] * len(outs),
-        compiler_params=pltpu.CompilerParams(vmem_limit_bytes=40 * 1024 * 1024),
+        scratch_shapes=list(scratch),
+        compiler_params=pltpu.CompilerParams(vmem_limit_bytes=16 * 1024 * 1024),
         cost_estimate=pl.CostEstimate(flops=flops, bytes_accessed=nbytes, transcendentals=0),
     )(*args)
     return got[0] if single else got
@@ -39,6 +40,37 @@
 
 def exchange(x, axis):
     return lax.all_to_all(x, axis, split_axis=0, concat_axis=0, tiled=True)
+
+
+def rows_body(part, top, at_ref, hidden_ref, routes_ref, gates_ref, out_ref):
+    count, tok, lanes = out_ref.shape
+    odd = at_ref[1]
+    start = pl.multiple_of(at_ref[0] * 2 * part + odd * (part // 128 * 128), 128)
+    wide = hidden_ref[:, pl.ds(start, LANES)].astype(F32)
+    mine = jnp.where(odd == 1, wide[:, LANES - part :], wide[:, :part])
+    gates = gates_ref[...]
+    high = gates.astype(BF16).astype(F32)
+    extra = jnp.concatenate([routes_ref[...].astype(F32), high, gates - high], axis=0).astype(BF16)
+    eye = (lax.broadcasted_iota(I32, (tok, tok), 0) == lax.broadcasted_iota(I32, (tok, tok), 1)).astype(BF16)
+    extra = lax.dot_general(eye, extra, (((1,), (1,)), ((), ())), preferred_element_type=F32)
+    spare = jnp.zeros((tok, lanes - part - 3 * top), F32)
+    rows = jnp.concatenate([mine, extra, spare], axis=1).astype(BF16)
+    for i in range(count):
+        out_ref[i] = rows
+
+
+def pack_body(n_nar, part, at_ref, gate_ref, up_ref, down_ref, *rest):
+    outs, turned_ref = rest[:n_nar], rest[-1]
+    units = gate_ref.shape[2]
+    turned_ref[...] = jnp.transpose(down_ref[0])
+    for k in range(n_nar):
+        to = lax.rem(at_ref[0] + k, n_nar)
+        for i in range(2):
+            rows = pl.ds(pl.multiple_of((to * 2 + i) * part, 64), part)
+            outs[k][i, :, :units] = gate_ref[0, rows]
+            outs[k][i, :, units:] = up_ref[0, rows]
+            rows = pl.ds(pl.multiple_of((i * n_nar + to) * part, 64), part)
+            outs[k][2, :, i * units : (i + 1) * units] = turned_ref[rows]
 
 
 def pick_body(part, top, far_ref, rows_ref, *rest):
@@ -104,12 +136,11 @@
 def down_body(n_nar, me_ref, inner_ref, *rest):
     parts, out_ref = rest[:n_nar], rest[-1]
     half = out_ref.shape[0] // 2
+    units = inner_ref.shape[2]
+    left = jnp.concatenate([inner_ref[lax.rem(me_ref[0] - k + n_nar, n_nar)] for k in range(n_nar)], axis=1)
     for i in range(2):
-        out = 0.0
-        for k in range(n_nar):
-            left = inner_ref[lax.rem(me_ref[0] - k + n_nar, n_nar)]
-            out = out + jnp.dot(left, parts[k][i], preferred_element_type=F32)
-        out = out.astype(BF16)
+        right = jnp.concatenate([parts[k][2, :, i * units : (i + 1) * units] for k in range(n_nar)], axis=1)
+        out = lax.dot_general(left, right, (((1,), (1,)), ((), ())), preferred_element_type=F32).astype(BF16)
         out_ref[i * half : (i + 1) * half] = out.reshape(half, -1, out.shape[1])
 
 
@@ -130,33 +161,32 @@
     top = routes.shape[1]
     n_grp, n_nar, n_far = lax.axis_size("grp"), lax.axis_size("narrow"), lax.axis_size(FAR)
     g, n = lax.axis_index("grp"), lax.axis_index("narrow")
-    me = n.astype(I32).reshape(1)
     far = lax.axis_index(FAR).astype(I32).reshape(1)
     units = gate_proj.shape[2]
     part = width // (n_grp * n_nar)
     near = 16
     slots = 8 * n_far * CAP
 
-    mine = lax.dynamic_slice_in_dim(hidden, (n * n_grp + g) * part, part, 1)
-    gate_hi = route_gates.astype(BF16)
-    gate_lo = (route_gates - gate_hi.astype(F32)).astype(BF16)
-    spare = jnp.zeros((tok, LANES - part - 3 * top), BF16)
-    rows = jnp.concatenate([mine, routes.astype(BF16), gate_hi, gate_lo, spare], axis=1)
-    rows = exchange(jnp.broadcast_to(rows[None], (n_far, tok, LANES)), FAR)
-
-    gate_up = jnp.concatenate([gate_proj[0], up_proj[0]], axis=1).reshape(n_nar, n_grp, part, 2 * units)
-    down = down_proj[0].reshape(units, n_grp, n_nar, part).transpose(2, 1, 0, 3)
-    gu_parts, down_parts = [], []
-    for k in range(n_nar):
-        to = lax.rem(n + k, n_nar)
-        gu = lax.dynamic_index_in_dim(gate_up, to, 0, keepdims=False)
-        dn = lax.dynamic_index_in_dim(down, to, 0, keepdims=False)
-        if k:
-            pairs = [(i, (i + k) % n_nar) for i in range(n_nar)]
-            gu = lax.ppermute(gu, "narrow", pairs)
-            dn = lax.ppermute(dn, "narrow", pairs)
-        gu_parts.append(gu)
-        down_parts.append(dn)
+    at = jnp.stack([n, g]).astype(I32)
+    rows = call(
+        functools.partial(rows_body, part, top),
+        jax.ShapeDtypeStruct((n_far, tok, LANES), BF16),
+        [SMEM, VMEM, VMEM, VMEM],
+        [at, hidden, routes.T, route_gates.T],
+    )
+    rows = exchange(rows, FAR)
+
+    parts = call(
+        functools.partial(pack_body, n_nar, part),
+        [jax.ShapeDtypeStruct((3, part, 2 * units), BF16)] * n_nar,
+        [SMEM, VMEM, VMEM, VMEM],
+        [at, gate_proj, up_proj, down_proj],
+        scratch=[pltpu.VMEM((width, units), BF16)],
+    )
+    parts = list(parts)
+    for k in range(1, n_nar):
+        parts[k] = lax.ppermute(parts[k], "narrow", [(i, (i + k) % n_nar) for i in range(n_nar)])
+    sides = [parts[1], parts[-1]]
 
     picked, weight = call(
         functools.partial(pick_body, part, top),
@@ -164,8 +194,8 @@
             jax.ShapeDtypeStruct((near, n_far * CAP, part), BF16),
             jax.ShapeDtypeStruct((slots, 2 * n_far * tok), BF16),
         ],
-        [SMEM, VMEM] + [ANY] * (n_nar - 1),
-        [far, rows] + gu_parts[1:],
+        [SMEM, VMEM] + [ANY] * 2,
+        [far, rows] + sides,
         flops=2 * slots * n_far * tok * part,
     )
     rows = exchange(picked, NEAR)
@@ -173,8 +203,8 @@
     acts = call(
         functools.partial(gate_up_body, n_nar),
         jax.ShapeDtypeStruct((n_nar, slots, 2 * units), BF16),
-        [SMEM, VMEM] + [VMEM] * n_nar + [ANY] * (n_nar - 1),
-        [me, rows] + gu_parts + down_parts[1:],
+        [SMEM, VMEM] + [VMEM] * n_nar,
+        [at, rows] + parts,
         flops=2 * slots * part * 2 * units * 2 * n_nar,
     )
     acts = exchange(acts, "narrow")
@@ -184,7 +214,7 @@
         functools.partial(down_body, n_nar),
         jax.ShapeDtypeStruct((near, n_far * CAP, part), BF16),
         [SMEM, VMEM] + [VMEM] * n_nar,
-        [me, inner] + down_parts,
+        [at, inner] + parts,
         flops=2 * slots * units * n_nar * 2 * part,
     )
     outs = exchange(outs, NEAR)

time: 174 us -> 165 us (0.948)
  starting transfers between devices: 45 us -> 30.2 us
  blocking collectives: 71.5 us -> 82.7 us
  local copies, waits for them, and re-layouts: 13.6 us -> 9.38 us
  other arithmetic: 4.44 us -> 0.73 us
  Pallas kernels: 5.79 us -> 8.15 us
    all_to_all x3 -> x4, blocking collectives: 71.5 us -> 82.7 us  [exchange(): return lax.all_to_all(x, axis, split_axis=0, concat_axis=0, tiled=True)]
    ppermute x6 -> x3, starting transfers between devices: 19.9 us -> 10.1 us  [per_device(): lax.ppermute(parts[k], 'narrow', [(i, (i + k) % n_nar) for i in range(n_n...]
    ppermute x6 -> x3, waiting for transfers between devices: 26.7 us -> 33.2 us  [per_device(): lax.ppermute(parts[k], 'narrow', [(i, (i + k) % n_nar) for i in range(n_n...]
    all_to_all x3 -> x2, waiting for transfers between devices: 6.48 us -> 0.01 us  [exchange(): return lax.all_to_all(x, axis, split_axis=0, concat_axis=0, tiled=True)]
    all_to_all x3 -> x2, starting transfers between devices: 25.1 us -> 20.1 us  [exchange(): return lax.all_to_all(x, axis, split_axis=0, concat_axis=0, tiled=True)]
    pallas_call x5 -> x7, Pallas kernels: 5.79 us -> 8.15 us  [call(): pl.pallas_call(body, out_shape=outs, in_specs=specs, out_specs=[VMEM] * l...]
    squeeze x1 -> x0, other arithmetic: 2.29 us -> none  [per_device(): gu = lax.dynamic_index_in_dim(gate_up, to, 0, keepdims=False)]
    another operation x1 -> x0, local copies, waits for them, and re-layouts: 2.17 us -> none
  transfers between devices with their start and end apart: 9 -> 5, of which waited for: 6 -> 3; matrix products, arithmetic and copies ran while one was open for 6% -> 0% of each run, Pallas kernels for 0% -> 1%
where the time goes in v3:
time: 165 us; the launch traced here: 164 us
  blocking collectives  82.7 us (50%)
  waiting for transfers between devices  33.2 us (20%)
  starting transfers between devices  30.2 us (18%)
  local copies, waits for them, and re-layouts  9.38 us (6%)
  Pallas kernels  8.15 us (5%)
    all_to_all x4, blocking collectives, exchange(): return lax.all_to_all(x, axis, split_axis=0, concat_axis=0, tiled=True)  82.7 us
    ppermute x3, waiting for transfers between devices, per_device(): lax.ppermute(parts[k], 'narrow', [(i, (i + k) % n_nar) for i in range(n_n...  33.2 us
    all_to_all x2, starting transfers between devices, exchange(): return lax.all_to_all(x, axis, split_axis=0, concat_axis=0, tiled=True)  20.1 us
    ppermute x3, starting transfers between devices, per_device(): lax.ppermute(parts[k], 'narrow', [(i, (i + k) % n_nar) for i in range(n_n...  10.1 us
    unnamed x24, local copies, waits for them, and re-layouts  9.38 us
    pallas_call x7, Pallas kernels, call(): pl.pallas_call(body, out_shape=outs, in_specs=specs, out_specs=[VMEM] * l...  8.15 us
  transfers between devices with their start and end apart: 5, of which 3 were waited for; matrix products, arithmetic and copies ran while one was open for 0% of the time, Pallas kernels for 1%

profile of v3, /device:TPU:2, one launch (start us, length us, event | category | flops | bytes accessed | tf_op | source)
XLA Modules:
  0.0 164.5 jit_solution(16682849513426025419)
XLA Ops:
  0.0 0.0 copy-start.3
  0.0 0.1 pad_add_fusion.at_ref.me_ref
  0.1 0.0 copy-start.8
  0.1 1.0 copy-done.8
  1.1 0.0 copy-start.9
  1.1 0.7 copy-done.9
  1.8 0.0 copy-start.10
  1.8 0.7 copy-done.10
  2.5 1.5 shard_map.64
  3.9 15.1 %all-to-all-start = ((bf16[8,32,512]{2,1,0:T(8,128)(2,1)}), bf16[8,32,512]{2,1,0:T(8,128)(2,1)S(1)}, u32[]{:S(2)}, u32[]{:S(2)}) async-start(bf16[8,32,512]{2,1,0:T(8,128)(2,1)} %shard_map.64), calls=%async_computation | async-start | bytes 524288 | tf_op jit(solution)/shard_map/all_to_all | solution.py:42
  19.0 0.0 copy-done.3
  19.0 0.0 copy-start.4
  19.0 1.2 copy-done.4
  20.2 0.0 copy-start.5
  20.2 1.2 copy-done.5
  21.4 2.1 %shard_map.65 = (bf16[3,448,256]{2,1,0:T(8,128)(2,1)S(1)}, bf16[3,448,256]{2,1,0:T(8,128)(2,1)}, bf16[3,448,256]{2,1,0:T(8,128)(2,1)S(1)}, bf16[3,448,256]{2,1,0:T(8,128)(2,1)S(1)}) custom-call(s32[2]{0:T(128)S(1)} %pad_add_fusion.at_ref.me_ref, bf16[1,3584,128]{2,1,0:T(8,128)(2,1)S(1)} %copy-done.3, bf16[1,3584,128]{2,1,0:T(8,128)(2,1)S(1)} %copy-done.4, ...), custom_call_target="tpu_custom_call" | custom-call | bytes 5505032 | tf_op jit(solution)/shard_map/pallas_call | solution.py:29
  23.5 0.0 copy-start.11
  23.5 0.9 copy-done.11
  24.4 3.4 %collective-permute-start = (bf16[3,448,256]{2,1,0:T(8,128)(2,1)}, bf16[3,448,256]{2,1,0:T(8,128)(2,1)S(1)}, u32[]{:S(2)}, u32[]{:S(2)}) collective-permute-start(bf16[3,448,256]{2,1,0:T(8,128)(2,1)} %get-tuple-element.11), channel_id=1, source_target_pairs={{0,1},{1,2},{2,3},{3,0},{4,5},{5,6},{6,7},{7,4},{8,9},{9,10},{10,1... | collective-permute-start | bytes 2064392 | tf_op jit(solution)/shard_map/ppermute | solution.py:188
  27.7 2.4 %collective-permute-start.1 = (bf16[3,448,256]{2,1,0:T(8,128)(2,1)S(1)}, bf16[3,448,256]{2,1,0:T(8,128)(2,1)S(1)}, u32[]{:S(2)}, u32[]{:S(2)}) collective-permute-start(bf16[3,448,256]{2,1,0:T(8,128)(2,1)S(1)} %get-tuple-element.12), channel_id=1, source_target_pairs={{0,3},{1,0},{2,1},{3,2},{4,7},{5,4},{6,5},{7,6},{8,11},{9,8},{10,9... | collective-permute-start | bytes 2064392 | tf_op jit(solution)/shard_map/ppermute | solution.py:188
  30.2 13.1 %collective-permute-done.rest_0_.rest_1_ = bf16[3,448,256]{2,1,0:T(8,128)(2,1)S(1)} collective-permute-done((bf16[3,448,256]{2,1,0:T(8,128)(2,1)}, bf16[3,448,256]{2,1,0:T(8,128)(2,1)S(1)}, u32[]{:S(2)}, u32[]{:S(2)}) %collective-permute-start) | collective-permute-done | bytes 688160 | tf_op jit(solution)/shard_map/ppermute | solution.py:188
  43.3 2.9 %collective-permute-done.1.rest_1_.rest_3_ = bf16[3,448,256]{2,1,0:T(8,128)(2,1)S(1)} collective-permute-done((bf16[3,448,256]{2,1,0:T(8,128)(2,1)S(1)}, bf16[3,448,256]{2,1,0:T(8,128)(2,1)S(1)}, u32[]{:S(2)}, u32[]{:S(2)}) %collective-permute-start.1) | collective-permute-done | bytes 688160 | tf_op jit(solution)/shard_map/ppermute | solution.py:188
  46.3 0.0 all-to-all-done.rows_ref
  46.3 0.6 shard_map.66
  46.9 0.0 copy-start.2
  46.9 1.0 copy-done.2
  47.9 0.0 copy-start.6
  47.9 0.8 copy-done.6
  48.7 5.0 %all-to-all-start.1 = ((bf16[16,64,448]{2,1,0:T(8,128)(2,1)}), bf16[16,64,448]{2,1,0:T(8,128)(2,1)S(1)}, u32[]{:S(2)}, u32[]{:S(2)}) async-start(bf16[16,64,448]{2,1,0:T(8,128)(2,1)} %copy-done.2), calls=%async_computation.1 | async-start | bytes 2097152 | tf_op jit(solution)/shard_map/all_to_all | solution.py:42
  53.7 4.2 %collective-permute-start.2 = (bf16[3,448,256]{2,1,0:T(8,128)(2,1)}, bf16[3,448,256]{2,1,0:T(8,128)(2,1)S(1)}, u32[]{:S(2)}, u32[]{:S(2)}) collective-permute-start(bf16[3,448,256]{2,1,0:T(8,128)(2,1)} %copy-done.11), channel_id=1, source_target_pairs={{0,2},{1,3},{2,0},{3,1},{4,6},{5,7},{6,4},{7,5},{8,10},{9,11},{10,... | collective-permute-start | bytes 2064392 | tf_op jit(solution)/shard_map/ppermute | solution.py:188
  58.0 17.1 %collective-permute-done.2.rest_2_ = bf16[3,448,256]{2,1,0:T(8,128)(2,1)S(1)} collective-permute-done((bf16[3,448,256]{2,1,0:T(8,128)(2,1)}, bf16[3,448,256]{2,1,0:T(8,128)(2,1)S(1)}, u32[]{:S(2)}, u32[]{:S(2)}) %collective-permute-start.2) | collective-permute-done | bytes 688160 | tf_op jit(solution)/shard_map/ppermute | solution.py:188
  75.1 0.0 copy-start
  75.1 0.9 copy-done
  76.0 0.0 all-to-all-done.1.rows_ref
  76.0 0.0 copy-start.1
  76.0 1.1 copy-done.1
  77.1 1.8 %shard_map.67 = bf16[4,512,256]{2,1,0:T(8,128)(2,1)S(1)} custom-call(s32[2]{0:T(128)S(1)} %pad_add_fusion.at_ref.me_ref, bf16[16,64,448]{2,1,0:T(8,128)(2,1)S(1)} %all-to-all-done.1.rows_ref, bf16[3,448,256]{2,1,0:T(8,128)(2,1)S(1)} %get-tuple-element.14.rest_0_, bf16[3,448,256]{2,1,0:T(8,128)(2,1)S(1)} %collective-permute-done.rest_0_.rest_1_, ...), custom_call_target="tpu_custom_call" | custom-call | flops 939524096 | bytes 4718600 | tf_op jit(solution)/shard_map/pallas_call | solution.py:29
  78.9 18.0 %all_to_all.30.acts_ref = bf16[4,512,256]{2,1,0:T(8,128)(2,1)S(1)} all-to-all(bf16[4,512,256]{2,1,0:T(8,128)(2,1)S(1)} %shard_map.67), channel_id=1, replica_groups=mesh['grp'=2,'ylo'=2,'zfar'=8,'znear'=2,'core'=2,'narrow'=4] {'narrow'}, dimensions={0} | all-to-all | bytes 2097152 | tf_op jit(solution)/shard_map/all_to_all | solution.py:42
  96.9 0.2 shard_map.68
  97.1 10.8 %all_to_all.31.inner_ref = bf16[4,512,128]{2,1,0:T(8,128)(2,1)S(1)} all-to-all(bf16[4,512,128]{2,1,0:T(8,128)(2,1)S(1)} %shard_map.68), channel_id=1, replica_groups=mesh['grp'=2,'ylo'=2,'zfar'=8,'znear'=2,'core'=2,'narrow'=4] {'narrow'}, dimensions={0} | all-to-all | bytes 1048576 | tf_op jit(solution)/shard_map/all_to_all | solution.py:42
  107.8 1.3 shard_map.69
  109.1 0.0 copy-start.7
  109.1 21.2 %all_to_all.32.rows_ref = bf16[16,64,448]{2,1,0:T(8,128)(2,1)S(1)} all-to-all(bf16[16,64,448]{2,1,0:T(8,128)(2,1)S(1)} %shard_map.69), channel_id=1, replica_groups=mesh['grp'=2,'ylo'=2,'zfar'=8,'znear'=2,'core'=2,'narrow'=4] {'grp','ylo..., dimensions={0} | all-to-all | bytes 1835008 | tf_op jit(solution)/shard_map/all_to_all | solution.py:42
  130.3 0.0 copy-done.7
  130.4 0.7 shard_map.70
  131.1 32.7 %all_to_all.33 = bf16[8,32,448]{2,1,0:T(8,128)(2,1)S(1)} all-to-all(bf16[8,32,448]{2,1,0:T(8,128)(2,1)S(1)} %shard_map.70), channel_id=1, replica_groups=mesh['grp'=2,'ylo'=2,'zfar'=8,'znear'=2,'core'=2,'narrow'=4] {'zfar'}, dimensions={0} | all-to-all | bytes 458752 | tf_op jit(solution)/shard_map/all_to_all | solution.py:42
  163.8 0.7 reduce_sum.12
Async XLA Ops:
  0.0 19.0 %copy-start.3 = (bf16[1,3584,128]{2,1,0:T(8,128)(2,1)S(1)}, bf16[1,3584,128]{2,1,0:T(8,128)(2,1)}, u32[]{:S(2)}) copy-start(bf16[1,3584,128]{2,1,0:T(8,128)(2,1)} %gate_ref.1) | copy-start | bytes 2752516
  0.1 1.0 copy-start.8
  1.1 0.7 copy-start.9
  1.8 0.7 copy-start.10
  3.9 42.3 %all-to-all-start = ((bf16[8,32,512]{2,1,0:T(8,128)(2,1)}), bf16[8,32,512]{2,1,0:T(8,128)(2,1)S(1)}, u32[]{:S(2)}, u32[]{:S(2)}) async-start(bf16[8,32,512]{2,1,0:T(8,128)(2,1)} %shard_map.64), calls=%async_computation | async-start | bytes 524288 | tf_op jit(solution)/shard_map/all_to_all | solution.py:42
  19.0 1.2 copy-start.4
  20.2 1.2 copy-start.5
  23.5 0.9 copy-start.11
  24.4 19.0 %collective-permute-start = (bf16[3,448,256]{2,1,0:T(8,128)(2,1)}, bf16[3,448,256]{2,1,0:T(8,128)(2,1)S(1)}, u32[]{:S(2)}, u32[]{:S(2)}) collective-permute-start(bf16[3,448,256]{2,1,0:T(8,128)(2,1)} %get-tuple-element.11), channel_id=1, source_target_pairs={{0,1},{1,2},{2,3},{3,0},{4,5},{5,6},{6,7},{7,4},{8,9},{9,10},{10,1... | collective-permute-start | bytes 2064392 | tf_op jit(solution)/shard_map/ppermute | solution.py:188
  27.7 18.5 %collective-permute-start.1 = (bf16[3,448,256]{2,1,0:T(8,128)(2,1)S(1)}, bf16[3,448,256]{2,1,0:T(8,128)(2,1)S(1)}, u32[]{:S(2)}, u32[]{:S(2)}) collective-permute-start(bf16[3,448,256]{2,1,0:T(8,128)(2,1)S(1)} %get-tuple-element.12), channel_id=1, source_target_pairs={{0,3},{1,0},{2,1},{3,2},{4,7},{5,4},{6,5},{7,6},{8,11},{9,8},{10,9... | collective-permute-start | bytes 2064392 | tf_op jit(solution)/shard_map/ppermute | solution.py:188
  46.9 1.0 copy-start.2
  47.9 0.8 copy-start.6
  48.7 27.3 %all-to-all-start.1 = ((bf16[16,64,448]{2,1,0:T(8,128)(2,1)}), bf16[16,64,448]{2,1,0:T(8,128)(2,1)S(1)}, u32[]{:S(2)}, u32[]{:S(2)}) async-start(bf16[16,64,448]{2,1,0:T(8,128)(2,1)} %copy-done.2), calls=%async_computation.1 | async-start | bytes 2097152 | tf_op jit(solution)/shard_map/all_to_all | solution.py:42
  53.7 21.4 %collective-permute-start.2 = (bf16[3,448,256]{2,1,0:T(8,128)(2,1)}, bf16[3,448,256]{2,1,0:T(8,128)(2,1)S(1)}, u32[]{:S(2)}, u32[]{:S(2)}) collective-permute-start(bf16[3,448,256]{2,1,0:T(8,128)(2,1)} %copy-done.11), channel_id=1, source_target_pairs={{0,2},{1,3},{2,0},{3,1},{4,6},{5,7},{6,4},{7,5},{8,10},{9,11},{10,... | collective-permute-start | bytes 2064392 | tf_op jit(solution)/shard_map/ppermute | solution.py:188
  75.1 0.9 copy-start
  76.0 1.1 copy-start.1
  109.1 21.3 %copy-start.7 = (bf16[512,512]{1,0:T(8,128)(2,1)S(1)}, bf16[512,512]{1,0:T(8,128)(2,1)}, u32[]{:S(2)}) copy-start(bf16[512,512]{1,0:T(8,128)(2,1)} %copy-done.6) | copy-start | bytes 1572868

commit v4 on v3

--- a/solution.py
+++ b/solution.py
@@ -16,13 +16,15 @@
 AXES = ("grp", "ylo", "zfar", "znear", "core", "narrow")
 WIDE = ("ylo", "zfar", "znear", "core")
 LANES = 512
+HOLD = 200 * 10**9
 
 VMEM = pl.BlockSpec(memory_space=pltpu.VMEM)
 SMEM = pl.BlockSpec(memory_space=pltpu.SMEM)
 ANY = pl.BlockSpec(memory_space=pl.ANY)
-
-
-def call(body, outs, specs, args, flops=0, scratch=()):
+HBM = pl.BlockSpec(memory_space=pltpu.HBM)
+
+
+def call(body, outs, specs, args, flops=0, scratch=(), mib=16):
     single = not isinstance(outs, list)
     outs = [outs] if single else outs
     nbytes = sum(a.size * a.dtype.itemsize for a in args) + sum(o.size * o.dtype.itemsize for o in outs)
@@ -32,7 +34,7 @@
         in_specs=specs,
         out_specs=[VMEM] * len(outs),
         scratch_shapes=list(scratch),
-        compiler_params=pltpu.CompilerParams(vmem_limit_bytes=16 * 1024 * 1024),
+        compiler_params=pltpu.CompilerParams(vmem_limit_bytes=mib * 1024 * 1024),
         cost_estimate=pl.CostEstimate(flops=flops, bytes_accessed=nbytes, transcendentals=0),
     )(*args)
     return got[0] if single else got
@@ -42,11 +44,20 @@
     return lax.all_to_all(x, axis, split_axis=0, concat_axis=0, tiled=True)
 
 
-def rows_body(part, top, at_ref, hidden_ref, routes_ref, gates_ref, out_ref):
+def rows_body(part, top, at_ref, hidden_hbm, routes_hbm, gates_hbm, out_ref, wide_ref, routes_ref, gates_ref, sems):
     count, tok, lanes = out_ref.shape
     odd = at_ref[1]
     start = pl.multiple_of(at_ref[0] * 2 * part + odd * (part // 128 * 128), 128)
-    wide = hidden_ref[:, pl.ds(start, LANES)].astype(F32)
+    copies = [
+        pltpu.make_async_copy(hidden_hbm.at[:, pl.ds(start, LANES)], wide_ref, sems.at[0]),
+        pltpu.make_async_copy(routes_hbm, routes_ref, sems.at[1]),
+        pltpu.make_async_copy(gates_hbm, gates_ref, sems.at[2]),
+    ]
+    for copy in copies:
+        copy.start()
+    for copy in copies:
+        copy.wait()
+    wide = wide_ref[...].astype(F32)
     mine = jnp.where(odd == 1, wide[:, LANES - part :], wide[:, :part])
     gates = gates_ref[...]
     high = gates.astype(BF16).astype(F32)
@@ -59,22 +70,37 @@
         out_ref[i] = rows
 
 
-def pack_body(n_nar, part, at_ref, gate_ref, up_ref, down_ref, *rest):
-    outs, turned_ref = rest[:n_nar], rest[-1]
-    units = gate_ref.shape[2]
-    turned_ref[...] = jnp.transpose(down_ref[0])
+def pack_body(n_nar, part, at_ref, gate_hbm, up_hbm, down_hbm, *rest):
+    outs, (down_ref, turned_ref, sems, down_sem) = rest[:n_nar], rest[n_nar:]
+    units = gate_hbm.shape[2]
+    fetch = pltpu.make_async_copy(down_hbm.at[0], down_ref, down_sem)
+    fetch.start()
+    copies = []
     for k in range(n_nar):
         to = lax.rem(at_ref[0] + k, n_nar)
         for i in range(2):
             rows = pl.ds(pl.multiple_of((to * 2 + i) * part, 64), part)
-            outs[k][i, :, :units] = gate_ref[0, rows]
-            outs[k][i, :, units:] = up_ref[0, rows]
+            for m, source in enumerate((gate_hbm, up_hbm)):
+                place = outs[k].at[i, :, m * units : (m + 1) * units]
+                copies.append(pltpu.make_async_copy(source.at[0, rows], place, sems.at[k, i, m]))
+    for copy in copies:
+        copy.start()
+    fetch.wait()
+    turned_ref[...] = jnp.transpose(down_ref[...])
+    for k in range(n_nar):
+        to = lax.rem(at_ref[0] + k, n_nar)
+        for i in range(2):
             rows = pl.ds(pl.multiple_of((i * n_nar + to) * part, 64), part)
             outs[k][2, :, i * units : (i + 1) * units] = turned_ref[rows]
-
-
-def pick_body(part, top, far_ref, rows_ref, *rest):
-    out_ref, weight_ref = rest[-2:]
+    for copy in copies:
+        copy.wait()
+
+
+def arrived_body(*refs):
+    refs[-1][...] = jnp.zeros(refs[-1].shape, F32)
+
+
+def pick_body(part, top, far_ref, rows_ref, out_ref, weight_ref):
     blocks, tok, _ = rows_ref.shape
     count = blocks * tok
     rows = rows_ref[...].reshape(count, LANES)
@@ -171,22 +197,37 @@
     rows = call(
         functools.partial(rows_body, part, top),
         jax.ShapeDtypeStruct((n_far, tok, LANES), BF16),
-        [SMEM, VMEM, VMEM, VMEM],
+        [SMEM, HBM, HBM, HBM],
         [at, hidden, routes.T, route_gates.T],
+        scratch=[
+            pltpu.VMEM((tok, LANES), BF16),
+            pltpu.VMEM((top, tok), I32),
+            pltpu.VMEM((top, tok), F32),
+            pltpu.SemaphoreType.DMA((3,)),
+        ],
+        mib=60,
     )
     rows = exchange(rows, FAR)
 
     parts = call(
         functools.partial(pack_body, n_nar, part),
         [jax.ShapeDtypeStruct((3, part, 2 * units), BF16)] * n_nar,
-        [SMEM, VMEM, VMEM, VMEM],
+        [SMEM, HBM, HBM, HBM],
         [at, gate_proj, up_proj, down_proj],
-        scratch=[pltpu.VMEM((width, units), BF16)],
+        scratch=[
+            pltpu.VMEM((units, width), BF16),
+            pltpu.VMEM((width, units), BF16),
+            pltpu.SemaphoreType.DMA((n_nar, 2, 2)),
+            pltpu.SemaphoreType.DMA,
+        ],
+        mib=60,
     )
     parts = list(parts)
     for k in range(1, n_nar):
         parts[k] = lax.ppermute(parts[k], "narrow", [(i, (i + k) % n_nar) for i in range(n_nar)])
-    sides = [parts[1], parts[-1]]
+    arrived = call(
+        arrived_body, jax.ShapeDtypeStruct((8, 128), F32), [ANY] * (n_nar - 1), parts[1:], flops=HOLD
+    )
 
     picked, weight = call(
         functools.partial(pick_body, part, top),
@@ -194,8 +235,8 @@
             jax.ShapeDtypeStruct((near, n_far * CAP, part), BF16),
             jax.ShapeDtypeStruct((slots, 2 * n_far * tok), BF16),
         ],
-        [SMEM, VMEM] + [ANY] * 2,
-        [far, rows] + sides,
+        [SMEM, VMEM],
+        [far, rows],
         flops=2 * slots * n_far * tok * part,
     )
     rows = exchange(picked, NEAR)
@@ -203,8 +244,8 @@
     acts = call(
         functools.partial(gate_up_body, n_nar),
         jax.ShapeDtypeStruct((n_nar, slots, 2 * units), BF16),
-        [SMEM, VMEM] + [VMEM] * n_nar,
-        [at, rows] + parts,
+        [SMEM, VMEM] + [VMEM] * n_nar + [ANY],
+        [at, rows] + parts + [arrived],
         flops=2 * slots * part * 2 * units * 2 * n_nar,
     )
     acts = exchange(acts, "narrow")

time: 165 us -> 150 us (0.909)
  waiting for transfers between devices: 33.2 us -> 22.8 us
  local copies, waits for them, and re-layouts: 9.38 us -> 0.01 us
  Pallas kernels: 8.15 us -> 13.3 us
    ppermute x3, waiting for transfers between devices: 33.2 us -> 15.4 us  [per_device(): lax.ppermute(parts[k], 'narrow', [(i, (i + k) % n_nar) for i in range(n_n...]
    unnamed x24 -> x4, local copies, waits for them, and re-layouts: 9.38 us -> 0.01 us
    all_to_all x2, waiting for transfers between devices: 0.01 us -> 7.48 us  [exchange(): return lax.all_to_all(x, axis, split_axis=0, concat_axis=0, tiled=True)]
    pallas_call x7 -> x8, Pallas kernels: 8.15 us -> 13.3 us  [call(): pl.pallas_call(body, out_shape=outs, in_specs=specs, out_specs=[VMEM] * l...]
  transfers between devices with their start and end apart: 5 -> 5, of which waited for: 3 -> 4; matrix products, arithmetic and copies ran while one was open for 0% -> 0% of each run, Pallas kernels for 1% -> 4%
where the time goes in v4:
time: 150 us
  blocking collectives  81.8 us (55%)
  starting transfers between devices  30.2 us (20%)
  waiting for transfers between devices  22.8 us (15%)
  Pallas kernels  13.3 us (9%)
    all_to_all x4, blocking collectives, exchange(): return lax.all_to_all(x, axis, split_axis=0, concat_axis=0, tiled=True)  81.8 us
    all_to_all x2, starting transfers between devices, exchange(): return lax.all_to_all(x, axis, split_axis=0, concat_axis=0, tiled=True)  19.7 us
    ppermute x3, waiting for transfers between devices, per_device(): lax.ppermute(parts[k], 'narrow', [(i, (i + k) % n_nar) for i in range(n_n...  15.4 us
    pallas_call x8, Pallas kernels, call(): pl.pallas_call(body, out_shape=outs, in_specs=specs, out_specs=[VMEM] * l...  13.3 us
    ppermute x3, starting transfers between devices, per_device(): lax.ppermute(parts[k], 'narrow', [(i, (i + k) % n_nar) for i in range(n_n...  10.5 us
    all_to_all x2, waiting for transfers between devices, exchange(): return lax.all_to_all(x, axis, split_axis=0, concat_axis=0, tiled=True)  7.48 us
  transfers between devices with their start and end apart: 5, of which 4 were waited for; matrix products, arithmetic and copies ran while one was open for 0% of the time, Pallas kernels for 4%

profile of v4, /device:TPU:2, one launch (start us, length us, event | category | flops | bytes accessed | tf_op | source)
XLA Modules:
  0.0 149.6 jit_solution(14573178156335178537)
XLA Ops:
  0.0 0.6 pad_add_fusion.at_ref.me_ref
  0.6 2.4 %shard_map.64 = bf16[8,32,512]{2,1,0:T(8,128)(2,1)} custom-call(s32[2]{0:T(128)} %pad_add_fusion.at_ref.me_ref, bf16[32,3584]{1,0:T(8,128)(2,1)} %hidden_hbm.1, s32[8,32]{1,0:T(8,128)} %bitcast.5, f32[8,32]{1,0:T(8,128)} %bitcast.6), custom_call_target="tpu_custom_call" | custom-call | bytes 493576 | tf_op jit(solution)/shard_map/pallas_call | solution.py:31
  3.0 15.1 %all-to-all-start = ((bf16[8,32,512]{2,1,0:T(8,128)(2,1)}), bf16[8,32,512]{2,1,0:T(8,128)(2,1)S(1)}, u32[]{:S(2)}, u32[]{:S(2)}) async-start(bf16[8,32,512]{2,1,0:T(8,128)(2,1)} %shard_map.64), calls=%async_computation | async-start | bytes 524288 | tf_op jit(solution)/shard_map/all_to_all | solution.py:44
  18.1 4.7 %shard_map.66 = (bf16[3,448,256]{2,1,0:T(8,128)(2,1)}, bf16[3,448,256]{2,1,0:T(8,128)(2,1)}, bf16[3,448,256]{2,1,0:T(8,128)(2,1)}, bf16[3,448,256]{2,1,0:T(8,128)(2,1)}) custom-call(s32[2]{0:T(128)} %pad_add_fusion.at_ref.me_ref, bf16[1,3584,128]{2,1,0:T(8,128)(2,1)} %gate_hbm.1, bf16[1,3584,128]{2,1,0:T(8,128)(2,1)} %up_hbm.1, bf16[1,128,3584]{2,1,0:T(8,128)(2,1)} %down_hbm.1), custom_call_target="tpu_custom_call" | custom-call | bytes 5505032 | tf_op jit(solution)/shard_map/pallas_call | solution.py:31
  22.8 3.4 %collective-permute-start = (bf16[3,448,256]{2,1,0:T(8,128)(2,1)}, bf16[3,448,256]{2,1,0:T(8,128)(2,1)S(1)}, u32[]{:S(2)}, u32[]{:S(2)}) collective-permute-start(bf16[3,448,256]{2,1,0:T(8,128)(2,1)} %get-tuple-element.13), channel_id=1, source_target_pairs={{0,1},{1,2},{2,3},{3,0},{4,5},{5,6},{6,7},{7,4},{8,9},{9,10},{10,1... | collective-permute-start | bytes 2064392 | tf_op jit(solution)/shard_map/ppermute | solution.py:227
  26.2 3.0 %collective-permute-start.1 = (bf16[3,448,256]{2,1,0:T(8,128)(2,1)}, bf16[3,448,256]{2,1,0:T(8,128)(2,1)S(1)}, u32[]{:S(2)}, u32[]{:S(2)}) collective-permute-start(bf16[3,448,256]{2,1,0:T(8,128)(2,1)} %get-tuple-element.14), channel_id=1, source_target_pairs={{0,2},{1,3},{2,0},{3,1},{4,6},{5,7},{6,4},{7,5},{8,10},{9,11},{10,... | collective-permute-start | bytes 2064392 | tf_op jit(solution)/shard_map/ppermute | solution.py:227
  29.2 4.1 %collective-permute-start.2 = (bf16[3,448,256]{2,1,0:T(8,128)(2,1)}, bf16[3,448,256]{2,1,0:T(8,128)(2,1)S(1)}, u32[]{:S(2)}, u32[]{:S(2)}) collective-permute-start(bf16[3,448,256]{2,1,0:T(8,128)(2,1)} %get-tuple-element.15), channel_id=1, source_target_pairs={{0,3},{1,0},{2,1},{3,2},{4,7},{5,4},{6,5},{7,6},{8,11},{9,8},{10,9... | collective-permute-start | bytes 2064392 | tf_op jit(solution)/shard_map/ppermute | solution.py:227
  33.3 6.2 %all-to-all-done.rows_ref = bf16[8,32,512]{2,1,0:T(8,128)(2,1)S(1)} async-done(((bf16[8,32,512]{2,1,0:T(8,128)(2,1)}), bf16[8,32,512]{2,1,0:T(8,128)(2,1)S(1)}, u32[]{:S(2)}, u32[]{:S(2)}) %all-to-all-start) | async-done | bytes 262176 | tf_op jit(solution)/shard_map/all_to_all | solution.py:44
  39.5 1.7 %shard_map.65 = (bf16[16,64,448]{2,1,0:T(8,128)(2,1)}, bf16[512,512]{1,0:T(8,128)(2,1)S(1)}) custom-call(s32[1]{0:T(128)} %bitcast.2.far_ref, bf16[8,32,512]{2,1,0:T(8,128)(2,1)S(1)} %all-to-all-done.rows_ref), custom_call_target="tpu_custom_call" | custom-call | flops 117440512 | bytes 1703940 | tf_op jit(solution)/shard_map/pallas_call | solution.py:31
  41.2 4.6 %all-to-all-start.1 = ((bf16[16,64,448]{2,1,0:T(8,128)(2,1)}), bf16[16,64,448]{2,1,0:T(8,128)(2,1)}, u32[]{:S(2)}, u32[]{:S(2)}) async-start(bf16[16,64,448]{2,1,0:T(8,128)(2,1)} %get-tuple-element.11), calls=%async_computation.1 | async-start | bytes 2097152 | tf_op jit(solution)/shard_map/all_to_all | solution.py:44
  45.8 0.0 collective-permute-done.refs_0_.rest_1_
  45.8 2.4 %collective-permute-done.1.refs_1_.rest_2_ = bf16[3,448,256]{2,1,0:T(8,128)(2,1)S(1)} collective-permute-done((bf16[3,448,256]{2,1,0:T(8,128)(2,1)}, bf16[3,448,256]{2,1,0:T(8,128)(2,1)S(1)}, u32[]{:S(2)}, u32[]{:S(2)}) %collective-permute-start.1) | collective-permute-done | bytes 688160 | tf_op jit(solution)/shard_map/ppermute | solution.py:227
  48.2 12.9 %collective-permute-done.2.refs_2_.rest_3_ = bf16[3,448,256]{2,1,0:T(8,128)(2,1)S(1)} collective-permute-done((bf16[3,448,256]{2,1,0:T(8,128)(2,1)}, bf16[3,448,256]{2,1,0:T(8,128)(2,1)S(1)}, u32[]{:S(2)}, u32[]{:S(2)}) %collective-permute-start.2) | collective-permute-done | bytes 688160 | tf_op jit(solution)/shard_map/ppermute | solution.py:227
  61.1 0.0 copy-start
  61.2 0.0 copy-start.1
  61.2 1.3 all-to-all-done.1.rows_ref
  62.4 0.0 copy-done
  62.4 0.0 copy-done.1
  62.4 2.5 %shard_map.68 = bf16[4,512,256]{2,1,0:T(8,128)(2,1)S(1)} custom-call(s32[2]{0:T(128)S(1)} %copy-done.1, bf16[16,64,448]{2,1,0:T(8,128)(2,1)} %all-to-all-done.1.rows_ref, bf16[3,448,256]{2,1,0:T(8,128)(2,1)S(1)} %copy-done, bf16[3,448,256]{2,1,0:T(8,128)(2,1)S(1)} %collective-permute-done.refs_0_.rest_1_, ...), custom_call_target="tpu_custom_call" | custom-call | flops 939524096 | bytes 4722696 | tf_op jit(solution)/shard_map/pallas_call | solution.py:31
  64.9 18.1 %all_to_all.30.acts_ref = bf16[4,512,256]{2,1,0:T(8,128)(2,1)S(1)} all-to-all(bf16[4,512,256]{2,1,0:T(8,128)(2,1)S(1)} %shard_map.68), channel_id=1, replica_groups=mesh['grp'=2,'ylo'=2,'zfar'=8,'znear'=2,'core'=2,'narrow'=4] {'narrow'}, dimensions={0} | all-to-all | bytes 2097152 | tf_op jit(solution)/shard_map/all_to_all | solution.py:44
  83.0 0.2 shard_map.69
  83.2 10.8 %all_to_all.31.inner_ref = bf16[4,512,128]{2,1,0:T(8,128)(2,1)S(1)} all-to-all(bf16[4,512,128]{2,1,0:T(8,128)(2,1)S(1)} %shard_map.69), channel_id=1, replica_groups=mesh['grp'=2,'ylo'=2,'zfar'=8,'znear'=2,'core'=2,'narrow'=4] {'narrow'}, dimensions={0} | all-to-all | bytes 1048576 | tf_op jit(solution)/shard_map/all_to_all | solution.py:44
  93.9 1.3 shard_map.70
  95.2 20.3 %all_to_all.32.rows_ref = bf16[16,64,448]{2,1,0:T(8,128)(2,1)S(1)} all-to-all(bf16[16,64,448]{2,1,0:T(8,128)(2,1)S(1)} %shard_map.70), channel_id=1, replica_groups=mesh['grp'=2,'ylo'=2,'zfar'=8,'znear'=2,'core'=2,'narrow'=4] {'grp','ylo..., dimensions={0} | all-to-all | bytes 1835008 | tf_op jit(solution)/shard_map/all_to_all | solution.py:44
  115.5 0.7 shard_map.71
  116.2 32.7 %all_to_all.33 = bf16[8,32,448]{2,1,0:T(8,128)(2,1)S(1)} all-to-all(bf16[8,32,448]{2,1,0:T(8,128)(2,1)S(1)} %shard_map.71), channel_id=1, replica_groups=mesh['grp'=2,'ylo'=2,'zfar'=8,'znear'=2,'core'=2,'narrow'=4] {'zfar'}, dimensions={0} | all-to-all | bytes 458752 | tf_op jit(solution)/shard_map/all_to_all | solution.py:44
  148.9 0.7 reduce_sum.12
  (1 shorter events, 0.0 us)
Async XLA Ops:
  3.0 36.5 %all-to-all-start = ((bf16[8,32,512]{2,1,0:T(8,128)(2,1)}), bf16[8,32,512]{2,1,0:T(8,128)(2,1)S(1)}, u32[]{:S(2)}, u32[]{:S(2)}) async-start(bf16[8,32,512]{2,1,0:T(8,128)(2,1)} %shard_map.64), calls=%async_computation | async-start | bytes 524288 | tf_op jit(solution)/shard_map/all_to_all | solution.py:44
  22.8 23.0 %collective-permute-start = (bf16[3,448,256]{2,1,0:T(8,128)(2,1)}, bf16[3,448,256]{2,1,0:T(8,128)(2,1)S(1)}, u32[]{:S(2)}, u32[]{:S(2)}) collective-permute-start(bf16[3,448,256]{2,1,0:T(8,128)(2,1)} %get-tuple-element.13), channel_id=1, source_target_pairs={{0,1},{1,2},{2,3},{3,0},{4,5},{5,6},{6,7},{7,4},{8,9},{9,10},{10,1... | collective-permute-start | bytes 2064392 | tf_op jit(solution)/shard_map/ppermute | solution.py:227
  26.2 22.0 %collective-permute-start.1 = (bf16[3,448,256]{2,1,0:T(8,128)(2,1)}, bf16[3,448,256]{2,1,0:T(8,128)(2,1)S(1)}, u32[]{:S(2)}, u32[]{:S(2)}) collective-permute-start(bf16[3,448,256]{2,1,0:T(8,128)(2,1)} %get-tuple-element.14), channel_id=1, source_target_pairs={{0,2},{1,3},{2,0},{3,1},{4,6},{5,7},{6,4},{7,5},{8,10},{9,11},{10,... | collective-permute-start | bytes 2064392 | tf_op jit(solution)/shard_map/ppermute | solution.py:227
  29.2 31.9 %collective-permute-start.2 = (bf16[3,448,256]{2,1,0:T(8,128)(2,1)}, bf16[3,448,256]{2,1,0:T(8,128)(2,1)S(1)}, u32[]{:S(2)}, u32[]{:S(2)}) collective-permute-start(bf16[3,448,256]{2,1,0:T(8,128)(2,1)} %get-tuple-element.15), channel_id=1, source_target_pairs={{0,3},{1,0},{2,1},{3,2},{4,7},{5,4},{6,5},{7,6},{8,11},{9,8},{10,9... | collective-permute-start | bytes 2064392 | tf_op jit(solution)/shard_map/ppermute | solution.py:227
  41.2 21.3 %all-to-all-start.1 = ((bf16[16,64,448]{2,1,0:T(8,128)(2,1)}), bf16[16,64,448]{2,1,0:T(8,128)(2,1)}, u32[]{:S(2)}, u32[]{:S(2)}) async-start(bf16[16,64,448]{2,1,0:T(8,128)(2,1)} %get-tuple-element.11), calls=%async_computation.1 | async-start | bytes 2097152 | tf_op jit(solution)/shard_map/all_to_all | solution.py:44
  61.1 1.3 copy-start
  61.2 1.3 copy-start.1

commit v5 on v4

v5 whole, which is shorter than its diff:
```python
import functools

import jax
import jax.numpy as jnp
from jax import lax
from jax.experimental import pallas as pl
from jax.experimental.pallas import tpu as pltpu
from jax.sharding import Mesh, PartitionSpec as P

CAP = 8
F32 = jnp.float32
BF16 = jnp.bfloat16
I32 = jnp.int32
FAR = "zfar"
NEAR = ("grp", "ylo", "znear", "core")
AXES = ("grp", "ylo", "zfar", "znear", "core", "narrow")
WIDE = ("ylo", "zfar", "znear", "core")
LANES = 512
HOLD = 200 * 10**9

VMEM = pl.BlockSpec(memory_space=pltpu.VMEM)
SMEM = pl.BlockSpec(memory_space=pltpu.SMEM)
ANY = pl.BlockSpec(memory_space=pl.ANY)
HBM = pl.BlockSpec(memory_space=pltpu.HBM)


def call(body, outs, specs, args, flops=0, scratch=(), mib=16, place=None):
    single = not isinstance(outs, list)
    outs = [outs] if single else outs
    nbytes = sum(a.size * a.dtype.itemsize for a in args) + sum(o.size * o.dtype.itemsize for o in outs)
    got = pl.pallas_call(
        body,
        out_shape=outs,
        in_specs=specs,
        out_specs=[place or VMEM] * len(outs),
        scratch_shapes=list(scratch),
        compiler_params=pltpu.CompilerParams(vmem_limit_bytes=mib * 1024 * 1024),
        cost_estimate=pl.CostEstimate(flops=flops, bytes_accessed=nbytes, transcendentals=0),
    )(*args)
    return got[0] if single else got


def exchange(x, axis):
    return lax.all_to_all(x, axis, split_axis=0, concat_axis=0, tiled=True)


def rows_body(part, top, hidden_hbm, routes_hbm, gates_hbm, out_ref, wide_ref, routes_ref, gates_ref, sems):
    count, tok, lanes = out_ref.shape
    odd = lax.axis_index("grp")
    start = pl.multiple_of(lax.axis_index("narrow") * 2 * part + odd * (part // 128 * 128), 128)
    copies = [
        pltpu.make_async_copy(hidden_hbm.at[:, pl.ds(start, LANES)], wide_ref, sems.at[0]),
        pltpu.make_async_copy(routes_hbm, routes_ref, sems.at[1]),
        pltpu.make_async_copy(gates_hbm, gates_ref, sems.at[2]),
    ]
    for copy in copies:
        copy.start()
    for copy in copies:
        copy.wait()
    wide = wide_ref[...].astype(F32)
    mine = jnp.where(odd == 1, wide[:, LANES - part :], wide[:, :part])
    gates = gates_ref[...]
    high = gates.astype(BF16).astype(F32)
    extra = jnp.concatenate([routes_ref[...].astype(F32), high, gates - high], axis=0).astype(BF16)
    eye = (lax.broadcasted_iota(I32, (tok, tok), 0) == lax.broadcasted_iota(I32, (tok, tok), 1)).astype(BF16)
    extra = lax.dot_general(eye, extra, (((1,), (1,)), ((), ())), preferred_element_type=F32)
    spare = jnp.zeros((tok, lanes - part - 3 * top), F32)
    rows = jnp.concatenate([mine, extra, spare], axis=1).astype(BF16)
    for i in range(count):
        out_ref[i] = rows


def pack_body(n_nar, part, gate_hbm, up_hbm, down_hbm, *rest):
    outs, (down_ref, turned_ref, sems, turned_sems, down_sem) = rest[:n_nar], rest[n_nar:]
    units = gate_hbm.shape[2]
    me = lax.axis_index("narrow")
    fetch = pltpu.make_async_copy(down_hbm.at[0], down_ref, down_sem)
    fetch.start()
    copies = []
    for k in range(1, n_nar + 1):
        k = k % n_nar
        to = lax.rem(me + k, n_nar)
        for i in range(2):
            rows = pl.ds(pl.multiple_of((to * 2 + i) * part, 64), part)
            for m, source in enumerate((gate_hbm, up_hbm)):
                place = outs[k].at[i, :, m * units : (m + 1) * units]
                copies.append(pltpu.make_async_copy(source.at[0, rows], place, sems.at[k, i, m]))
    for copy in copies:
        copy.start()
    fetch.wait()
    turned_ref[...] = jnp.transpose(down_ref[...])
    for k in range(n_nar):
        to = lax.rem(me + k, n_nar)
        for i in range(2):
            rows = pl.ds(pl.multiple_of((i * n_nar + to) * part, 64), part)
            place = outs[k].at[2, :, i * units : (i + 1) * units]
            copy = pltpu.make_async_copy(turned_ref.at[rows], place, turned_sems.at[k, i])
            copy.start()
            copies.append(copy)
    for copy in copies:
        copy.wait()


def arrived_body(*refs):
    refs[-1][...] = jnp.zeros(refs[-1].shape, F32)


def slots_of(part, top, rows_ref):
    blocks, tok, _ = rows_ref.shape
    count = blocks * tok
    extra = rows_ref[...].reshape(count, LANES)[:, part : part + 3 * top]
    eye = (
        lax.broadcasted_iota(I32, (3 * top, 3 * top), 0) == lax.broadcasted_iota(I32, (3 * top, 3 * top), 1)
    ).astype(BF16)
    extra = lax.dot_general(eye, extra, (((1,), (1,)), ((), ())), preferred_element_type=F32)
    j = lax.broadcasted_iota(I32, (8, count), 0)
    z_count = 2 * lax.axis_size(FAR)
    expert = (((j // 4) * z_count + lax.axis_index(FAR) * 2 + (j // 2) % 2) * 2 + j % 2).astype(F32)
    chosen = jnp.zeros((8, count), F32)
    gate = jnp.zeros((8, count), F32)
    for k in range(top):
        same = extra[k : k + 1] == expert
        chosen = jnp.where(same, 1.0, chosen)
        value = extra[top + k : top + k + 1] + extra[2 * top + k : 2 * top + k + 1]
        gate = gate + jnp.where(same, value, 0.0)
    first = lax.broadcasted_iota(I32, (count, count), 0)
    second = lax.broadcasted_iota(I32, (count, count), 1)
    before = ((first < second) & (first // tok == second // tok)).astype(BF16)
    place = jnp.dot(chosen.astype(BF16), before, preferred_element_type=F32)
    block = (lax.broadcasted_iota(I32, (8, count), 1) // tok).astype(F32)
    slot = jnp.where(chosen > 0.0, place + block * CAP, -1.0)
    want = lax.broadcasted_iota(I32, (8, blocks * CAP, count), 1).astype(F32)
    return slot[:, None, :] == want, gate


def pick_body(part, top, rows_ref, out_ref):
    near, half, _ = out_ref.shape
    near = near // 2
    hit, _ = slots_of(part, top, rows_ref)
    picker = jnp.where(hit, 1.0, 0.0).astype(BF16)
    rows = rows_ref[...].reshape(-1, LANES)[:, :part]
    sides = []
    for i in range(2):
        left = picker[:, i * half : (i + 1) * half].reshape(near * half, -1)
        sides.append(jnp.dot(left, rows, preferred_element_type=F32))
    got = jnp.concatenate(sides, axis=1).astype(BF16).reshape(near, half, 2 * part)
    out_ref[:near] = got
    out_ref[near:] = got


def weight_body(part, top, rows_ref, out_ref):
    _, half, count = out_ref.shape
    hit, gate = slots_of(part, top, rows_ref)
    weight = jnp.where(hit, gate[:, None, :], 0.0)
    high = weight.astype(BF16)
    low = (weight - high.astype(F32)).astype(BF16)
    both = jnp.concatenate([high, low], axis=2)
    near = both.shape[0]
    for i in range(2):
        side = both[:, i * (both.shape[1] // 2) : (i + 1) * (both.shape[1] // 2)]
        out_ref[i] = side.reshape(half, count)


def two_sides(rows, part):
    rows = rows.reshape(-1, 2 * part)
    return jnp.concatenate([rows[:, :part], rows[:, part:]], axis=0)


def gate_up_body(n_nar, rows_ref, *rest):
    parts, out_ref = rest[:n_nar], rest[-1]
    me = lax.axis_index("narrow")
    part = rows_ref.shape[2] // 2
    half = rows_ref.shape[0] // 2
    left = two_sides(rows_ref[:half], part)
    right = two_sides(rows_ref[half:], part)
    for k in range(n_nar):
        act = jnp.dot(left, parts[k][0], preferred_element_type=F32)
        act = act + jnp.dot(right, parts[k][1], preferred_element_type=F32)
        out_ref[lax.rem(me - k + n_nar, n_nar)] = act.astype(BF16)


def inner_body(acts_ref, out_ref):
    count, _, units = out_ref.shape
    act = sum(acts_ref[i].astype(F32) for i in range(count))
    gate, up = act[:, :units], act[:, units:]
    inner = (gate / (1.0 + jnp.exp(-gate)) * up).astype(BF16)
    for i in range(count):
        out_ref[i] = inner


def down_body(n_nar, inner_ref, *rest):
    parts, out_ref = rest[:n_nar], rest[-1]
    me = lax.axis_index("narrow")
    near = out_ref.shape[0] // 2
    units = inner_ref.shape[2]
    left = jnp.concatenate([inner_ref[lax.rem(me - k + n_nar, n_nar)] for k in range(n_nar)], axis=1)
    count = left.shape[0] // 2
    for i in range(2):
        right = jnp.concatenate([parts[k][2, :, i * units : (i + 1) * units] for k in range(n_nar)], axis=1)
        out = lax.dot_general(left, right, (((1,), (1,)), ((), ())), preferred_element_type=F32)
        out = jnp.concatenate([out[:count], out[count:]], axis=1).astype(BF16)
        out_ref[i * near : (i + 1) * near] = out.reshape(near, -1, out.shape[1])


def combine_body(rows_ref, weight_ref, out_ref):
    blocks, half, width = out_ref.shape
    near = rows_ref.shape[0] // 2
    part = width // 2
    total = 0.0
    for i in range(2):
        rows = rows_ref[i * near : (i + 1) * near].reshape(-1, width)
        for h in range(2):
            side = rows[:, h * part : (h + 1) * part]
            total = total + lax.dot_general(
                weight_ref[h], side, (((0,), (0,)), ((), ())), preferred_element_type=F32
            )
    count = total.shape[0] // 2
    total = (total[:count] + total[count:]).reshape(blocks, 2 * half, part)
    total = jnp.concatenate([total[:, :half], total[:, half:]], axis=2)
    out_ref[...] = total.astype(BF16)


def last_body(sums_ref, out_ref):
    total = sum(sums_ref[i].astype(F32) for i in range(sums_ref.shape[0]))
    half, width = total.shape
    out_ref[:half] = total[:, : width // 2].astype(BF16)
    out_ref[half:] = total[:, width // 2 :].astype(BF16)


def per_device(hidden, routes, route_gates, gate_proj, up_proj, down_proj):
    tok, width = hidden.shape
    top = routes.shape[1]
    n_grp, n_nar, n_far = lax.axis_size("grp"), lax.axis_size("narrow"), lax.axis_size(FAR)
    units = gate_proj.shape[2]
    part = width // (n_grp * n_nar)
    near = 16
    slots = 8 * n_far * CAP

    rows = call(
        functools.partial(rows_body, part, top),
        jax.ShapeDtypeStruct((n_far, tok, LANES), BF16),
        [HBM, HBM, HBM],
        [hidden, routes.T, route_gates.T],
        scratch=[
            pltpu.VMEM((tok, LANES), BF16),
            pltpu.VMEM((top, tok), I32),
            pltpu.VMEM((top, tok), F32),
            pltpu.SemaphoreType.DMA((3,)),
        ],
        mib=60,
    )
    rows = exchange(rows, FAR)

    parts = call(
        functools.partial(pack_body, n_nar, part),
        [jax.ShapeDtypeStruct((3, part, 2 * units), BF16)] * n_nar,
        [HBM, HBM, HBM],
        [gate_proj, up_proj, down_proj],
        place=HBM,
        scratch=[
            pltpu.VMEM((units, width), BF16),
            pltpu.VMEM((width, units), BF16),
            pltpu.SemaphoreType.DMA((n_nar, 2, 2)),
            pltpu.SemaphoreType.DMA((n_nar, 2)),
            pltpu.SemaphoreType.DMA,
        ],
        mib=60,
    )
    parts = list(parts)
    for k in range(1, n_nar):
        parts[k] = lax.ppermute(parts[k], "narrow", [(i, (i + k) % n_nar) for i in range(n_nar)])
    arrived = call(
        arrived_body, jax.ShapeDtypeStruct((8, 128), F32), [ANY] * (n_nar - 1), parts[1:], flops=HOLD
    )

    half = n_far * CAP // 2
    picked = call(
        functools.partial(pick_body, part, top),
        jax.ShapeDtypeStruct((near, half, 2 * part), BF16),
        [VMEM],
        [rows],
        flops=2 * slots * n_far * tok * part,
    )
    weight = call(
        functools.partial(weight_body, part, top),
        jax.ShapeDtypeStruct((2, slots // 2, 2 * n_far * tok), BF16),
        [VMEM],
        [rows],
    )
    rows = exchange(picked, NEAR)

    acts = call(
        functools.partial(gate_up_body, n_nar),
        jax.ShapeDtypeStruct((n_nar, slots, 2 * units), BF16),
        [VMEM] + [VMEM] * n_nar + [ANY],
        [rows] + parts + [arrived],
        flops=2 * slots * part * 2 * units * 2 * n_nar,
    )
    acts = exchange(acts, "narrow")
    inner = call(inner_body, jax.ShapeDtypeStruct((n_nar, slots, units), BF16), [VMEM], [acts])
    inner = exchange(inner, "narrow")
    outs = call(
        functools.partial(down_body, n_nar),
        jax.ShapeDtypeStruct((near, half, 2 * part), BF16),
        [VMEM] + [VMEM] * n_nar,
        [inner] + parts,
        flops=2 * slots * units * n_nar * 2 * part,
    )
    outs = exchange(outs, NEAR)
    sums = call(
        combine_body,
        jax.ShapeDtypeStruct((n_far, tok // 2, 2 * part), BF16),
        [VMEM, VMEM],
        [outs, weight],
        flops=2 * slots * 2 * 2 * n_far * tok * part,
    )
    sums = exchange(sums, FAR)
    return call(last_body, jax.ShapeDtypeStruct((tok, part), BF16), [VMEM], [sums])


def solution(mesh):
    n_grp, n_wide, n_nar = mesh.devices.shape
    fine = Mesh(mesh.devices.reshape(n_grp, 2, n_wide // 8, 2, 2, n_nar), AXES)
    return jax.shard_map(
        per_device,
        mesh=fine,
        in_specs=(
            P(WIDE, None),
            P(WIDE, None),
            P(WIDE, None),
            P(WIDE, None, ("grp", "narrow")),
            P(WIDE, None, ("grp", "narrow")),
            P(WIDE, ("grp", "narrow"), None),
        ),
        out_specs=P(WIDE, ("grp", "narrow")),
        check_vma=False,
    )
```

time: 150 us -> 200 us (1.33)
  Pallas kernels: 13.3 us -> 66.7 us
  blocking collectives: 81.8 us -> 59.4 us
  waiting for transfers between devices: 22.8 us -> 35.8 us
  starting transfers between devices: 30.2 us -> 35.9 us
    pallas_call x8 -> x10, Pallas kernels: 13.3 us -> 66.7 us  [call(): pl.pallas_call(body, out_shape=outs, in_specs=specs, out_specs=[place or...]
    all_to_all x4 -> x3, blocking collectives: 81.8 us -> 59.4 us  [exchange(): return lax.all_to_all(x, axis, split_axis=0, concat_axis=0, tiled=True)]
    all_to_all x2 -> x3, waiting for transfers between devices: 7.48 us -> 14.7 us  [exchange(): return lax.all_to_all(x, axis, split_axis=0, concat_axis=0, tiled=True)]
    ppermute x3, waiting for transfers between devices: 15.4 us -> 21.1 us  [per_device(): lax.ppermute(parts[k], 'narrow', [(i, (i + k) % n_nar) for i in range(n_n...]
    all_to_all x2 -> x3, starting transfers between devices: 19.7 us -> 25.4 us  [exchange(): return lax.all_to_all(x, axis, split_axis=0, concat_axis=0, tiled=True)]
  transfers between devices with their start and end apart: 5 -> 6, of which waited for: 4 -> 4; matrix products, arithmetic and copies ran while one was open for 0% -> 0% of each run, Pallas kernels for 4% -> 30%
where the time goes in v5:
time: 200 us; the launch traced here: 199 us
  Pallas kernels  66.7 us (33%)
  blocking collectives  59.4 us (30%)
  starting transfers between devices  35.9 us (18%)
  waiting for transfers between devices  35.8 us (18%)
    pallas_call x10, Pallas kernels, call(): pl.pallas_call(body, out_shape=outs, in_specs=specs, out_specs=[place or...  66.7 us
    all_to_all x3, blocking collectives, exchange(): return lax.all_to_all(x, axis, split_axis=0, concat_axis=0, tiled=True)  59.4 us
    all_to_all x3, starting transfers between devices, exchange(): return lax.all_to_all(x, axis, split_axis=0, concat_axis=0, tiled=True)  25.4 us
    ppermute x3, waiting for transfers between devices, per_device(): lax.ppermute(parts[k], 'narrow', [(i, (i + k) % n_nar) for i in range(n_n...  21.1 us
    all_to_all x3, waiting for transfers between devices, exchange(): return lax.all_to_all(x, axis, split_axis=0, concat_axis=0, tiled=True)  14.7 us
    ppermute x3, starting transfers between devices, per_device(): lax.ppermute(parts[k], 'narrow', [(i, (i + k) % n_nar) for i in range(n_n...  10.5 us
  transfers between devices with their start and end apart: 6, of which 4 were waited for; matrix products, arithmetic and copies ran while one was open for 0% of the time, Pallas kernels for 30%

profile of v5, /device:TPU:2, one launch (start us, length us, event | category | flops | bytes accessed | tf_op | source)
XLA Modules:
  0.0 199.0 jit_solution(8186022989641149737)
XLA Ops:
  0.0 1.7 shard_map.64
  1.7 15.1 %all-to-all-start = ((bf16[8,32,512]{2,1,0:T(8,128)(2,1)}), bf16[8,32,512]{2,1,0:T(8,128)(2,1)S(1)}, u32[]{:S(2)}, u32[]{:S(2)}) async-start(bf16[8,32,512]{2,1,0:T(8,128)(2,1)} %shard_map.64), calls=%async_computation | async-start | bytes 524288 | tf_op jit(solution)/shard_map/all_to_all | solution.py:44
  16.8 56.9 %shard_map.66 = (bf16[3,448,256]{2,1,0:T(8,128)(2,1)}, bf16[3,448,256]{2,1,0:T(8,128)(2,1)}, bf16[3,448,256]{2,1,0:T(8,128)(2,1)}, bf16[3,448,256]{2,1,0:T(8,128)(2,1)}) custom-call(bf16[1,3584,128]{2,1,0:T(8,128)(2,1)} %gate_hbm.1, bf16[1,3584,128]{2,1,0:T(8,128)(2,1)} %up_hbm.1, bf16[1,128,3584]{2,1,0:T(8,128)(2,1)} %down_hbm.1), custom_call_target="tpu_custom_call" | custom-call | bytes 5505024 | tf_op jit(solution)/shard_map/pallas_call | solution.py:31
  73.7 3.4 %collective-permute-start = (bf16[3,448,256]{2,1,0:T(8,128)(2,1)}, bf16[3,448,256]{2,1,0:T(8,128)(2,1)S(1)}, u32[]{:S(2)}, u32[]{:S(2)}) collective-permute-start(bf16[3,448,256]{2,1,0:T(8,128)(2,1)} %get-tuple-element.10), channel_id=1, source_target_pairs={{0,1},{1,2},{2,3},{3,0},{4,5},{5,6},{6,7},{7,4},{8,9},{9,10},{10,1... | collective-permute-start | bytes 2064392 | tf_op jit(solution)/shard_map/ppermute | solution.py:271
  77.2 3.0 %collective-permute-start.1 = (bf16[3,448,256]{2,1,0:T(8,128)(2,1)}, bf16[3,448,256]{2,1,0:T(8,128)(2,1)S(1)}, u32[]{:S(2)}, u32[]{:S(2)}) collective-permute-start(bf16[3,448,256]{2,1,0:T(8,128)(2,1)} %get-tuple-element.11), channel_id=1, source_target_pairs={{0,2},{1,3},{2,0},{3,1},{4,6},{5,7},{6,4},{7,5},{8,10},{9,11},{10,... | collective-permute-start | bytes 2064392 | tf_op jit(solution)/shard_map/ppermute | solution.py:271
  80.2 4.1 %collective-permute-start.2 = (bf16[3,448,256]{2,1,0:T(8,128)(2,1)}, bf16[3,448,256]{2,1,0:T(8,128)(2,1)S(1)}, u32[]{:S(2)}, u32[]{:S(2)}) collective-permute-start(bf16[3,448,256]{2,1,0:T(8,128)(2,1)} %get-tuple-element.12), channel_id=1, source_target_pairs={{0,3},{1,0},{2,1},{3,2},{4,7},{5,4},{6,5},{7,6},{8,11},{9,8},{10,9... | collective-permute-start | bytes 2064392 | tf_op jit(solution)/shard_map/ppermute | solution.py:271
  84.2 0.0 all-to-all-done.rows_ref
  84.3 0.0 copy-start.1
  84.3 1.7 shard_map.65
  85.9 0.0 copy-done.1
  85.9 5.1 %all-to-all-start.1 = ((bf16[16,32,896]{2,1,0:T(8,128)(2,1)}), bf16[16,32,896]{2,1,0:T(8,128)(2,1)}, u32[]{:S(2)}, u32[]{:S(2)}) async-start(bf16[16,32,896]{2,1,0:T(8,128)(2,1)} %shard_map.65), calls=%async_computation.1 | async-start | bytes 1835008 | tf_op jit(solution)/shard_map/all_to_all | solution.py:44
  91.0 3.2 %collective-permute-done.refs_0_.rest_1_ = bf16[3,448,256]{2,1,0:T(8,128)(2,1)S(1)} collective-permute-done((bf16[3,448,256]{2,1,0:T(8,128)(2,1)}, bf16[3,448,256]{2,1,0:T(8,128)(2,1)S(1)}, u32[]{:S(2)}, u32[]{:S(2)}) %collective-permute-start) | collective-permute-done | bytes 688160 | tf_op jit(solution)/shard_map/ppermute | solution.py:271
  94.2 5.0 %collective-permute-done.1.refs_1_.rest_2_ = bf16[3,448,256]{2,1,0:T(8,128)(2,1)S(1)} collective-permute-done((bf16[3,448,256]{2,1,0:T(8,128)(2,1)}, bf16[3,448,256]{2,1,0:T(8,128)(2,1)S(1)}, u32[]{:S(2)}, u32[]{:S(2)}) %collective-permute-start.1) | collective-permute-done | bytes 688160 | tf_op jit(solution)/shard_map/ppermute | solution.py:271
  99.2 12.9 %collective-permute-done.2.refs_2_.rest_3_ = bf16[3,448,256]{2,1,0:T(8,128)(2,1)S(1)} collective-permute-done((bf16[3,448,256]{2,1,0:T(8,128)(2,1)}, bf16[3,448,256]{2,1,0:T(8,128)(2,1)S(1)}, u32[]{:S(2)}, u32[]{:S(2)}) %collective-permute-start.2) | collective-permute-done | bytes 688160 | tf_op jit(solution)/shard_map/ppermute | solution.py:271
  112.1 0.0 copy-start
  112.1 0.0 all-to-all-done.1.rows_ref
  112.1 1.1 copy-done
  113.2 2.4 %shard_map.68 = bf16[4,512,256]{2,1,0:T(8,128)(2,1)S(1)} custom-call(bf16[16,32,896]{2,1,0:T(8,128)(2,1)} %all-to-all-done.1.rows_ref, bf16[3,448,256]{2,1,0:T(8,128)(2,1)S(1)} %copy-done, bf16[3,448,256]{2,1,0:T(8,128)(2,1)S(1)} %collective-permute-done.refs_0_.rest_1_, bf16[3,448,256]{2,1,0:T(8,128)(2,1)S(1)} %collective-permute-done.1.refs_1_.rest_2_, ...), custom_call_target="tpu_custom_call" | custom-call | flops 939524096 | bytes 4722688 | tf_op jit(solution)/shard_map/pallas_call | solution.py:31
  115.7 17.2 %all_to_all.30.acts_ref = bf16[4,512,256]{2,1,0:T(8,128)(2,1)S(1)} all-to-all(bf16[4,512,256]{2,1,0:T(8,128)(2,1)S(1)} %shard_map.68), channel_id=1, replica_groups=mesh['grp'=2,'ylo'=2,'zfar'=8,'znear'=2,'core'=2,'narrow'=4] {'narrow'}, dimensions={0} | all-to-all | bytes 2097152 | tf_op jit(solution)/shard_map/all_to_all | solution.py:44
  132.8 0.2 shard_map.69
  133.0 10.7 %all_to_all.31.inner_ref = bf16[4,512,128]{2,1,0:T(8,128)(2,1)S(1)} all-to-all(bf16[4,512,128]{2,1,0:T(8,128)(2,1)S(1)} %shard_map.69), channel_id=1, replica_groups=mesh['grp'=2,'ylo'=2,'zfar'=8,'znear'=2,'core'=2,'narrow'=4] {'narrow'}, dimensions={0} | all-to-all | bytes 1048576 | tf_op jit(solution)/shard_map/all_to_all | solution.py:44
  143.8 1.7 shard_map.70
  145.5 0.0 copy-start.2
  145.5 5.2 %all-to-all-start.4 = ((bf16[16,32,896]{2,1,0:T(8,128)(2,1)}), bf16[16,32,896]{2,1,0:T(8,128)(2,1)S(1)}, u32[]{:S(2)}, u32[]{:S(2)}) async-start(bf16[16,32,896]{2,1,0:T(8,128)(2,1)} %shard_map.70), calls=%async_computation.4 | async-start | bytes 1835008 | tf_op jit(solution)/shard_map/all_to_all | solution.py:44
  150.7 0.0 copy-done.2
  150.7 0.5 shard_map.71.weight_ref
  151.2 14.6 %all-to-all-done.4.rows_ref = bf16[16,32,896]{2,1,0:T(8,128)(2,1)S(1)} async-done(((bf16[16,32,896]{2,1,0:T(8,128)(2,1)}), bf16[16,32,896]{2,1,0:T(8,128)(2,1)S(1)}, u32[]{:S(2)}, u32[]{:S(2)}) %all-to-all-start.4) | async-done | bytes 917536 | tf_op jit(solution)/shard_map/all_to_all | solution.py:44
  165.9 0.9 shard_map.72
  166.8 31.5 %all_to_all.32.sums_ref = bf16[8,16,896]{2,1,0:T(8,128)(2,1)S(1)} all-to-all(bf16[8,16,896]{2,1,0:T(8,128)(2,1)S(1)} %shard_map.72), channel_id=1, replica_groups=mesh['grp'=2,'ylo'=2,'zfar'=8,'znear'=2,'core'=2,'narrow'=4] {'zfar'}, dimensions={0} | all-to-all | bytes 458752 | tf_op jit(solution)/shard_map/all_to_all | solution.py:44
  198.3 0.7 shard_map.73
  (1 shorter events, 0.0 us)
Async XLA Ops:
  1.7 82.5 %all-to-all-start = ((bf16[8,32,512]{2,1,0:T(8,128)(2,1)}), bf16[8,32,512]{2,1,0:T(8,128)(2,1)S(1)}, u32[]{:S(2)}, u32[]{:S(2)}) async-start(bf16[8,32,512]{2,1,0:T(8,128)(2,1)} %shard_map.64), calls=%async_computation | async-start | bytes 524288 | tf_op jit(solution)/shard_map/all_to_all | solution.py:44
  73.7 20.5 %collective-permute-start = (bf16[3,448,256]{2,1,0:T(8,128)(2,1)}, bf16[3,448,256]{2,1,0:T(8,128)(2,1)S(1)}, u32[]{:S(2)}, u32[]{:S(2)}) collective-permute-start(bf16[3,448,256]{2,1,0:T(8,128)(2,1)} %get-tuple-element.10), channel_id=1, source_target_pairs={{0,1},{1,2},{2,3},{3,0},{4,5},{5,6},{6,7},{7,4},{8,9},{9,10},{10,1... | collective-permute-start | bytes 2064392 | tf_op jit(solution)/shard_map/ppermute | solution.py:271
  77.2 22.0 %collective-permute-start.1 = (bf16[3,448,256]{2,1,0:T(8,128)(2,1)}, bf16[3,448,256]{2,1,0:T(8,128)(2,1)S(1)}, u32[]{:S(2)}, u32[]{:S(2)}) collective-permute-start(bf16[3,448,256]{2,1,0:T(8,128)(2,1)} %get-tuple-element.11), channel_id=1, source_target_pairs={{0,2},{1,3},{2,0},{3,1},{4,6},{5,7},{6,4},{7,5},{8,10},{9,11},{10,... | collective-permute-start | bytes 2064392 | tf_op jit(solution)/shard_map/ppermute | solution.py:271
  80.2 31.9 %collective-permute-start.2 = (bf16[3,448,256]{2,1,0:T(8,128)(2,1)}, bf16[3,448,256]{2,1,0:T(8,128)(2,1)S(1)}, u32[]{:S(2)}, u32[]{:S(2)}) collective-permute-start(bf16[3,448,256]{2,1,0:T(8,128)(2,1)} %get-tuple-element.12), channel_id=1, source_target_pairs={{0,3},{1,0},{2,1},{3,2},{4,7},{5,4},{6,5},{7,6},{8,11},{9,8},{10,9... | collective-permute-start | bytes 2064392 | tf_op jit(solution)/shard_map/ppermute | solution.py:271
  84.3 1.7 copy-start.1
  85.9 26.2 %all-to-all-start.1 = ((bf16[16,32,896]{2,1,0:T(8,128)(2,1)}), bf16[16,32,896]{2,1,0:T(8,128)(2,1)}, u32[]{:S(2)}, u32[]{:S(2)}) async-start(bf16[16,32,896]{2,1,0:T(8,128)(2,1)} %shard_map.65), calls=%async_computation.1 | async-start | bytes 1835008 | tf_op jit(solution)/shard_map/all_to_all | solution.py:44
  112.1 1.1 copy-start
  145.5 5.2 %copy-start.2 = (bf16[8,32,512]{2,1,0:T(8,128)(2,1)S(1)}, bf16[8,32,512]{2,1,0:T(8,128)(2,1)}, u32[]{:S(2)}) copy-start(bf16[8,32,512]{2,1,0:T(8,128)(2,1)} %copy-done.1) | copy-start | bytes 786436
  145.5 20.4 %all-to-all-start.4 = ((bf16[16,32,896]{2,1,0:T(8,128)(2,1)}), bf16[16,32,896]{2,1,0:T(8,128)(2,1)S(1)}, u32[]{:S(2)}, u32[]{:S(2)}) async-start(bf16[16,32,896]{2,1,0:T(8,128)(2,1)} %shard_map.70), calls=%async_computation.4 | async-start | bytes 1835008 | tf_op jit(solution)/shard_map/all_to_all | solution.py:44

commit v6 on v5

--- a/solution.py
+++ b/solution.py
@@ -24,7 +24,7 @@
 HBM = pl.BlockSpec(memory_space=pltpu.HBM)
 
 
-def call(body, outs, specs, args, flops=0, scratch=(), mib=16, place=None):
+def call(body, outs, specs, args, flops=0, scratch=(), mib=16):
     single = not isinstance(outs, list)
     outs = [outs] if single else outs
     nbytes = sum(a.size * a.dtype.itemsize for a in args) + sum(o.size * o.dtype.itemsize for o in outs)
@@ -32,7 +32,7 @@
         body,
         out_shape=outs,
         in_specs=specs,
-        out_specs=[place or VMEM] * len(outs),
+        out_specs=[VMEM] * len(outs),
         scratch_shapes=list(scratch),
         compiler_params=pltpu.CompilerParams(vmem_limit_bytes=mib * 1024 * 1024),
         cost_estimate=pl.CostEstimate(flops=flops, bytes_accessed=nbytes, transcendentals=0),
@@ -71,14 +71,13 @@
 
 
 def pack_body(n_nar, part, gate_hbm, up_hbm, down_hbm, *rest):
-    outs, (down_ref, turned_ref, sems, turned_sems, down_sem) = rest[:n_nar], rest[n_nar:]
+    outs, (down_ref, turned_ref, sems, down_sem) = rest[:n_nar], rest[n_nar:]
     units = gate_hbm.shape[2]
     me = lax.axis_index("narrow")
     fetch = pltpu.make_async_copy(down_hbm.at[0], down_ref, down_sem)
     fetch.start()
     copies = []
-    for k in range(1, n_nar + 1):
-        k = k % n_nar
+    for k in range(n_nar):
         to = lax.rem(me + k, n_nar)
         for i in range(2):
             rows = pl.ds(pl.multiple_of((to * 2 + i) * part, 64), part)
@@ -93,10 +92,7 @@
         to = lax.rem(me + k, n_nar)
         for i in range(2):
             rows = pl.ds(pl.multiple_of((i * n_nar + to) * part, 64), part)
-            place = outs[k].at[2, :, i * units : (i + 1) * units]
-            copy = pltpu.make_async_copy(turned_ref.at[rows], place, turned_sems.at[k, i])
-            copy.start()
-            copies.append(copy)
+            outs[k][2, :, i * units : (i + 1) * units] = turned_ref[rows]
     for copy in copies:
         copy.wait()
 
@@ -256,12 +252,10 @@
         [jax.ShapeDtypeStruct((3, part, 2 * units), BF16)] * n_nar,
         [HBM, HBM, HBM],
         [gate_proj, up_proj, down_proj],
-        place=HBM,
         scratch=[
             pltpu.VMEM((units, width), BF16),
             pltpu.VMEM((width, units), BF16),
             pltpu.SemaphoreType.DMA((n_nar, 2, 2)),
-            pltpu.SemaphoreType.DMA((n_nar, 2)),
             pltpu.SemaphoreType.DMA,
         ],
         mib=60,

time: 200 us -> 147 us (0.73)
  Pallas kernels: 66.7 us -> 13.8 us
    pallas_call x10, Pallas kernels: 66.7 us -> 13.8 us  [call(): pl.pallas_call(body, out_shape=outs, in_specs=specs, out_specs=[VMEM] * l...]
    all_to_all x3, waiting for transfers between devices: 14.7 us -> 22 us  [exchange(): return lax.all_to_all(x, axis, split_axis=0, concat_axis=0, tiled=True)]
    ppermute x3, waiting for transfers between devices: 21.1 us -> 14.7 us  [per_device(): lax.ppermute(parts[k], 'narrow', [(i, (i + k) % n_nar) for i in range(n_n...]
  transfers between devices with their start and end apart: 6 -> 6, of which waited for: 4 -> 5; matrix products, arithmetic and copies ran while one was open for 0% -> 0% of each run, Pallas kernels for 30% -> 4%
where the time goes in v6:
time: 147 us; the launch traced here: 146 us
  blocking collectives  59.7 us (41%)
  waiting for transfers between devices  36.7 us (25%)
  starting transfers between devices  35.1 us (24%)
  Pallas kernels  13.8 us (9%)
    all_to_all x3, blocking collectives, exchange(): return lax.all_to_all(x, axis, split_axis=0, concat_axis=0, tiled=True)  59.7 us
    all_to_all x3, starting transfers between devices, exchange(): return lax.all_to_all(x, axis, split_axis=0, concat_axis=0, tiled=True)  24.6 us
    all_to_all x3, waiting for transfers between devices, exchange(): return lax.all_to_all(x, axis, split_axis=0, concat_axis=0, tiled=True)  22 us
    ppermute x3, waiting for transfers between devices, per_device(): lax.ppermute(parts[k], 'narrow', [(i, (i + k) % n_nar) for i in range(n_n...  14.7 us
    pallas_call x10, Pallas kernels, call(): pl.pallas_call(body, out_shape=outs, in_specs=specs, out_specs=[VMEM] * l...  13.8 us
    ppermute x3, starting transfers between devices, per_device(): lax.ppermute(parts[k], 'narrow', [(i, (i + k) % n_nar) for i in range(n_n...  10.5 us
  transfers between devices with their start and end apart: 6, of which 5 were waited for; matrix products, arithmetic and copies ran while one was open for 0% of the time, Pallas kernels for 4%

profile of v6, /device:TPU:2, one launch (start us, length us, event | category | flops | bytes accessed | tf_op | source)
XLA Modules:
  0.0 146.1 jit_solution(14218242635954318270)
XLA Ops:
  0.0 1.7 %shard_map.64 = bf16[8,32,512]{2,1,0:T(8,128)(2,1)} custom-call(bf16[32,3584]{1,0:T(8,128)(2,1)} %hidden_hbm.1, s32[8,32]{1,0:T(8,128)} %bitcast.2, f32[8,32]{1,0:T(8,128)} %bitcast.3), custom_call_target="tpu_custom_call" | custom-call | bytes 493568 | tf_op jit(solution)/shard_map/pallas_call | solution.py:31
  1.7 15.1 %all-to-all-start = ((bf16[8,32,512]{2,1,0:T(8,128)(2,1)}), bf16[8,32,512]{2,1,0:T(8,128)(2,1)S(1)}, u32[]{:S(2)}, u32[]{:S(2)}) async-start(bf16[8,32,512]{2,1,0:T(8,128)(2,1)} %shard_map.64), calls=%async_computation | async-start | bytes 524288 | tf_op jit(solution)/shard_map/all_to_all | solution.py:44
  16.8 4.0 %shard_map.66 = (bf16[3,448,256]{2,1,0:T(8,128)(2,1)}, bf16[3,448,256]{2,1,0:T(8,128)(2,1)}, bf16[3,448,256]{2,1,0:T(8,128)(2,1)}, bf16[3,448,256]{2,1,0:T(8,128)(2,1)}) custom-call(bf16[1,3584,128]{2,1,0:T(8,128)(2,1)} %gate_hbm.1, bf16[1,3584,128]{2,1,0:T(8,128)(2,1)} %up_hbm.1, bf16[1,128,3584]{2,1,0:T(8,128)(2,1)} %down_hbm.1), custom_call_target="tpu_custom_call" | custom-call | bytes 5505024 | tf_op jit(solution)/shard_map/pallas_call | solution.py:31
  20.8 3.4 %collective-permute-start = (bf16[3,448,256]{2,1,0:T(8,128)(2,1)}, bf16[3,448,256]{2,1,0:T(8,128)(2,1)S(1)}, u32[]{:S(2)}, u32[]{:S(2)}) collective-permute-start(bf16[3,448,256]{2,1,0:T(8,128)(2,1)} %get-tuple-element.10), channel_id=1, source_target_pairs={{0,1},{1,2},{2,3},{3,0},{4,5},{5,6},{6,7},{7,4},{8,9},{9,10},{10,1... | collective-permute-start | bytes 2064392 | tf_op jit(solution)/shard_map/ppermute | solution.py:265
  24.2 3.0 %collective-permute-start.1 = (bf16[3,448,256]{2,1,0:T(8,128)(2,1)}, bf16[3,448,256]{2,1,0:T(8,128)(2,1)S(1)}, u32[]{:S(2)}, u32[]{:S(2)}) collective-permute-start(bf16[3,448,256]{2,1,0:T(8,128)(2,1)} %get-tuple-element.11), channel_id=1, source_target_pairs={{0,2},{1,3},{2,0},{3,1},{4,6},{5,7},{6,4},{7,5},{8,10},{9,11},{10,... | collective-permute-start | bytes 2064392 | tf_op jit(solution)/shard_map/ppermute | solution.py:265
  27.3 4.1 %collective-permute-start.2 = (bf16[3,448,256]{2,1,0:T(8,128)(2,1)}, bf16[3,448,256]{2,1,0:T(8,128)(2,1)S(1)}, u32[]{:S(2)}, u32[]{:S(2)}) collective-permute-start(bf16[3,448,256]{2,1,0:T(8,128)(2,1)} %get-tuple-element.12), channel_id=1, source_target_pairs={{0,3},{1,0},{2,1},{3,2},{4,7},{5,4},{6,5},{7,6},{8,11},{9,8},{10,9... | collective-permute-start | bytes 2064392 | tf_op jit(solution)/shard_map/ppermute | solution.py:265
  31.3 6.8 %all-to-all-done.rows_ref = bf16[8,32,512]{2,1,0:T(8,128)(2,1)S(1)} async-done(((bf16[8,32,512]{2,1,0:T(8,128)(2,1)}), bf16[8,32,512]{2,1,0:T(8,128)(2,1)S(1)}, u32[]{:S(2)}, u32[]{:S(2)}) %all-to-all-start) | async-done | bytes 262176 | tf_op jit(solution)/shard_map/all_to_all | solution.py:44
  38.2 0.0 copy-start.1
  38.2 1.7 %shard_map.65 = bf16[16,32,896]{2,1,0:T(8,128)(2,1)} custom-call(bf16[8,32,512]{2,1,0:T(8,128)(2,1)S(1)} %all-to-all-done.rows_ref), custom_call_target="tpu_custom_call" | custom-call | flops 117440512 | bytes 1179648 | tf_op jit(solution)/shard_map/pallas_call | solution.py:31
  39.8 0.0 copy-done.1
  39.9 4.6 %all-to-all-start.1 = ((bf16[16,32,896]{2,1,0:T(8,128)(2,1)}), bf16[16,32,896]{2,1,0:T(8,128)(2,1)}, u32[]{:S(2)}, u32[]{:S(2)}) async-start(bf16[16,32,896]{2,1,0:T(8,128)(2,1)} %shard_map.65), calls=%async_computation.1 | async-start | bytes 1835008 | tf_op jit(solution)/shard_map/all_to_all | solution.py:44
  44.5 0.0 collective-permute-done.refs_0_.rest_1_
  44.5 1.8 %collective-permute-done.1.refs_1_.rest_2_ = bf16[3,448,256]{2,1,0:T(8,128)(2,1)S(1)} collective-permute-done((bf16[3,448,256]{2,1,0:T(8,128)(2,1)}, bf16[3,448,256]{2,1,0:T(8,128)(2,1)S(1)}, u32[]{:S(2)}, u32[]{:S(2)}) %collective-permute-start.1) | collective-permute-done | bytes 688160 | tf_op jit(solution)/shard_map/ppermute | solution.py:265
  46.3 12.9 %collective-permute-done.2.refs_2_.rest_3_ = bf16[3,448,256]{2,1,0:T(8,128)(2,1)S(1)} collective-permute-done((bf16[3,448,256]{2,1,0:T(8,128)(2,1)}, bf16[3,448,256]{2,1,0:T(8,128)(2,1)S(1)}, u32[]{:S(2)}, u32[]{:S(2)}) %collective-permute-start.2) | collective-permute-done | bytes 688160 | tf_op jit(solution)/shard_map/ppermute | solution.py:265
  59.2 0.0 copy-start
  59.2 0.5 all-to-all-done.1.rows_ref
  59.7 0.6 copy-done
  60.3 2.4 %shard_map.68 = bf16[4,512,256]{2,1,0:T(8,128)(2,1)S(1)} custom-call(bf16[16,32,896]{2,1,0:T(8,128)(2,1)} %all-to-all-done.1.rows_ref, bf16[3,448,256]{2,1,0:T(8,128)(2,1)S(1)} %copy-done, bf16[3,448,256]{2,1,0:T(8,128)(2,1)S(1)} %collective-permute-done.refs_0_.rest_1_, bf16[3,448,256]{2,1,0:T(8,128)(2,1)S(1)} %collective-permute-done.1.refs_1_.rest_2_, ...), custom_call_target="tpu_custom_call" | custom-call | flops 939524096 | bytes 4722688 | tf_op jit(solution)/shard_map/pallas_call | solution.py:31
  62.8 17.5 %all_to_all.30.acts_ref = bf16[4,512,256]{2,1,0:T(8,128)(2,1)S(1)} all-to-all(bf16[4,512,256]{2,1,0:T(8,128)(2,1)S(1)} %shard_map.68), channel_id=1, replica_groups=mesh['grp'=2,'ylo'=2,'zfar'=8,'znear'=2,'core'=2,'narrow'=4] {'narrow'}, dimensions={0} | all-to-all | bytes 2097152 | tf_op jit(solution)/shard_map/all_to_all | solution.py:44
  80.2 0.2 shard_map.69
  80.4 10.8 %all_to_all.31.inner_ref = bf16[4,512,128]{2,1,0:T(8,128)(2,1)S(1)} all-to-all(bf16[4,512,128]{2,1,0:T(8,128)(2,1)S(1)} %shard_map.69), channel_id=1, replica_groups=mesh['grp'=2,'ylo'=2,'zfar'=8,'znear'=2,'core'=2,'narrow'=4] {'narrow'}, dimensions={0} | all-to-all | bytes 1048576 | tf_op jit(solution)/shard_map/all_to_all | solution.py:44
  91.2 1.7 %shard_map.70 = bf16[16,32,896]{2,1,0:T(8,128)(2,1)} custom-call(bf16[4,512,128]{2,1,0:T(8,128)(2,1)S(1)} %all_to_all.31.inner_ref, bf16[3,448,256]{2,1,0:T(8,128)(2,1)S(1)} %copy-done, bf16[3,448,256]{2,1,0:T(8,128)(2,1)S(1)} %collective-permute-done.refs_0_.rest_1_, bf16[3,448,256]{2,1,0:T(8,128)(2,1)S(1)} %collective-permute-done.1.refs_1_.rest_2_, ...), custom_call_target="tpu_custom_call" | custom-call | flops 469762048 | bytes 4194304 | tf_op jit(solution)/shard_map/pallas_call | solution.py:31
  92.9 0.0 copy-start.2
  92.9 4.9 %all-to-all-start.4 = ((bf16[16,32,896]{2,1,0:T(8,128)(2,1)}), bf16[16,32,896]{2,1,0:T(8,128)(2,1)S(1)}, u32[]{:S(2)}, u32[]{:S(2)}) async-start(bf16[16,32,896]{2,1,0:T(8,128)(2,1)} %shard_map.70), calls=%async_computation.4 | async-start | bytes 1835008 | tf_op jit(solution)/shard_map/all_to_all | solution.py:44
  97.8 0.0 copy-done.2
  97.8 0.5 shard_map.71.weight_ref
  98.3 14.6 %all-to-all-done.4.rows_ref = bf16[16,32,896]{2,1,0:T(8,128)(2,1)S(1)} async-done(((bf16[16,32,896]{2,1,0:T(8,128)(2,1)}), bf16[16,32,896]{2,1,0:T(8,128)(2,1)S(1)}, u32[]{:S(2)}, u32[]{:S(2)}) %all-to-all-start.4) | async-done | bytes 917536 | tf_op jit(solution)/shard_map/all_to_all | solution.py:44
  113.0 0.9 shard_map.72
  113.9 31.5 %all_to_all.32.sums_ref = bf16[8,16,896]{2,1,0:T(8,128)(2,1)S(1)} all-to-all(bf16[8,16,896]{2,1,0:T(8,128)(2,1)S(1)} %shard_map.72), channel_id=1, replica_groups=mesh['grp'=2,'ylo'=2,'zfar'=8,'znear'=2,'core'=2,'narrow'=4] {'zfar'}, dimensions={0} | all-to-all | bytes 458752 | tf_op jit(solution)/shard_map/all_to_all | solution.py:44
  145.4 0.7 shard_map.73
  (1 shorter events, 0.0 us)
Async XLA Ops:
  1.7 36.5 %all-to-all-start = ((bf16[8,32,512]{2,1,0:T(8,128)(2,1)}), bf16[8,32,512]{2,1,0:T(8,128)(2,1)S(1)}, u32[]{:S(2)}, u32[]{:S(2)}) async-start(bf16[8,32,512]{2,1,0:T(8,128)(2,1)} %shard_map.64), calls=%async_computation | async-start | bytes 524288 | tf_op jit(solution)/shard_map/all_to_all | solution.py:44
  20.8 23.6 %collective-permute-start = (bf16[3,448,256]{2,1,0:T(8,128)(2,1)}, bf16[3,448,256]{2,1,0:T(8,128)(2,1)S(1)}, u32[]{:S(2)}, u32[]{:S(2)}) collective-permute-start(bf16[3,448,256]{2,1,0:T(8,128)(2,1)} %get-tuple-element.10), channel_id=1, source_target_pairs={{0,1},{1,2},{2,3},{3,0},{4,5},{5,6},{6,7},{7,4},{8,9},{9,10},{10,1... | collective-permute-start | bytes 2064392 | tf_op jit(solution)/shard_map/ppermute | solution.py:265
  24.2 22.0 %collective-permute-start.1 = (bf16[3,448,256]{2,1,0:T(8,128)(2,1)}, bf16[3,448,256]{2,1,0:T(8,128)(2,1)S(1)}, u32[]{:S(2)}, u32[]{:S(2)}) collective-permute-start(bf16[3,448,256]{2,1,0:T(8,128)(2,1)} %get-tuple-element.11), channel_id=1, source_target_pairs={{0,2},{1,3},{2,0},{3,1},{4,6},{5,7},{6,4},{7,5},{8,10},{9,11},{10,... | collective-permute-start | bytes 2064392 | tf_op jit(solution)/shard_map/ppermute | solution.py:265
  27.3 31.9 %collective-permute-start.2 = (bf16[3,448,256]{2,1,0:T(8,128)(2,1)}, bf16[3,448,256]{2,1,0:T(8,128)(2,1)S(1)}, u32[]{:S(2)}, u32[]{:S(2)}) collective-permute-start(bf16[3,448,256]{2,1,0:T(8,128)(2,1)} %get-tuple-element.12), channel_id=1, source_target_pairs={{0,3},{1,0},{2,1},{3,2},{4,7},{5,4},{6,5},{7,6},{8,11},{9,8},{10,9... | collective-permute-start | bytes 2064392 | tf_op jit(solution)/shard_map/ppermute | solution.py:265
  38.2 1.7 %copy-start.1 = (bf16[8,32,512]{2,1,0:T(8,128)(2,1)}, bf16[8,32,512]{2,1,0:T(8,128)(2,1)S(1)}, u32[]{:S(2)}) copy-start(bf16[8,32,512]{2,1,0:T(8,128)(2,1)S(1)} %all-to-all-done.rows_ref) | copy-start | bytes 786436
  39.9 19.8 %all-to-all-start.1 = ((bf16[16,32,896]{2,1,0:T(8,128)(2,1)}), bf16[16,32,896]{2,1,0:T(8,128)(2,1)}, u32[]{:S(2)}, u32[]{:S(2)}) async-start(bf16[16,32,896]{2,1,0:T(8,128)(2,1)} %shard_map.65), calls=%async_computation.1 | async-start | bytes 1835008 | tf_op jit(solution)/shard_map/all_to_all | solution.py:44
  59.2 1.1 copy-start
  92.9 4.9 %copy-start.2 = (bf16[8,32,512]{2,1,0:T(8,128)(2,1)S(1)}, bf16[8,32,512]{2,1,0:T(8,128)(2,1)}, u32[]{:S(2)}) copy-start(bf16[8,32,512]{2,1,0:T(8,128)(2,1)} %copy-done.1) | copy-start | bytes 786436
  92.9 20.1 %all-to-all-start.4 = ((bf16[16,32,896]{2,1,0:T(8,128)(2,1)}), bf16[16,32,896]{2,1,0:T(8,128)(2,1)S(1)}, u32[]{:S(2)}, u32[]{:S(2)}) async-start(bf16[16,32,896]{2,1,0:T(8,128)(2,1)} %shard_map.70), calls=%async_computation.4 | async-start | bytes 1835008 | tf_op jit(solution)/shard_map/all_to_all | solution.py:44

commit v7 on v6

--- a/solution.py
+++ b/solution.py
@@ -12,7 +12,7 @@
 BF16 = jnp.bfloat16
 I32 = jnp.int32
 FAR = "zfar"
-NEAR = ("grp", "ylo", "znear", "core")
+NEAR = ("grp", "core", "znear", "ylo")
 AXES = ("grp", "ylo", "zfar", "znear", "core", "narrow")
 WIDE = ("ylo", "zfar", "znear", "core")
 LANES = 512
@@ -41,7 +41,11 @@
 
 
 def exchange(x, axis):
-    return lax.all_to_all(x, axis, split_axis=0, concat_axis=0, tiled=True)
+    groups = None
+    if isinstance(axis, str):
+        count = lax.axis_size(axis)
+        groups = [[-i % count for i in range(count)]]
+    return lax.all_to_all(x, axis, split_axis=0, concat_axis=0, tiled=True, axis_index_groups=groups)
 
 
 def rows_body(part, top, hidden_hbm, routes_hbm, gates_hbm, out_ref, wide_ref, routes_ref, gates_ref, sems):
@@ -111,7 +115,7 @@
     extra = lax.dot_general(eye, extra, (((1,), (1,)), ((), ())), preferred_element_type=F32)
     j = lax.broadcasted_iota(I32, (8, count), 0)
     z_count = 2 * lax.axis_size(FAR)
-    expert = (((j // 4) * z_count + lax.axis_index(FAR) * 2 + (j // 2) % 2) * 2 + j % 2).astype(F32)
+    expert = (((j % 2) * z_count + lax.axis_index(FAR) * 2 + (j // 2) % 2) * 2 + j // 4).astype(F32)
     chosen = jnp.zeros((8, count), F32)
     gate = jnp.zeros((8, count), F32)
     for k in range(top):
@@ -172,7 +176,7 @@
     for k in range(n_nar):
         act = jnp.dot(left, parts[k][0], preferred_element_type=F32)
         act = act + jnp.dot(right, parts[k][1], preferred_element_type=F32)
-        out_ref[lax.rem(me - k + n_nar, n_nar)] = act.astype(BF16)
+        out_ref[lax.rem(k - me + n_nar, n_nar)] = act.astype(BF16)
 
 
 def inner_body(acts_ref, out_ref):
@@ -189,7 +193,7 @@
     me = lax.axis_index("narrow")
     near = out_ref.shape[0] // 2
     units = inner_ref.shape[2]
-    left = jnp.concatenate([inner_ref[lax.rem(me - k + n_nar, n_nar)] for k in range(n_nar)], axis=1)
+    left = jnp.concatenate([inner_ref[lax.rem(k - me + n_nar, n_nar)] for k in range(n_nar)], axis=1)
     count = left.shape[0] // 2
     for i in range(2):
         right = jnp.concatenate([parts[k][2, :, i * units : (i + 1) * units] for k in range(n_nar)], axis=1)

time: 147 us -> 145 us (0.986)
  the two profiles are of different devices: /device:TPU:2 before, /device:TPU:8 now
where the time goes in v7:
time: 145 us; the launch traced here: 144 us
  blocking collectives  59.9 us (41%)
  starting transfers between devices  37 us (26%)
  waiting for transfers between devices  32.5 us (22%)
  Pallas kernels  13.8 us (10%)
    all_to_all x3, blocking collectives, exchange(): lax.all_to_all(x, axis, split_axis=0, concat_axis=0, tiled=True, axis_ind...  59.9 us
    all_to_all x3, starting transfers between devices, exchange(): lax.all_to_all(x, axis, split_axis=0, concat_axis=0, tiled=True, axis_ind...  25.6 us
    all_to_all x3, waiting for transfers between devices, exchange(): lax.all_to_all(x, axis, split_axis=0, concat_axis=0, tiled=True, axis_ind...  16.4 us
    ppermute x3, waiting for transfers between devices, per_device(): lax.ppermute(parts[k], 'narrow', [(i, (i + k) % n_nar) for i in range(n_n...  16.1 us
    pallas_call x10, Pallas kernels, call(): pl.pallas_call(body, out_shape=outs, in_specs=specs, out_specs=[VMEM] * l...  13.8 us
    ppermute x3, starting transfers between devices, per_device(): lax.ppermute(parts[k], 'narrow', [(i, (i + k) % n_nar) for i in range(n_n...  11.4 us
  transfers between devices with their start and end apart: 6, of which 4 were waited for; matrix products, arithmetic and copies ran while one was open for 0% of the time, Pallas kernels for 4%

profile of v7, /device:TPU:8, one launch (start us, length us, event | category | flops | bytes accessed | tf_op | source)
XLA Modules:
  0.0 144.4 jit_solution(3041308387084856489)
XLA Ops:
  0.0 1.7 %shard_map.64 = bf16[8,32,512]{2,1,0:T(8,128)(2,1)} custom-call(bf16[32,3584]{1,0:T(8,128)(2,1)} %hidden_hbm.1, s32[8,32]{1,0:T(8,128)} %bitcast.2, f32[8,32]{1,0:T(8,128)} %bitcast.3), custom_call_target="tpu_custom_call" | custom-call | bytes 493568 | tf_op jit(solution)/shard_map/pallas_call | solution.py:31
  1.7 15.1 %all-to-all-start = ((bf16[8,32,512]{2,1,0:T(8,128)(2,1)}), bf16[8,32,512]{2,1,0:T(8,128)(2,1)S(1)}, u32[]{:S(2)}, u32[]{:S(2)}) async-start(bf16[8,32,512]{2,1,0:T(8,128)(2,1)} %shard_map.64), calls=%async_computation | async-start | bytes 524288 | tf_op jit(solution)/shard_map/all_to_all | solution.py:48
  16.8 4.0 %shard_map.66 = (bf16[3,448,256]{2,1,0:T(8,128)(2,1)}, bf16[3,448,256]{2,1,0:T(8,128)(2,1)}, bf16[3,448,256]{2,1,0:T(8,128)(2,1)}, bf16[3,448,256]{2,1,0:T(8,128)(2,1)}) custom-call(bf16[1,3584,128]{2,1,0:T(8,128)(2,1)} %gate_hbm.1, bf16[1,3584,128]{2,1,0:T(8,128)(2,1)} %up_hbm.1, bf16[1,128,3584]{2,1,0:T(8,128)(2,1)} %down_hbm.1), custom_call_target="tpu_custom_call" | custom-call | bytes 5505024 | tf_op jit(solution)/shard_map/pallas_call | solution.py:31
  20.8 3.4 %collective-permute-start = (bf16[3,448,256]{2,1,0:T(8,128)(2,1)}, bf16[3,448,256]{2,1,0:T(8,128)(2,1)S(1)}, u32[]{:S(2)}, u32[]{:S(2)}) collective-permute-start(bf16[3,448,256]{2,1,0:T(8,128)(2,1)} %get-tuple-element.10), channel_id=1, source_target_pairs={{0,1},{1,2},{2,3},{3,0},{4,5},{5,6},{6,7},{7,4},{8,9},{9,10},{10,1... | collective-permute-start | bytes 2064392 | tf_op jit(solution)/shard_map/ppermute | solution.py:269
  24.2 4.6 %collective-permute-start.1 = (bf16[3,448,256]{2,1,0:T(8,128)(2,1)}, bf16[3,448,256]{2,1,0:T(8,128)(2,1)S(1)}, u32[]{:S(2)}, u32[]{:S(2)}) collective-permute-start(bf16[3,448,256]{2,1,0:T(8,128)(2,1)} %get-tuple-element.11), channel_id=1, source_target_pairs={{0,2},{1,3},{2,0},{3,1},{4,6},{5,7},{6,4},{7,5},{8,10},{9,11},{10,... | collective-permute-start | bytes 2064392 | tf_op jit(solution)/shard_map/ppermute | solution.py:269
  28.9 3.3 %collective-permute-start.2 = (bf16[3,448,256]{2,1,0:T(8,128)(2,1)}, bf16[3,448,256]{2,1,0:T(8,128)(2,1)S(1)}, u32[]{:S(2)}, u32[]{:S(2)}) collective-permute-start(bf16[3,448,256]{2,1,0:T(8,128)(2,1)} %get-tuple-element.12), channel_id=1, source_target_pairs={{0,3},{1,0},{2,1},{3,2},{4,7},{5,4},{6,5},{7,6},{8,11},{9,8},{10,9... | collective-permute-start | bytes 2064392 | tf_op jit(solution)/shard_map/ppermute | solution.py:269
  32.2 3.4 %all-to-all-done.rows_ref = bf16[8,32,512]{2,1,0:T(8,128)(2,1)S(1)} async-done(((bf16[8,32,512]{2,1,0:T(8,128)(2,1)}), bf16[8,32,512]{2,1,0:T(8,128)(2,1)S(1)}, u32[]{:S(2)}, u32[]{:S(2)}) %all-to-all-start) | async-done | bytes 262176 | tf_op jit(solution)/shard_map/all_to_all | solution.py:48
  35.7 0.0 copy-start.1
  35.7 1.7 %shard_map.65 = bf16[16,32,896]{2,1,0:T(8,128)(2,1)} custom-call(bf16[8,32,512]{2,1,0:T(8,128)(2,1)S(1)} %all-to-all-done.rows_ref), custom_call_target="tpu_custom_call" | custom-call | flops 117440512 | bytes 1179648 | tf_op jit(solution)/shard_map/pallas_call | solution.py:31
  37.3 0.0 copy-done.1
  37.3 5.0 %all-to-all-start.1 = ((bf16[16,32,896]{2,1,0:T(8,128)(2,1)}), bf16[16,32,896]{2,1,0:T(8,128)(2,1)}, u32[]{:S(2)}, u32[]{:S(2)}) async-start(bf16[16,32,896]{2,1,0:T(8,128)(2,1)} %shard_map.65), calls=%async_computation.1 | async-start | bytes 1835008 | tf_op jit(solution)/shard_map/all_to_all | solution.py:48
  42.3 0.0 collective-permute-done.refs_0_.rest_1_
  42.3 14.5 %collective-permute-done.1.refs_1_.rest_2_ = bf16[3,448,256]{2,1,0:T(8,128)(2,1)S(1)} collective-permute-done((bf16[3,448,256]{2,1,0:T(8,128)(2,1)}, bf16[3,448,256]{2,1,0:T(8,128)(2,1)S(1)}, u32[]{:S(2)}, u32[]{:S(2)}) %collective-permute-start.1) | collective-permute-done | bytes 688160 | tf_op jit(solution)/shard_map/ppermute | solution.py:269
  56.8 1.6 %collective-permute-done.2.refs_2_.rest_3_ = bf16[3,448,256]{2,1,0:T(8,128)(2,1)S(1)} collective-permute-done((bf16[3,448,256]{2,1,0:T(8,128)(2,1)}, bf16[3,448,256]{2,1,0:T(8,128)(2,1)S(1)}, u32[]{:S(2)}, u32[]{:S(2)}) %collective-permute-start.2) | collective-permute-done | bytes 688160 | tf_op jit(solution)/shard_map/ppermute | solution.py:269
  58.3 0.0 copy-start
  58.3 0.0 all-to-all-done.1.rows_ref
  58.3 1.1 copy-done
  59.4 2.4 %shard_map.68 = bf16[4,512,256]{2,1,0:T(8,128)(2,1)S(1)} custom-call(bf16[16,32,896]{2,1,0:T(8,128)(2,1)} %all-to-all-done.1.rows_ref, bf16[3,448,256]{2,1,0:T(8,128)(2,1)S(1)} %copy-done, bf16[3,448,256]{2,1,0:T(8,128)(2,1)S(1)} %collective-permute-done.refs_0_.rest_1_, bf16[3,448,256]{2,1,0:T(8,128)(2,1)S(1)} %collective-permute-done.1.refs_1_.rest_2_, ...), custom_call_target="tpu_custom_call" | custom-call | flops 939524096 | bytes 4722688 | tf_op jit(solution)/shard_map/pallas_call | solution.py:31
  61.9 19.0 %all_to_all.30.acts_ref = bf16[4,512,256]{2,1,0:T(8,128)(2,1)S(1)} all-to-all(bf16[4,512,256]{2,1,0:T(8,128)(2,1)S(1)} %shard_map.68), channel_id=1, replica_groups={{0,3,2,1},{4,7,6,5},{8,11,10,9},{12,15,14,13},{16,19,18,17},{20,23,22,2..., dimensions={0} | all-to-all | bytes 2097152 | tf_op jit(solution)/shard_map/all_to_all | solution.py:48
  80.9 0.2 shard_map.69
  81.0 10.7 %all_to_all.31.inner_ref = bf16[4,512,128]{2,1,0:T(8,128)(2,1)S(1)} all-to-all(bf16[4,512,128]{2,1,0:T(8,128)(2,1)S(1)} %shard_map.69), channel_id=1, replica_groups={{0,3,2,1},{4,7,6,5},{8,11,10,9},{12,15,14,13},{16,19,18,17},{20,23,22,2..., dimensions={0} | all-to-all | bytes 1048576 | tf_op jit(solution)/shard_map/all_to_all | solution.py:48
  91.8 1.7 %shard_map.70 = bf16[16,32,896]{2,1,0:T(8,128)(2,1)} custom-call(bf16[4,512,128]{2,1,0:T(8,128)(2,1)S(1)} %all_to_all.31.inner_ref, bf16[3,448,256]{2,1,0:T(8,128)(2,1)S(1)} %copy-done, bf16[3,448,256]{2,1,0:T(8,128)(2,1)S(1)} %collective-permute-done.refs_0_.rest_1_, bf16[3,448,256]{2,1,0:T(8,128)(2,1)S(1)} %collective-permute-done.1.refs_1_.rest_2_, ...), custom_call_target="tpu_custom_call" | custom-call | flops 469762048 | bytes 4194304 | tf_op jit(solution)/shard_map/pallas_call | solution.py:31
  93.5 0.0 copy-start.2
  93.5 5.6 %all-to-all-start.4 = ((bf16[16,32,896]{2,1,0:T(8,128)(2,1)}), bf16[16,32,896]{2,1,0:T(8,128)(2,1)S(1)}, u32[]{:S(2)}, u32[]{:S(2)}) async-start(bf16[16,32,896]{2,1,0:T(8,128)(2,1)} %shard_map.70), calls=%async_computation.4 | async-start | bytes 1835008 | tf_op jit(solution)/shard_map/all_to_all | solution.py:48
  99.1 0.0 copy-done.2
  99.1 0.5 shard_map.71.weight_ref
  99.6 13.0 %all-to-all-done.4.rows_ref = bf16[16,32,896]{2,1,0:T(8,128)(2,1)S(1)} async-done(((bf16[16,32,896]{2,1,0:T(8,128)(2,1)}), bf16[16,32,896]{2,1,0:T(8,128)(2,1)S(1)}, u32[]{:S(2)}, u32[]{:S(2)}) %all-to-all-start.4) | async-done | bytes 917536 | tf_op jit(solution)/shard_map/all_to_all | solution.py:48
  112.6 0.9 shard_map.72
  113.5 30.2 %all_to_all.32.sums_ref = bf16[8,16,896]{2,1,0:T(8,128)(2,1)S(1)} all-to-all(bf16[8,16,896]{2,1,0:T(8,128)(2,1)S(1)} %shard_map.72), channel_id=1, replica_groups={{0,112,96,80,64,48,32,16},{1,113,97,81,65,49,33,17},{2,114,98,82,66,50,..., dimensions={0} | all-to-all | bytes 458752 | tf_op jit(solution)/shard_map/all_to_all | solution.py:48
  143.7 0.7 shard_map.73
  (1 shorter events, 0.0 us)
Async XLA Ops:
  1.7 33.9 %all-to-all-start = ((bf16[8,32,512]{2,1,0:T(8,128)(2,1)}), bf16[8,32,512]{2,1,0:T(8,128)(2,1)S(1)}, u32[]{:S(2)}, u32[]{:S(2)}) async-start(bf16[8,32,512]{2,1,0:T(8,128)(2,1)} %shard_map.64), calls=%async_computation | async-start | bytes 524288 | tf_op jit(solution)/shard_map/all_to_all | solution.py:48
  20.8 21.4 %collective-permute-start = (bf16[3,448,256]{2,1,0:T(8,128)(2,1)}, bf16[3,448,256]{2,1,0:T(8,128)(2,1)S(1)}, u32[]{:S(2)}, u32[]{:S(2)}) collective-permute-start(bf16[3,448,256]{2,1,0:T(8,128)(2,1)} %get-tuple-element.10), channel_id=1, source_target_pairs={{0,1},{1,2},{2,3},{3,0},{4,5},{5,6},{6,7},{7,4},{8,9},{9,10},{10,1... | collective-permute-start | bytes 2064392 | tf_op jit(solution)/shard_map/ppermute | solution.py:269
  24.2 32.5 %collective-permute-start.1 = (bf16[3,448,256]{2,1,0:T(8,128)(2,1)}, bf16[3,448,256]{2,1,0:T(8,128)(2,1)S(1)}, u32[]{:S(2)}, u32[]{:S(2)}) collective-permute-start(bf16[3,448,256]{2,1,0:T(8,128)(2,1)} %get-tuple-element.11), channel_id=1, source_target_pairs={{0,2},{1,3},{2,0},{3,1},{4,6},{5,7},{6,4},{7,5},{8,10},{9,11},{10,... | collective-permute-start | bytes 2064392 | tf_op jit(solution)/shard_map/ppermute | solution.py:269
  28.9 29.4 %collective-permute-start.2 = (bf16[3,448,256]{2,1,0:T(8,128)(2,1)}, bf16[3,448,256]{2,1,0:T(8,128)(2,1)S(1)}, u32[]{:S(2)}, u32[]{:S(2)}) collective-permute-start(bf16[3,448,256]{2,1,0:T(8,128)(2,1)} %get-tuple-element.12), channel_id=1, source_target_pairs={{0,3},{1,0},{2,1},{3,2},{4,7},{5,4},{6,5},{7,6},{8,11},{9,8},{10,9... | collective-permute-start | bytes 2064392 | tf_op jit(solution)/shard_map/ppermute | solution.py:269
  35.7 1.7 %copy-start.1 = (bf16[8,32,512]{2,1,0:T(8,128)(2,1)}, bf16[8,32,512]{2,1,0:T(8,128)(2,1)S(1)}, u32[]{:S(2)}) copy-start(bf16[8,32,512]{2,1,0:T(8,128)(2,1)S(1)} %all-to-all-done.rows_ref) | copy-start | bytes 786436
  37.3 21.0 %all-to-all-start.1 = ((bf16[16,32,896]{2,1,0:T(8,128)(2,1)}), bf16[16,32,896]{2,1,0:T(8,128)(2,1)}, u32[]{:S(2)}, u32[]{:S(2)}) async-start(bf16[16,32,896]{2,1,0:T(8,128)(2,1)} %shard_map.65), calls=%async_computation.1 | async-start | bytes 1835008 | tf_op jit(solution)/shard_map/all_to_all | solution.py:48
  58.3 1.1 copy-start
  93.5 5.6 %copy-start.2 = (bf16[8,32,512]{2,1,0:T(8,128)(2,1)S(1)}, bf16[8,32,512]{2,1,0:T(8,128)(2,1)}, u32[]{:S(2)}) copy-start(bf16[8,32,512]{2,1,0:T(8,128)(2,1)} %copy-done.1) | copy-start | bytes 786436
  93.5 19.1 %all-to-all-start.4 = ((bf16[16,32,896]{2,1,0:T(8,128)(2,1)}), bf16[16,32,896]{2,1,0:T(8,128)(2,1)S(1)}, u32[]{:S(2)}, u32[]{:S(2)}) async-start(bf16[16,32,896]{2,1,0:T(8,128)(2,1)} %shard_map.70), calls=%async_computation.4 | async-start | bytes 1835008 | tf_op jit(solution)/shard_map/all_to_all | solution.py:48

commit v8 on v6

--- a/solution.py
+++ b/solution.py
@@ -12,11 +12,12 @@
 BF16 = jnp.bfloat16
 I32 = jnp.int32
 FAR = "zfar"
-NEAR = ("grp", "ylo", "znear", "core")
+NEAR = ("grp", "core", "ylo", "znear")
 AXES = ("grp", "ylo", "zfar", "znear", "core", "narrow")
 WIDE = ("ylo", "zfar", "znear", "core")
 LANES = 512
 HOLD = 200 * 10**9
+ORDER = (2, 1, 3, 0)
 
 VMEM = pl.BlockSpec(memory_space=pltpu.VMEM)
 SMEM = pl.BlockSpec(memory_space=pltpu.SMEM)
@@ -41,7 +42,12 @@
 
 
 def exchange(x, axis):
-    return lax.all_to_all(x, axis, split_axis=0, concat_axis=0, tiled=True)
+    groups = {FAR: [[0, 2, 4, 6, 1, 3, 5, 7]], "narrow": [[0, 3, 1, 2]]}.get(axis)
+    return lax.all_to_all(x, axis, split_axis=0, concat_axis=0, tiled=True, axis_index_groups=groups)
+
+
+def place_of(index):
+    return jnp.where(index == 0, 0, jnp.where(index == 3, 1, index + 1))
 
 
 def rows_body(part, top, hidden_hbm, routes_hbm, gates_hbm, out_ref, wide_ref, routes_ref, gates_ref, sems):
@@ -71,7 +77,8 @@
 
 
 def pack_body(n_nar, part, gate_hbm, up_hbm, down_hbm, *rest):
-    outs, (down_ref, turned_ref, sems, down_sem) = rest[:n_nar], rest[n_nar:]
+    outs = [rest[ORDER.index(k)] for k in range(n_nar)]
+    down_ref, turned_ref, sems, down_sem = rest[n_nar:]
     units = gate_hbm.shape[2]
     me = lax.axis_index("narrow")
     fetch = pltpu.make_async_copy(down_hbm.at[0], down_ref, down_sem)
@@ -97,6 +104,12 @@
         copy.wait()
 
 
+def own_body(part_hbm, _, out_ref, sem):
+    copy = pltpu.make_async_copy(part_hbm, out_ref, sem)
+    copy.start()
+    copy.wait()
+
+
 def arrived_body(*refs):
     refs[-1][...] = jnp.zeros(refs[-1].shape, F32)
 
@@ -111,7 +124,7 @@
     extra = lax.dot_general(eye, extra, (((1,), (1,)), ((), ())), preferred_element_type=F32)
     j = lax.broadcasted_iota(I32, (8, count), 0)
     z_count = 2 * lax.axis_size(FAR)
-    expert = (((j // 4) * z_count + lax.axis_index(FAR) * 2 + (j // 2) % 2) * 2 + j % 2).astype(F32)
+    expert = (((j // 2 % 2) * z_count + lax.axis_index(FAR) * 2 + j % 2) * 2 + j // 4).astype(F32)
     chosen = jnp.zeros((8, count), F32)
     gate = jnp.zeros((8, count), F32)
     for k in range(top):
@@ -163,7 +176,7 @@
 
 
 def gate_up_body(n_nar, rows_ref, *rest):
-    parts, out_ref = rest[:n_nar], rest[-1]
+    parts, out_ref = [rest[ORDER.index(k)] for k in range(n_nar)], rest[-1]
     me = lax.axis_index("narrow")
     part = rows_ref.shape[2] // 2
     half = rows_ref.shape[0] // 2
@@ -172,7 +185,7 @@
     for k in range(n_nar):
         act = jnp.dot(left, parts[k][0], preferred_element_type=F32)
         act = act + jnp.dot(right, parts[k][1], preferred_element_type=F32)
-        out_ref[lax.rem(me - k + n_nar, n_nar)] = act.astype(BF16)
+        out_ref[place_of(lax.rem(me - k + n_nar, n_nar))] = act.astype(BF16)
 
 
 def inner_body(acts_ref, out_ref):
@@ -185,11 +198,11 @@
 
 
 def down_body(n_nar, inner_ref, *rest):
-    parts, out_ref = rest[:n_nar], rest[-1]
+    parts, out_ref = [rest[ORDER.index(k)] for k in range(n_nar)], rest[-1]
     me = lax.axis_index("narrow")
     near = out_ref.shape[0] // 2
     units = inner_ref.shape[2]
-    left = jnp.concatenate([inner_ref[lax.rem(me - k + n_nar, n_nar)] for k in range(n_nar)], axis=1)
+    left = jnp.concatenate([inner_ref[place_of(lax.rem(me - k + n_nar, n_nar))] for k in range(n_nar)], axis=1)
     count = left.shape[0] // 2
     for i in range(2):
         right = jnp.concatenate([parts[k][2, :, i * units : (i + 1) * units] for k in range(n_nar)], axis=1)
@@ -260,13 +273,9 @@
         ],
         mib=60,
     )
-    parts = list(parts)
-    for k in range(1, n_nar):
+    parts = [parts[ORDER.index(k)] for k in range(n_nar)]
+    for k in ORDER[:-1]:
         parts[k] = lax.ppermute(parts[k], "narrow", [(i, (i + k) % n_nar) for i in range(n_nar)])
-    arrived = call(
-        arrived_body, jax.ShapeDtypeStruct((8, 128), F32), [ANY] * (n_nar - 1), parts[1:], flops=HOLD
-    )
-
     half = n_far * CAP // 2
     picked = call(
         functools.partial(pick_body, part, top),
@@ -281,13 +290,23 @@
         [VMEM],
         [rows],
     )
+    parts[0] = call(
+        own_body,
+        jax.ShapeDtypeStruct(parts[0].shape, BF16),
+        [HBM, ANY],
+        [parts[0], picked],
+        scratch=[pltpu.SemaphoreType.DMA],
+    )
+    arrived = call(
+        arrived_body, jax.ShapeDtypeStruct((8, 128), F32), [ANY] * n_nar, [parts[k] for k in ORDER], flops=HOLD
+    )
     rows = exchange(picked, NEAR)
 
     acts = call(
         functools.partial(gate_up_body, n_nar),
         jax.ShapeDtypeStruct((n_nar, slots, 2 * units), BF16),
         [VMEM] + [VMEM] * n_nar + [ANY],
-        [rows] + parts + [arrived],
+        [rows] + [parts[k] for k in ORDER] + [arrived],
         flops=2 * slots * part * 2 * units * 2 * n_nar,
     )
     acts = exchange(acts, "narrow")
@@ -297,7 +316,7 @@
         functools.partial(down_body, n_nar),
         jax.ShapeDtypeStruct((near, half, 2 * part), BF16),
         [VMEM] + [VMEM] * n_nar,
-        [inner] + parts,
+        [inner] + [parts[k] for k in ORDER],
         flops=2 * slots * units * n_nar * 2 * part,
     )
     outs = exchange(outs, NEAR)

time: 147 us -> 141 us (0.959)
  the two profiles are of different devices: /device:TPU:2 before, /device:TPU:32 now
where the time goes in v8:
time: 141 us
  blocking collectives  60.4 us (43%)
  starting transfers between devices  37.3 us (26%)
  waiting for transfers between devices  28.6 us (20%)
  Pallas kernels  14.1 us (10%)
    all_to_all x3, blocking collectives, exchange(): lax.all_to_all(x, axis, split_axis=0, concat_axis=0, tiled=True, axis_ind...  60.4 us
    all_to_all x3, starting transfers between devices, exchange(): lax.all_to_all(x, axis, split_axis=0, concat_axis=0, tiled=True, axis_ind...  25.3 us
    all_to_all x3, waiting for transfers between devices, exchange(): lax.all_to_all(x, axis, split_axis=0, concat_axis=0, tiled=True, axis_ind...  16 us
    pallas_call x11, Pallas kernels, call(): pl.pallas_call(body, out_shape=outs, in_specs=specs, out_specs=[VMEM] * l...  14.1 us
    ppermute x3, waiting for transfers between devices, per_device(): lax.ppermute(parts[k], 'narrow', [(i, (i + k) % n_nar) for i in range(n_n...  12.6 us
    ppermute x3, starting transfers between devices, per_device(): lax.ppermute(parts[k], 'narrow', [(i, (i + k) % n_nar) for i in range(n_n...  12 us
  transfers between devices with their start and end apart: 6, of which 5 were waited for; matrix products, arithmetic and copies ran while one was open for 0% of the time, Pallas kernels for 5%

profile of v8, /device:TPU:32, one launch (start us, length us, event | category | flops | bytes accessed | tf_op | source)
XLA Modules:
  0.0 140.5 jit_solution(1507301165867180393)
XLA Ops:
  0.0 1.7 %shard_map.64 = bf16[8,32,512]{2,1,0:T(8,128)(2,1)} custom-call(bf16[32,3584]{1,0:T(8,128)(2,1)} %hidden_hbm.1, s32[8,32]{1,0:T(8,128)} %bitcast.2, f32[8,32]{1,0:T(8,128)} %bitcast.3), custom_call_target="tpu_custom_call" | custom-call | bytes 493568 | tf_op jit(solution)/shard_map/pallas_call | solution.py:32
  1.7 14.2 %all-to-all-start = ((bf16[8,32,512]{2,1,0:T(8,128)(2,1)}), bf16[8,32,512]{2,1,0:T(8,128)(2,1)S(1)}, u32[]{:S(2)}, u32[]{:S(2)}) async-start(bf16[8,32,512]{2,1,0:T(8,128)(2,1)} %shard_map.64), calls=%async_computation | async-start | bytes 524288 | tf_op jit(solution)/shard_map/all_to_all | solution.py:46
  15.9 4.0 %shard_map.66 = (bf16[3,448,256]{2,1,0:T(8,128)(2,1)}, bf16[3,448,256]{2,1,0:T(8,128)(2,1)}, bf16[3,448,256]{2,1,0:T(8,128)(2,1)}, bf16[3,448,256]{2,1,0:T(8,128)(2,1)}) custom-call(bf16[1,3584,128]{2,1,0:T(8,128)(2,1)} %gate_hbm.1, bf16[1,3584,128]{2,1,0:T(8,128)(2,1)} %up_hbm.1, bf16[1,128,3584]{2,1,0:T(8,128)(2,1)} %down_hbm.1), custom_call_target="tpu_custom_call" | custom-call | bytes 5505024 | tf_op jit(solution)/shard_map/pallas_call | solution.py:32
  19.9 4.9 %collective-permute-start = (bf16[3,448,256]{2,1,0:T(8,128)(2,1)}, bf16[3,448,256]{2,1,0:T(8,128)(2,1)S(1)}, u32[]{:S(2)}, u32[]{:S(2)}) collective-permute-start(bf16[3,448,256]{2,1,0:T(8,128)(2,1)} %get-tuple-element.9), channel_id=1, source_target_pairs={{0,2},{1,3},{2,0},{3,1},{4,6},{5,7},{6,4},{7,5},{8,10},{9,11},{10,... | collective-permute-start | bytes 2064392 | tf_op jit(solution)/shard_map/ppermute | solution.py:278
  24.9 2.5 %collective-permute-start.1 = (bf16[3,448,256]{2,1,0:T(8,128)(2,1)}, bf16[3,448,256]{2,1,0:T(8,128)(2,1)S(1)}, u32[]{:S(2)}, u32[]{:S(2)}) collective-permute-start(bf16[3,448,256]{2,1,0:T(8,128)(2,1)} %get-tuple-element.10), channel_id=1, source_target_pairs={{0,1},{1,2},{2,3},{3,0},{4,5},{5,6},{6,7},{7,4},{8,9},{9,10},{10,1... | collective-permute-start | bytes 2064392 | tf_op jit(solution)/shard_map/ppermute | solution.py:278
  27.4 4.6 %collective-permute-start.2 = (bf16[3,448,256]{2,1,0:T(8,128)(2,1)}, bf16[3,448,256]{2,1,0:T(8,128)(2,1)S(1)}, u32[]{:S(2)}, u32[]{:S(2)}) collective-permute-start(bf16[3,448,256]{2,1,0:T(8,128)(2,1)} %get-tuple-element.11), channel_id=1, source_target_pairs={{0,3},{1,0},{2,1},{3,2},{4,7},{5,4},{6,5},{7,6},{8,11},{9,8},{10,9... | collective-permute-start | bytes 2064392 | tf_op jit(solution)/shard_map/ppermute | solution.py:278
  32.0 2.7 %all-to-all-done.rows_ref = bf16[8,32,512]{2,1,0:T(8,128)(2,1)S(1)} async-done(((bf16[8,32,512]{2,1,0:T(8,128)(2,1)}), bf16[8,32,512]{2,1,0:T(8,128)(2,1)S(1)}, u32[]{:S(2)}, u32[]{:S(2)}) %all-to-all-start) | async-done | bytes 262176 | tf_op jit(solution)/shard_map/all_to_all | solution.py:46
  34.7 0.0 copy-start
  34.7 1.7 %shard_map.65._ = bf16[16,32,896]{2,1,0:T(8,128)(2,1)} custom-call(bf16[8,32,512]{2,1,0:T(8,128)(2,1)S(1)} %all-to-all-done.rows_ref), custom_call_target="tpu_custom_call" | custom-call | flops 117440512 | bytes 1179648 | tf_op jit(solution)/shard_map/pallas_call | solution.py:32
  36.3 0.0 copy-done
  36.3 0.0 copy-start.2
  36.3 6.1 %all-to-all-start.1 = ((bf16[16,32,896]{2,1,0:T(8,128)(2,1)}), bf16[16,32,896]{2,1,0:T(8,128)(2,1)}, u32[]{:S(2)}, u32[]{:S(2)}) async-start(bf16[16,32,896]{2,1,0:T(8,128)(2,1)} %shard_map.65._), calls=%async_computation.1 | async-start | bytes 1835008 | tf_op jit(solution)/shard_map/all_to_all | solution.py:46
  42.4 0.0 copy-done.2
  42.4 0.3 shard_map.67.refs_3_.rest_3_
  42.7 0.0 collective-permute-done.refs_0_.rest_0_
  42.7 12.5 %collective-permute-done.1.refs_1_.rest_1_ = bf16[3,448,256]{2,1,0:T(8,128)(2,1)S(1)} collective-permute-done((bf16[3,448,256]{2,1,0:T(8,128)(2,1)}, bf16[3,448,256]{2,1,0:T(8,128)(2,1)S(1)}, u32[]{:S(2)}, u32[]{:S(2)}) %collective-permute-start.1) | collective-permute-done | bytes 688160 | tf_op jit(solution)/shard_map/ppermute | solution.py:278
  55.2 0.1 collective-permute-done.2.refs_2_.rest_2_
  55.3 0.5 all-to-all-done.1.rows_ref
  55.8 2.4 %shard_map.69 = bf16[4,512,256]{2,1,0:T(8,128)(2,1)S(1)} custom-call(bf16[16,32,896]{2,1,0:T(8,128)(2,1)} %all-to-all-done.1.rows_ref, bf16[3,448,256]{2,1,0:T(8,128)(2,1)S(1)} %collective-permute-done.refs_0_.rest_0_, bf16[3,448,256]{2,1,0:T(8,128)(2,1)S(1)} %collective-permute-done.1.refs_1_.rest_1_, ...), custom_call_target="tpu_custom_call" | custom-call | flops 939524096 | bytes 4722688 | tf_op jit(solution)/shard_map/pallas_call | solution.py:32
  58.3 19.3 %all_to_all.30.acts_ref = bf16[4,512,256]{2,1,0:T(8,128)(2,1)S(1)} all-to-all(bf16[4,512,256]{2,1,0:T(8,128)(2,1)S(1)} %shard_map.69), channel_id=1, replica_groups={{0,3,1,2},{4,7,5,6},{8,11,9,10},{12,15,13,14},{16,19,17,18},{20,23,21,2..., dimensions={0} | all-to-all | bytes 2097152 | tf_op jit(solution)/shard_map/all_to_all | solution.py:46
  77.5 0.2 shard_map.70
  77.7 11.0 %all_to_all.31.inner_ref = bf16[4,512,128]{2,1,0:T(8,128)(2,1)S(1)} all-to-all(bf16[4,512,128]{2,1,0:T(8,128)(2,1)S(1)} %shard_map.70), channel_id=1, replica_groups={{0,3,1,2},{4,7,5,6},{8,11,9,10},{12,15,13,14},{16,19,17,18},{20,23,21,2..., dimensions={0} | all-to-all | bytes 1048576 | tf_op jit(solution)/shard_map/all_to_all | solution.py:46
  88.7 1.7 %shard_map.71 = bf16[16,32,896]{2,1,0:T(8,128)(2,1)} custom-call(bf16[4,512,128]{2,1,0:T(8,128)(2,1)S(1)} %all_to_all.31.inner_ref, bf16[3,448,256]{2,1,0:T(8,128)(2,1)S(1)} %collective-permute-done.refs_0_.rest_0_, bf16[3,448,256]{2,1,0:T(8,128)(2,1)S(1)} %collective-permute-done.1.refs_1_.rest_1_, ...), custom_call_target="tpu_custom_call" | custom-call | flops 469762048 | bytes 4194304 | tf_op jit(solution)/shard_map/pallas_call | solution.py:32
  90.4 0.0 copy-start.1
  90.4 5.0 %all-to-all-start.4 = ((bf16[16,32,896]{2,1,0:T(8,128)(2,1)}), bf16[16,32,896]{2,1,0:T(8,128)(2,1)S(1)}, u32[]{:S(2)}, u32[]{:S(2)}) async-start(bf16[16,32,896]{2,1,0:T(8,128)(2,1)} %shard_map.71), calls=%async_computation.4 | async-start | bytes 1835008 | tf_op jit(solution)/shard_map/all_to_all | solution.py:46
  95.4 0.0 copy-done.1
  95.5 0.5 shard_map.72.weight_ref
  96.0 12.8 %all-to-all-done.4.rows_ref = bf16[16,32,896]{2,1,0:T(8,128)(2,1)S(1)} async-done(((bf16[16,32,896]{2,1,0:T(8,128)(2,1)}), bf16[16,32,896]{2,1,0:T(8,128)(2,1)S(1)}, u32[]{:S(2)}, u32[]{:S(2)}) %all-to-all-start.4) | async-done | bytes 917536 | tf_op jit(solution)/shard_map/all_to_all | solution.py:46
  108.8 0.9 shard_map.73
  109.7 30.1 %all_to_all.32.sums_ref = bf16[8,16,896]{2,1,0:T(8,128)(2,1)S(1)} all-to-all(bf16[8,16,896]{2,1,0:T(8,128)(2,1)S(1)} %shard_map.73), channel_id=1, replica_groups={{0,32,64,96,16,48,80,112},{1,33,65,97,17,49,81,113},{2,34,66,98,18,50,8..., dimensions={0} | all-to-all | bytes 458752 | tf_op jit(solution)/shard_map/all_to_all | solution.py:46
  139.8 0.7 shard_map.74
  (1 shorter events, 0.0 us)
Async XLA Ops:
  1.7 32.9 %all-to-all-start = ((bf16[8,32,512]{2,1,0:T(8,128)(2,1)}), bf16[8,32,512]{2,1,0:T(8,128)(2,1)S(1)}, u32[]{:S(2)}, u32[]{:S(2)}) async-start(bf16[8,32,512]{2,1,0:T(8,128)(2,1)} %shard_map.64), calls=%async_computation | async-start | bytes 524288 | tf_op jit(solution)/shard_map/all_to_all | solution.py:46
  19.9 22.7 %collective-permute-start = (bf16[3,448,256]{2,1,0:T(8,128)(2,1)}, bf16[3,448,256]{2,1,0:T(8,128)(2,1)S(1)}, u32[]{:S(2)}, u32[]{:S(2)}) collective-permute-start(bf16[3,448,256]{2,1,0:T(8,128)(2,1)} %get-tuple-element.9), channel_id=1, source_target_pairs={{0,2},{1,3},{2,0},{3,1},{4,6},{5,7},{6,4},{7,5},{8,10},{9,11},{10,... | collective-permute-start | bytes 2064392 | tf_op jit(solution)/shard_map/ppermute | solution.py:278
  24.9 30.3 %collective-permute-start.1 = (bf16[3,448,256]{2,1,0:T(8,128)(2,1)}, bf16[3,448,256]{2,1,0:T(8,128)(2,1)S(1)}, u32[]{:S(2)}, u32[]{:S(2)}) collective-permute-start(bf16[3,448,256]{2,1,0:T(8,128)(2,1)} %get-tuple-element.10), channel_id=1, source_target_pairs={{0,1},{1,2},{2,3},{3,0},{4,5},{5,6},{6,7},{7,4},{8,9},{9,10},{10,1... | collective-permute-start | bytes 2064392 | tf_op jit(solution)/shard_map/ppermute | solution.py:278
  27.4 27.9 %collective-permute-start.2 = (bf16[3,448,256]{2,1,0:T(8,128)(2,1)}, bf16[3,448,256]{2,1,0:T(8,128)(2,1)S(1)}, u32[]{:S(2)}, u32[]{:S(2)}) collective-permute-start(bf16[3,448,256]{2,1,0:T(8,128)(2,1)} %get-tuple-element.11), channel_id=1, source_target_pairs={{0,3},{1,0},{2,1},{3,2},{4,7},{5,4},{6,5},{7,6},{8,11},{9,8},{10,9... | collective-permute-start | bytes 2064392 | tf_op jit(solution)/shard_map/ppermute | solution.py:278
  34.7 1.7 %copy-start = (bf16[8,32,512]{2,1,0:T(8,128)(2,1)}, bf16[8,32,512]{2,1,0:T(8,128)(2,1)S(1)}, u32[]{:S(2)}) copy-start(bf16[8,32,512]{2,1,0:T(8,128)(2,1)S(1)} %all-to-all-done.rows_ref) | copy-start | bytes 786436
  36.3 6.1 %copy-start.2 = (bf16[3,448,256]{2,1,0:T(8,128)(2,1)S(1)}, bf16[3,448,256]{2,1,0:T(8,128)(2,1)}, u32[]{:S(2)}) copy-start(bf16[3,448,256]{2,1,0:T(8,128)(2,1)} %get-tuple-element.12.part_hbm) | copy-start | bytes 2064388
  36.3 19.5 %all-to-all-start.1 = ((bf16[16,32,896]{2,1,0:T(8,128)(2,1)}), bf16[16,32,896]{2,1,0:T(8,128)(2,1)}, u32[]{:S(2)}, u32[]{:S(2)}) async-start(bf16[16,32,896]{2,1,0:T(8,128)(2,1)} %shard_map.65._), calls=%async_computation.1 | async-start | bytes 1835008 | tf_op jit(solution)/shard_map/all_to_all | solution.py:46
  90.4 5.0 %copy-start.1 = (bf16[8,32,512]{2,1,0:T(8,128)(2,1)S(1)}, bf16[8,32,512]{2,1,0:T(8,128)(2,1)}, u32[]{:S(2)}) copy-start(bf16[8,32,512]{2,1,0:T(8,128)(2,1)} %copy-done) | copy-start | bytes 786436
  90.4 18.4 %all-to-all-start.4 = ((bf16[16,32,896]{2,1,0:T(8,128)(2,1)}), bf16[16,32,896]{2,1,0:T(8,128)(2,1)S(1)}, u32[]{:S(2)}, u32[]{:S(2)}) async-start(bf16[16,32,896]{2,1,0:T(8,128)(2,1)} %shard_map.71), calls=%async_computation.4 | async-start | bytes 1835008 | tf_op jit(solution)/shard_map/all_to_all | solution.py:46

commit v9 on v8

--- a/solution.py
+++ b/solution.py
@@ -18,6 +18,8 @@
 LANES = 512
 HOLD = 200 * 10**9
 ORDER = (2, 1, 3, 0)
+FAR_ORDER = (0, 4, 1, 5, 2, 6, 3, 7)
+NARROW_ORDER = (0, 1, 3, 2)
 
 VMEM = pl.BlockSpec(memory_space=pltpu.VMEM)
 SMEM = pl.BlockSpec(memory_space=pltpu.SMEM)
@@ -25,7 +27,7 @@
 HBM = pl.BlockSpec(memory_space=pltpu.HBM)
 
 
-def call(body, outs, specs, args, flops=0, scratch=(), mib=16):
+def call(body, outs, specs, args, flops=0, scratch=(), mib=16, place=None):
     single = not isinstance(outs, list)
     outs = [outs] if single else outs
     nbytes = sum(a.size * a.dtype.itemsize for a in args) + sum(o.size * o.dtype.itemsize for o in outs)
@@ -33,7 +35,7 @@
         body,
         out_shape=outs,
         in_specs=specs,
-        out_specs=[VMEM] * len(outs),
+        out_specs=[place or VMEM] * len(outs),
         scratch_shapes=list(scratch),
         compiler_params=pltpu.CompilerParams(vmem_limit_bytes=mib * 1024 * 1024),
         cost_estimate=pl.CostEstimate(flops=flops, bytes_accessed=nbytes, transcendentals=0),
@@ -42,12 +44,12 @@
 
 
 def exchange(x, axis):
-    groups = {FAR: [[0, 2, 4, 6, 1, 3, 5, 7]], "narrow": [[0, 3, 1, 2]]}.get(axis)
+    groups = {FAR: [list(FAR_ORDER)], "narrow": [list(NARROW_ORDER)]}.get(axis)
     return lax.all_to_all(x, axis, split_axis=0, concat_axis=0, tiled=True, axis_index_groups=groups)
 
 
 def place_of(index):
-    return jnp.where(index == 0, 0, jnp.where(index == 3, 1, index + 1))
+    return sum(jnp.where(index == device, at, 0) for at, device in enumerate(NARROW_ORDER))
 
 
 def rows_body(part, top, hidden_hbm, routes_hbm, gates_hbm, out_ref, wide_ref, routes_ref, gates_ref, sems):
@@ -78,29 +80,36 @@
 
 def pack_body(n_nar, part, gate_hbm, up_hbm, down_hbm, *rest):
     outs = [rest[ORDER.index(k)] for k in range(n_nar)]
-    down_ref, turned_ref, sems, down_sem = rest[n_nar:]
+    down_ref, turned_ref, held_ref, sems, turned_sems, out_sems, down_sem = rest[n_nar:]
     units = gate_hbm.shape[2]
     me = lax.axis_index("narrow")
     fetch = pltpu.make_async_copy(down_hbm.at[0], down_ref, down_sem)
     fetch.start()
     copies = []
-    for k in range(n_nar):
+    for k in ORDER:
         to = lax.rem(me + k, n_nar)
         for i in range(2):
             rows = pl.ds(pl.multiple_of((to * 2 + i) * part, 64), part)
             for m, source in enumerate((gate_hbm, up_hbm)):
-                place = outs[k].at[i, :, m * units : (m + 1) * units]
+                place = held_ref.at[k, i, :, m * units : (m + 1) * units]
                 copies.append(pltpu.make_async_copy(source.at[0, rows], place, sems.at[k, i, m]))
     for copy in copies:
         copy.start()
     fetch.wait()
     turned_ref[...] = jnp.transpose(down_ref[...])
-    for k in range(n_nar):
+    sends = []
+    for at, k in enumerate(ORDER):
         to = lax.rem(me + k, n_nar)
+        for copy in copies[4 * at : 4 * at + 4]:
+            copy.wait()
+        sends.append(pltpu.make_async_copy(held_ref.at[k, :2], outs[k].at[:2], out_sems.at[k]))
+        sends[-1].start()
         for i in range(2):
             rows = pl.ds(pl.multiple_of((i * n_nar + to) * part, 64), part)
-            outs[k][2, :, i * units : (i + 1) * units] = turned_ref[rows]
-    for copy in copies:
+            held_ref[k, 2, :, i * units : (i + 1) * units] = turned_ref[rows]
+        sends.append(pltpu.make_async_copy(held_ref.at[k, 2], outs[k].at[2], turned_sems.at[k]))
+        sends[-1].start()
+    for copy in sends:
         copy.wait()
 
 
@@ -265,10 +274,14 @@
         [jax.ShapeDtypeStruct((3, part, 2 * units), BF16)] * n_nar,
         [HBM, HBM, HBM],
         [gate_proj, up_proj, down_proj],
+        place=HBM,
         scratch=[
             pltpu.VMEM((units, width), BF16),
             pltpu.VMEM((width, units), BF16),
+            pltpu.VMEM((n_nar, 3, part, 2 * units), BF16),
             pltpu.SemaphoreType.DMA((n_nar, 2, 2)),
+            pltpu.SemaphoreType.DMA((n_nar,)),
+            pltpu.SemaphoreType.DMA((n_nar,)),
             pltpu.SemaphoreType.DMA,
         ],
         mib=60,

time: 141 us -> 140 us (level)
  the two profiles are of different devices: /device:TPU:32 before, /device:TPU:64 now
where the time goes in v9:
time: 140 us
  blocking collectives  59.4 us (42%)
  starting transfers between devices  36 us (26%)
  waiting for transfers between devices  30.2 us (22%)
  Pallas kernels  13.9 us (10%)
    all_to_all x3, blocking collectives, exchange(): lax.all_to_all(x, axis, split_axis=0, concat_axis=0, tiled=True, axis_ind...  59.4 us
    all_to_all x3, starting transfers between devices, exchange(): lax.all_to_all(x, axis, split_axis=0, concat_axis=0, tiled=True, axis_ind...  24 us
    all_to_all x3, waiting for transfers between devices, exchange(): lax.all_to_all(x, axis, split_axis=0, concat_axis=0, tiled=True, axis_ind...  17.9 us
    pallas_call x11, Pallas kernels, call(): pl.pallas_call(body, out_shape=outs, in_specs=specs, out_specs=[place or...  13.9 us
    ppermute x3, waiting for transfers between devices, per_device(): lax.ppermute(parts[k], 'narrow', [(i, (i + k) % n_nar) for i in range(n_n...  12.3 us
    ppermute x3, starting transfers between devices, per_device(): lax.ppermute(parts[k], 'narrow', [(i, (i + k) % n_nar) for i in range(n_n...  12 us
  transfers between devices with their start and end apart: 6, of which 5 were waited for; matrix products, arithmetic and copies ran while one was open for 0% of the time, Pallas kernels for 4%

profile of v9, /device:TPU:64, one launch (start us, length us, event | category | flops | bytes accessed | tf_op | source)
XLA Modules:
  0.0 139.6 jit_solution(4336652925471417729)
XLA Ops:
  0.0 1.7 %shard_map.64 = bf16[8,32,512]{2,1,0:T(8,128)(2,1)} custom-call(bf16[32,3584]{1,0:T(8,128)(2,1)} %hidden_hbm.1, s32[8,32]{1,0:T(8,128)} %bitcast.2, f32[8,32]{1,0:T(8,128)} %bitcast.3), custom_call_target="tpu_custom_call" | custom-call | bytes 493568 | tf_op jit(solution)/shard_map/pallas_call | solution.py:34
  1.7 14.8 %all-to-all-start = ((bf16[8,32,512]{2,1,0:T(8,128)(2,1)}), bf16[8,32,512]{2,1,0:T(8,128)(2,1)S(1)}, u32[]{:S(2)}, u32[]{:S(2)}) async-start(bf16[8,32,512]{2,1,0:T(8,128)(2,1)} %shard_map.64), calls=%async_computation | async-start | bytes 524288 | tf_op jit(solution)/shard_map/all_to_all | solution.py:48
  16.5 3.8 %shard_map.66 = (bf16[3,448,256]{2,1,0:T(8,128)(2,1)}, bf16[3,448,256]{2,1,0:T(8,128)(2,1)}, bf16[3,448,256]{2,1,0:T(8,128)(2,1)}, bf16[3,448,256]{2,1,0:T(8,128)(2,1)}) custom-call(bf16[1,3584,128]{2,1,0:T(8,128)(2,1)} %gate_hbm.1, bf16[1,3584,128]{2,1,0:T(8,128)(2,1)} %up_hbm.1, bf16[1,128,3584]{2,1,0:T(8,128)(2,1)} %down_hbm.1), custom_call_target="tpu_custom_call" | custom-call | bytes 5505024 | tf_op jit(solution)/shard_map/pallas_call | solution.py:34
  20.3 4.9 %collective-permute-start = (bf16[3,448,256]{2,1,0:T(8,128)(2,1)}, bf16[3,448,256]{2,1,0:T(8,128)(2,1)S(1)}, u32[]{:S(2)}, u32[]{:S(2)}) collective-permute-start(bf16[3,448,256]{2,1,0:T(8,128)(2,1)} %get-tuple-element.9), channel_id=1, source_target_pairs={{0,2},{1,3},{2,0},{3,1},{4,6},{5,7},{6,4},{7,5},{8,10},{9,11},{10,... | collective-permute-start | bytes 2064392 | tf_op jit(solution)/shard_map/ppermute | solution.py:291
  25.3 2.5 %collective-permute-start.1 = (bf16[3,448,256]{2,1,0:T(8,128)(2,1)}, bf16[3,448,256]{2,1,0:T(8,128)(2,1)S(1)}, u32[]{:S(2)}, u32[]{:S(2)}) collective-permute-start(bf16[3,448,256]{2,1,0:T(8,128)(2,1)} %get-tuple-element.10), channel_id=1, source_target_pairs={{0,1},{1,2},{2,3},{3,0},{4,5},{5,6},{6,7},{7,4},{8,9},{9,10},{10,1... | collective-permute-start | bytes 2064392 | tf_op jit(solution)/shard_map/ppermute | solution.py:291
  27.8 4.6 %collective-permute-start.2 = (bf16[3,448,256]{2,1,0:T(8,128)(2,1)}, bf16[3,448,256]{2,1,0:T(8,128)(2,1)S(1)}, u32[]{:S(2)}, u32[]{:S(2)}) collective-permute-start(bf16[3,448,256]{2,1,0:T(8,128)(2,1)} %get-tuple-element.11), channel_id=1, source_target_pairs={{0,3},{1,0},{2,1},{3,2},{4,7},{5,4},{6,5},{7,6},{8,11},{9,8},{10,9... | collective-permute-start | bytes 2064392 | tf_op jit(solution)/shard_map/ppermute | solution.py:291
  32.3 3.3 %all-to-all-done.rows_ref = bf16[8,32,512]{2,1,0:T(8,128)(2,1)S(1)} async-done(((bf16[8,32,512]{2,1,0:T(8,128)(2,1)}), bf16[8,32,512]{2,1,0:T(8,128)(2,1)S(1)}, u32[]{:S(2)}, u32[]{:S(2)}) %all-to-all-start) | async-done | bytes 262176 | tf_op jit(solution)/shard_map/all_to_all | solution.py:48
  35.7 0.0 copy-start
  35.7 1.7 %shard_map.65._ = bf16[16,32,896]{2,1,0:T(8,128)(2,1)} custom-call(bf16[8,32,512]{2,1,0:T(8,128)(2,1)S(1)} %all-to-all-done.rows_ref), custom_call_target="tpu_custom_call" | custom-call | flops 117440512 | bytes 1179648 | tf_op jit(solution)/shard_map/pallas_call | solution.py:34
  37.3 0.0 copy-done
  37.3 0.0 copy-start.2
  37.3 5.5 %all-to-all-start.1 = ((bf16[16,32,896]{2,1,0:T(8,128)(2,1)}), bf16[16,32,896]{2,1,0:T(8,128)(2,1)}, u32[]{:S(2)}, u32[]{:S(2)}) async-start(bf16[16,32,896]{2,1,0:T(8,128)(2,1)} %shard_map.65._), calls=%async_computation.1 | async-start | bytes 1835008 | tf_op jit(solution)/shard_map/all_to_all | solution.py:48
  42.8 0.0 copy-done.2
  42.8 0.3 shard_map.67.refs_3_.rest_3_
  43.1 0.0 collective-permute-done.refs_0_.rest_0_
  43.1 12.2 %collective-permute-done.1.refs_1_.rest_1_ = bf16[3,448,256]{2,1,0:T(8,128)(2,1)S(1)} collective-permute-done((bf16[3,448,256]{2,1,0:T(8,128)(2,1)}, bf16[3,448,256]{2,1,0:T(8,128)(2,1)S(1)}, u32[]{:S(2)}, u32[]{:S(2)}) %collective-permute-start.1) | collective-permute-done | bytes 688160 | tf_op jit(solution)/shard_map/ppermute | solution.py:291
  55.3 0.1 collective-permute-done.2.refs_2_.rest_2_
  55.4 1.3 all-to-all-done.1.rows_ref
  56.7 2.4 %shard_map.69 = bf16[4,512,256]{2,1,0:T(8,128)(2,1)S(1)} custom-call(bf16[16,32,896]{2,1,0:T(8,128)(2,1)} %all-to-all-done.1.rows_ref, bf16[3,448,256]{2,1,0:T(8,128)(2,1)S(1)} %collective-permute-done.refs_0_.rest_0_, bf16[3,448,256]{2,1,0:T(8,128)(2,1)S(1)} %collective-permute-done.1.refs_1_.rest_1_, ...), custom_call_target="tpu_custom_call" | custom-call | flops 939524096 | bytes 4722688 | tf_op jit(solution)/shard_map/pallas_call | solution.py:34
  59.2 19.2 %all_to_all.30.acts_ref = bf16[4,512,256]{2,1,0:T(8,128)(2,1)S(1)} all-to-all(bf16[4,512,256]{2,1,0:T(8,128)(2,1)S(1)} %shard_map.69), channel_id=1, replica_groups={{0,1,3,2},{4,5,7,6},{8,9,11,10},{12,13,15,14},{16,17,19,18},{20,21,23,2..., dimensions={0} | all-to-all | bytes 2097152 | tf_op jit(solution)/shard_map/all_to_all | solution.py:48
  78.3 0.2 shard_map.70
  78.5 10.8 %all_to_all.31.inner_ref = bf16[4,512,128]{2,1,0:T(8,128)(2,1)S(1)} all-to-all(bf16[4,512,128]{2,1,0:T(8,128)(2,1)S(1)} %shard_map.70), channel_id=1, replica_groups={{0,1,3,2},{4,5,7,6},{8,9,11,10},{12,13,15,14},{16,17,19,18},{20,21,23,2..., dimensions={0} | all-to-all | bytes 1048576 | tf_op jit(solution)/shard_map/all_to_all | solution.py:48
  89.4 1.7 %shard_map.71 = bf16[16,32,896]{2,1,0:T(8,128)(2,1)} custom-call(bf16[4,512,128]{2,1,0:T(8,128)(2,1)S(1)} %all_to_all.31.inner_ref, bf16[3,448,256]{2,1,0:T(8,128)(2,1)S(1)} %collective-permute-done.refs_0_.rest_0_, bf16[3,448,256]{2,1,0:T(8,128)(2,1)S(1)} %collective-permute-done.1.refs_1_.rest_1_, ...), custom_call_target="tpu_custom_call" | custom-call | flops 469762048 | bytes 4194304 | tf_op jit(solution)/shard_map/pallas_call | solution.py:34
  91.1 0.0 copy-start.1
  91.1 3.8 %all-to-all-start.4 = ((bf16[16,32,896]{2,1,0:T(8,128)(2,1)}), bf16[16,32,896]{2,1,0:T(8,128)(2,1)S(1)}, u32[]{:S(2)}, u32[]{:S(2)}) async-start(bf16[16,32,896]{2,1,0:T(8,128)(2,1)} %shard_map.71), calls=%async_computation.4 | async-start | bytes 1835008 | tf_op jit(solution)/shard_map/all_to_all | solution.py:48
  94.8 0.0 copy-done.1
  94.9 0.5 shard_map.72.weight_ref
  95.4 13.3 %all-to-all-done.4.rows_ref = bf16[16,32,896]{2,1,0:T(8,128)(2,1)S(1)} async-done(((bf16[16,32,896]{2,1,0:T(8,128)(2,1)}), bf16[16,32,896]{2,1,0:T(8,128)(2,1)S(1)}, u32[]{:S(2)}, u32[]{:S(2)}) %all-to-all-start.4) | async-done | bytes 917536 | tf_op jit(solution)/shard_map/all_to_all | solution.py:48
  108.6 0.9 shard_map.73
  109.5 29.4 %all_to_all.32.sums_ref = bf16[8,16,896]{2,1,0:T(8,128)(2,1)S(1)} all-to-all(bf16[8,16,896]{2,1,0:T(8,128)(2,1)S(1)} %shard_map.73), channel_id=1, replica_groups={{0,64,16,80,32,96,48,112},{1,65,17,81,33,97,49,113},{2,66,18,82,34,98,5..., dimensions={0} | all-to-all | bytes 458752 | tf_op jit(solution)/shard_map/all_to_all | solution.py:48
  138.9 0.7 shard_map.74
  (1 shorter events, 0.0 us)
Async XLA Ops:
  1.7 33.9 %all-to-all-start = ((bf16[8,32,512]{2,1,0:T(8,128)(2,1)}), bf16[8,32,512]{2,1,0:T(8,128)(2,1)S(1)}, u32[]{:S(2)}, u32[]{:S(2)}) async-start(bf16[8,32,512]{2,1,0:T(8,128)(2,1)} %shard_map.64), calls=%async_computation | async-start | bytes 524288 | tf_op jit(solution)/shard_map/all_to_all | solution.py:48
  20.3 22.8 %collective-permute-start = (bf16[3,448,256]{2,1,0:T(8,128)(2,1)}, bf16[3,448,256]{2,1,0:T(8,128)(2,1)S(1)}, u32[]{:S(2)}, u32[]{:S(2)}) collective-permute-start(bf16[3,448,256]{2,1,0:T(8,128)(2,1)} %get-tuple-element.9), channel_id=1, source_target_pairs={{0,2},{1,3},{2,0},{3,1},{4,6},{5,7},{6,4},{7,5},{8,10},{9,11},{10,... | collective-permute-start | bytes 2064392 | tf_op jit(solution)/shard_map/ppermute | solution.py:291
  25.3 30.0 %collective-permute-start.1 = (bf16[3,448,256]{2,1,0:T(8,128)(2,1)}, bf16[3,448,256]{2,1,0:T(8,128)(2,1)S(1)}, u32[]{:S(2)}, u32[]{:S(2)}) collective-permute-start(bf16[3,448,256]{2,1,0:T(8,128)(2,1)} %get-tuple-element.10), channel_id=1, source_target_pairs={{0,1},{1,2},{2,3},{3,0},{4,5},{5,6},{6,7},{7,4},{8,9},{9,10},{10,1... | collective-permute-start | bytes 2064392 | tf_op jit(solution)/shard_map/ppermute | solution.py:291
  27.8 27.7 %collective-permute-start.2 = (bf16[3,448,256]{2,1,0:T(8,128)(2,1)}, bf16[3,448,256]{2,1,0:T(8,128)(2,1)S(1)}, u32[]{:S(2)}, u32[]{:S(2)}) collective-permute-start(bf16[3,448,256]{2,1,0:T(8,128)(2,1)} %get-tuple-element.11), channel_id=1, source_target_pairs={{0,3},{1,0},{2,1},{3,2},{4,7},{5,4},{6,5},{7,6},{8,11},{9,8},{10,9... | collective-permute-start | bytes 2064392 | tf_op jit(solution)/shard_map/ppermute | solution.py:291
  35.7 1.7 %copy-start = (bf16[8,32,512]{2,1,0:T(8,128)(2,1)}, bf16[8,32,512]{2,1,0:T(8,128)(2,1)S(1)}, u32[]{:S(2)}) copy-start(bf16[8,32,512]{2,1,0:T(8,128)(2,1)S(1)} %all-to-all-done.rows_ref) | copy-start | bytes 786436
  37.3 5.5 %copy-start.2 = (bf16[3,448,256]{2,1,0:T(8,128)(2,1)S(1)}, bf16[3,448,256]{2,1,0:T(8,128)(2,1)}, u32[]{:S(2)}) copy-start(bf16[3,448,256]{2,1,0:T(8,128)(2,1)} %get-tuple-element.12.part_hbm) | copy-start | bytes 2064388
  37.3 19.4 %all-to-all-start.1 = ((bf16[16,32,896]{2,1,0:T(8,128)(2,1)}), bf16[16,32,896]{2,1,0:T(8,128)(2,1)}, u32[]{:S(2)}, u32[]{:S(2)}) async-start(bf16[16,32,896]{2,1,0:T(8,128)(2,1)} %shard_map.65._), calls=%async_computation.1 | async-start | bytes 1835008 | tf_op jit(solution)/shard_map/all_to_all | solution.py:48
  91.1 3.8 %copy-start.1 = (bf16[8,32,512]{2,1,0:T(8,128)(2,1)S(1)}, bf16[8,32,512]{2,1,0:T(8,128)(2,1)}, u32[]{:S(2)}) copy-start(bf16[8,32,512]{2,1,0:T(8,128)(2,1)} %copy-done) | copy-start | bytes 786436
  91.1 17.6 %all-to-all-start.4 = ((bf16[16,32,896]{2,1,0:T(8,128)(2,1)}), bf16[16,32,896]{2,1,0:T(8,128)(2,1)S(1)}, u32[]{:S(2)}, u32[]{:S(2)}) async-start(bf16[16,32,896]{2,1,0:T(8,128)(2,1)} %shard_map.71), calls=%async_computation.4 | async-start | bytes 1835008 | tf_op jit(solution)/shard_map/all_to_all | solution.py:48

commit v10 on v9

--- a/solution.py
+++ b/solution.py
@@ -311,7 +311,7 @@
         scratch=[pltpu.SemaphoreType.DMA],
     )
     arrived = call(
-        arrived_body, jax.ShapeDtypeStruct((8, 128), F32), [ANY] * n_nar, [parts[k] for k in ORDER], flops=HOLD
+        arrived_body, jax.ShapeDtypeStruct((8, 128), F32), [ANY] * (n_nar + 1), [weight] + [parts[k] for k in ORDER], flops=HOLD
     )
     rows = exchange(picked, NEAR)
 

time: 140 us -> 140 us (level)
  blocking collectives: 59.4 us -> 77.9 us
  waiting for transfers between devices: 30.2 us -> 15.4 us
  starting transfers between devices: 36 us -> 32.1 us
    all_to_all x3 -> x4, blocking collectives: 59.4 us -> 77.9 us  [exchange(): lax.all_to_all(x, axis, split_axis=0, concat_axis=0, tiled=True, axis_ind...]
    all_to_all x3 -> x2, waiting for transfers between devices: 17.9 us -> 4.47 us  [exchange(): lax.all_to_all(x, axis, split_axis=0, concat_axis=0, tiled=True, axis_ind...]
    all_to_all x3 -> x2, starting transfers between devices: 24 us -> 20.1 us  [exchange(): lax.all_to_all(x, axis, split_axis=0, concat_axis=0, tiled=True, axis_ind...]
    ppermute x3, waiting for transfers between devices: 12.3 us -> 10.9 us  [per_device(): lax.ppermute(parts[k], 'narrow', [(i, (i + k) % n_nar) for i in range(n_n...]
  transfers between devices with their start and end apart: 6 -> 5, of which waited for: 5 -> 4; matrix products, arithmetic and copies ran while one was open for 0% -> 0% of each run, Pallas kernels for 4% -> 4%
where the time goes in v10:
time: 140 us
  blocking collectives  77.9 us (56%)
  starting transfers between devices  32.1 us (23%)
  waiting for transfers between devices  15.4 us (11%)
  Pallas kernels  12.9 us (9%)
    all_to_all x4, blocking collectives, exchange(): lax.all_to_all(x, axis, split_axis=0, concat_axis=0, tiled=True, axis_ind...  77.9 us
    all_to_all x2, starting transfers between devices, exchange(): lax.all_to_all(x, axis, split_axis=0, concat_axis=0, tiled=True, axis_ind...  20.1 us
    pallas_call x11, Pallas kernels, call(): pl.pallas_call(body, out_shape=outs, in_specs=specs, out_specs=[place or...  12.9 us
    ppermute x3, starting transfers between devices, per_device(): lax.ppermute(parts[k], 'narrow', [(i, (i + k) % n_nar) for i in range(n_n...  12 us
    ppermute x3, waiting for transfers between devices, per_device(): lax.ppermute(parts[k], 'narrow', [(i, (i + k) % n_nar) for i in range(n_n...  10.9 us
    all_to_all x2, waiting for transfers between devices, exchange(): lax.all_to_all(x, axis, split_axis=0, concat_axis=0, tiled=True, axis_ind...  4.47 us
  transfers between devices with their start and end apart: 5, of which 4 were waited for; matrix products, arithmetic and copies ran while one was open for 0% of the time, Pallas kernels for 4%

profile of v10, /device:TPU:64, one launch (start us, length us, event | category | flops | bytes accessed | tf_op | source)
XLA Modules:
  0.0 139.5 jit_solution(10299384158091073662)
XLA Ops:
  0.0 1.7 %shard_map.64 = bf16[8,32,512]{2,1,0:T(8,128)(2,1)} custom-call(bf16[32,3584]{1,0:T(8,128)(2,1)} %hidden_hbm.1, s32[8,32]{1,0:T(8,128)} %bitcast.2, f32[8,32]{1,0:T(8,128)} %bitcast.3), custom_call_target="tpu_custom_call" | custom-call | bytes 493568 | tf_op jit(solution)/shard_map/pallas_call | solution.py:34
  1.7 14.8 %all-to-all-start = ((bf16[8,32,512]{2,1,0:T(8,128)(2,1)}), bf16[8,32,512]{2,1,0:T(8,128)(2,1)S(1)}, u32[]{:S(2)}, u32[]{:S(2)}) async-start(bf16[8,32,512]{2,1,0:T(8,128)(2,1)} %shard_map.64), calls=%async_computation | async-start | bytes 524288 | tf_op jit(solution)/shard_map/all_to_all | solution.py:48
  16.5 3.8 %shard_map.66 = (bf16[3,448,256]{2,1,0:T(8,128)(2,1)}, bf16[3,448,256]{2,1,0:T(8,128)(2,1)}, bf16[3,448,256]{2,1,0:T(8,128)(2,1)}, bf16[3,448,256]{2,1,0:T(8,128)(2,1)}) custom-call(bf16[1,3584,128]{2,1,0:T(8,128)(2,1)} %gate_hbm.1, bf16[1,3584,128]{2,1,0:T(8,128)(2,1)} %up_hbm.1, bf16[1,128,3584]{2,1,0:T(8,128)(2,1)} %down_hbm.1), custom_call_target="tpu_custom_call" | custom-call | bytes 5505024 | tf_op jit(solution)/shard_map/pallas_call | solution.py:34
  20.3 4.9 %collective-permute-start = (bf16[3,448,256]{2,1,0:T(8,128)(2,1)}, bf16[3,448,256]{2,1,0:T(8,128)(2,1)S(1)}, u32[]{:S(2)}, u32[]{:S(2)}) collective-permute-start(bf16[3,448,256]{2,1,0:T(8,128)(2,1)} %get-tuple-element.9), channel_id=1, source_target_pairs={{0,2},{1,3},{2,0},{3,1},{4,6},{5,7},{6,4},{7,5},{8,10},{9,11},{10,... | collective-permute-start | bytes 2064392 | tf_op jit(solution)/shard_map/ppermute | solution.py:291
  25.2 2.5 %collective-permute-start.1 = (bf16[3,448,256]{2,1,0:T(8,128)(2,1)}, bf16[3,448,256]{2,1,0:T(8,128)(2,1)S(1)}, u32[]{:S(2)}, u32[]{:S(2)}) collective-permute-start(bf16[3,448,256]{2,1,0:T(8,128)(2,1)} %get-tuple-element.10), channel_id=1, source_target_pairs={{0,1},{1,2},{2,3},{3,0},{4,5},{5,6},{6,7},{7,4},{8,9},{9,10},{10,1... | collective-permute-start | bytes 2064392 | tf_op jit(solution)/shard_map/ppermute | solution.py:291
  27.8 4.6 %collective-permute-start.2 = (bf16[3,448,256]{2,1,0:T(8,128)(2,1)}, bf16[3,448,256]{2,1,0:T(8,128)(2,1)S(1)}, u32[]{:S(2)}, u32[]{:S(2)}) collective-permute-start(bf16[3,448,256]{2,1,0:T(8,128)(2,1)} %get-tuple-element.11), channel_id=1, source_target_pairs={{0,3},{1,0},{2,1},{3,2},{4,7},{5,4},{6,5},{7,6},{8,11},{9,8},{10,9... | collective-permute-start | bytes 2064392 | tf_op jit(solution)/shard_map/ppermute | solution.py:291
  32.3 3.3 %all-to-all-done.rows_ref = bf16[8,32,512]{2,1,0:T(8,128)(2,1)S(1)} async-done(((bf16[8,32,512]{2,1,0:T(8,128)(2,1)}), bf16[8,32,512]{2,1,0:T(8,128)(2,1)S(1)}, u32[]{:S(2)}, u32[]{:S(2)}) %all-to-all-start) | async-done | bytes 262176 | tf_op jit(solution)/shard_map/all_to_all | solution.py:48
  35.7 1.6 %shard_map.65._ = bf16[16,32,896]{2,1,0:T(8,128)(2,1)} custom-call(bf16[8,32,512]{2,1,0:T(8,128)(2,1)S(1)} %all-to-all-done.rows_ref), custom_call_target="tpu_custom_call" | custom-call | flops 117440512 | bytes 1179648 | tf_op jit(solution)/shard_map/pallas_call | solution.py:34
  37.3 5.3 %all-to-all-start.1 = ((bf16[16,32,896]{2,1,0:T(8,128)(2,1)}), bf16[16,32,896]{2,1,0:T(8,128)(2,1)}, u32[]{:S(2)}, u32[]{:S(2)}) async-start(bf16[16,32,896]{2,1,0:T(8,128)(2,1)} %shard_map.65._), calls=%async_computation.1 | async-start | bytes 1835008 | tf_op jit(solution)/shard_map/all_to_all | solution.py:48
  42.6 0.0 copy-start
  42.7 1.1 copy-done
  43.7 0.3 shard_map.67.refs_4_.rest_3_
  44.0 0.5 shard_map.68.refs_0_.weight_ref
  44.5 0.0 collective-permute-done.refs_1_.rest_0_
  44.5 10.8 %collective-permute-done.1.refs_2_.rest_1_ = bf16[3,448,256]{2,1,0:T(8,128)(2,1)S(1)} collective-permute-done((bf16[3,448,256]{2,1,0:T(8,128)(2,1)}, bf16[3,448,256]{2,1,0:T(8,128)(2,1)S(1)}, u32[]{:S(2)}, u32[]{:S(2)}) %collective-permute-start.1) | collective-permute-done | bytes 688160 | tf_op jit(solution)/shard_map/ppermute | solution.py:291
  55.3 0.1 collective-permute-done.2.refs_3_.rest_2_
  55.4 1.1 all-to-all-done.1.rows_ref
  56.6 2.4 %shard_map.70 = bf16[4,512,256]{2,1,0:T(8,128)(2,1)S(1)} custom-call(bf16[16,32,896]{2,1,0:T(8,128)(2,1)} %all-to-all-done.1.rows_ref, bf16[3,448,256]{2,1,0:T(8,128)(2,1)S(1)} %collective-permute-done.refs_1_.rest_0_, bf16[3,448,256]{2,1,0:T(8,128)(2,1)S(1)} %collective-permute-done.1.refs_2_.rest_1_, ...), custom_call_target="tpu_custom_call" | custom-call | flops 939524096 | bytes 4722688 | tf_op jit(solution)/shard_map/pallas_call | solution.py:34
  59.0 19.2 %all_to_all.30.acts_ref = bf16[4,512,256]{2,1,0:T(8,128)(2,1)S(1)} all-to-all(bf16[4,512,256]{2,1,0:T(8,128)(2,1)S(1)} %shard_map.70), channel_id=1, replica_groups={{0,1,3,2},{4,5,7,6},{8,9,11,10},{12,13,15,14},{16,17,19,18},{20,21,23,2..., dimensions={0} | all-to-all | bytes 2097152 | tf_op jit(solution)/shard_map/all_to_all | solution.py:48
  78.2 0.2 shard_map.71
  78.4 10.8 %all_to_all.31.inner_ref = bf16[4,512,128]{2,1,0:T(8,128)(2,1)S(1)} all-to-all(bf16[4,512,128]{2,1,0:T(8,128)(2,1)S(1)} %shard_map.71), channel_id=1, replica_groups={{0,1,3,2},{4,5,7,6},{8,9,11,10},{12,13,15,14},{16,17,19,18},{20,21,23,2..., dimensions={0} | all-to-all | bytes 1048576 | tf_op jit(solution)/shard_map/all_to_all | solution.py:48
  89.2 0.8 shard_map.72
  90.0 17.2 %all_to_all.32.rows_ref = bf16[16,32,896]{2,1,0:T(8,128)(2,1)S(1)} all-to-all(bf16[16,32,896]{2,1,0:T(8,128)(2,1)S(1)} %shard_map.72), channel_id=1, replica_groups=mesh['grp'=2,'ylo'=2,'zfar'=8,'znear'=2,'core'=2,'narrow'=4] {'grp','cor..., dimensions={0} | all-to-all | bytes 1835008 | tf_op jit(solution)/shard_map/all_to_all | solution.py:48
  107.2 0.9 shard_map.73
  108.1 30.8 %all_to_all.33.sums_ref = bf16[8,16,896]{2,1,0:T(8,128)(2,1)S(1)} all-to-all(bf16[8,16,896]{2,1,0:T(8,128)(2,1)S(1)} %shard_map.73), channel_id=1, replica_groups={{0,64,16,80,32,96,48,112},{1,65,17,81,33,97,49,113},{2,66,18,82,34,98,5..., dimensions={0} | all-to-all | bytes 458752 | tf_op jit(solution)/shard_map/all_to_all | solution.py:48
  138.8 0.7 shard_map.74
  (1 shorter events, 0.0 us)
Async XLA Ops:
  1.7 33.9 %all-to-all-start = ((bf16[8,32,512]{2,1,0:T(8,128)(2,1)}), bf16[8,32,512]{2,1,0:T(8,128)(2,1)S(1)}, u32[]{:S(2)}, u32[]{:S(2)}) async-start(bf16[8,32,512]{2,1,0:T(8,128)(2,1)} %shard_map.64), calls=%async_computation | async-start | bytes 524288 | tf_op jit(solution)/shard_map/all_to_all | solution.py:48
  20.3 24.2 %collective-permute-start = (bf16[3,448,256]{2,1,0:T(8,128)(2,1)}, bf16[3,448,256]{2,1,0:T(8,128)(2,1)S(1)}, u32[]{:S(2)}, u32[]{:S(2)}) collective-permute-start(bf16[3,448,256]{2,1,0:T(8,128)(2,1)} %get-tuple-element.9), channel_id=1, source_target_pairs={{0,2},{1,3},{2,0},{3,1},{4,6},{5,7},{6,4},{7,5},{8,10},{9,11},{10,... | collective-permute-start | bytes 2064392 | tf_op jit(solution)/shard_map/ppermute | solution.py:291
  25.2 30.0 %collective-permute-start.1 = (bf16[3,448,256]{2,1,0:T(8,128)(2,1)}, bf16[3,448,256]{2,1,0:T(8,128)(2,1)S(1)}, u32[]{:S(2)}, u32[]{:S(2)}) collective-permute-start(bf16[3,448,256]{2,1,0:T(8,128)(2,1)} %get-tuple-element.10), channel_id=1, source_target_pairs={{0,1},{1,2},{2,3},{3,0},{4,5},{5,6},{6,7},{7,4},{8,9},{9,10},{10,1... | collective-permute-start | bytes 2064392 | tf_op jit(solution)/shard_map/ppermute | solution.py:291
  27.8 27.7 %collective-permute-start.2 = (bf16[3,448,256]{2,1,0:T(8,128)(2,1)}, bf16[3,448,256]{2,1,0:T(8,128)(2,1)S(1)}, u32[]{:S(2)}, u32[]{:S(2)}) collective-permute-start(bf16[3,448,256]{2,1,0:T(8,128)(2,1)} %get-tuple-element.11), channel_id=1, source_target_pairs={{0,3},{1,0},{2,1},{3,2},{4,7},{5,4},{6,5},{7,6},{8,11},{9,8},{10,9... | collective-permute-start | bytes 2064392 | tf_op jit(solution)/shard_map/ppermute | solution.py:291
  37.3 19.3 %all-to-all-start.1 = ((bf16[16,32,896]{2,1,0:T(8,128)(2,1)}), bf16[16,32,896]{2,1,0:T(8,128)(2,1)}, u32[]{:S(2)}, u32[]{:S(2)}) async-start(bf16[16,32,896]{2,1,0:T(8,128)(2,1)} %shard_map.65._), calls=%async_computation.1 | async-start | bytes 1835008 | tf_op jit(solution)/shard_map/all_to_all | solution.py:48
  42.6 1.1 copy-start

commit v11 on v9

--- a/solution.py
+++ b/solution.py
@@ -18,7 +18,7 @@
 LANES = 512
 HOLD = 200 * 10**9
 ORDER = (2, 1, 3, 0)
-FAR_ORDER = (0, 4, 1, 5, 2, 6, 3, 7)
+FAR_ORDER = (0, 6, 3, 1, 7, 4, 2, 5)
 NARROW_ORDER = (0, 1, 3, 2)
 
 VMEM = pl.BlockSpec(memory_space=pltpu.VMEM)

time: 140 us -> 141 us (level)
  the two profiles are of different devices: /device:TPU:64 before, /device:TPU:33 now
where the time goes in v11:
time: 141 us
  blocking collectives  57.9 us (41%)
  starting transfers between devices  39.2 us (28%)
  waiting for transfers between devices  29.6 us (21%)
  Pallas kernels  13.9 us (10%)
    all_to_all x3, blocking collectives, exchange(): lax.all_to_all(x, axis, split_axis=0, concat_axis=0, tiled=True, axis_ind...  57.9 us
    all_to_all x3, starting transfers between devices, exchange(): lax.all_to_all(x, axis, split_axis=0, concat_axis=0, tiled=True, axis_ind...  28 us
    all_to_all x3, waiting for transfers between devices, exchange(): lax.all_to_all(x, axis, split_axis=0, concat_axis=0, tiled=True, axis_ind...  17.9 us
    pallas_call x11, Pallas kernels, call(): pl.pallas_call(body, out_shape=outs, in_specs=specs, out_specs=[place or...  13.9 us
    ppermute x3, waiting for transfers between devices, per_device(): lax.ppermute(parts[k], 'narrow', [(i, (i + k) % n_nar) for i in range(n_n...  11.6 us
    ppermute x3, starting transfers between devices, per_device(): lax.ppermute(parts[k], 'narrow', [(i, (i + k) % n_nar) for i in range(n_n...  11.1 us
  transfers between devices with their start and end apart: 6, of which 4 were waited for; matrix products, arithmetic and copies ran while one was open for 0% of the time, Pallas kernels for 4%

profile of v11, /device:TPU:33, one launch (start us, length us, event | category | flops | bytes accessed | tf_op | source)
XLA Modules:
  0.0 140.6 jit_solution(11524660743579206050)
XLA Ops:
  0.0 1.7 %shard_map.64 = bf16[8,32,512]{2,1,0:T(8,128)(2,1)} custom-call(bf16[32,3584]{1,0:T(8,128)(2,1)} %hidden_hbm.1, s32[8,32]{1,0:T(8,128)} %bitcast.2, f32[8,32]{1,0:T(8,128)} %bitcast.3), custom_call_target="tpu_custom_call" | custom-call | bytes 493568 | tf_op jit(solution)/shard_map/pallas_call | solution.py:34
  1.7 13.9 %all-to-all-start = ((bf16[8,32,512]{2,1,0:T(8,128)(2,1)}), bf16[8,32,512]{2,1,0:T(8,128)(2,1)S(1)}, u32[]{:S(2)}, u32[]{:S(2)}) async-start(bf16[8,32,512]{2,1,0:T(8,128)(2,1)} %shard_map.64), calls=%async_computation | async-start | bytes 524288 | tf_op jit(solution)/shard_map/all_to_all | solution.py:48
  15.6 3.9 %shard_map.66 = (bf16[3,448,256]{2,1,0:T(8,128)(2,1)}, bf16[3,448,256]{2,1,0:T(8,128)(2,1)}, bf16[3,448,256]{2,1,0:T(8,128)(2,1)}, bf16[3,448,256]{2,1,0:T(8,128)(2,1)}) custom-call(bf16[1,3584,128]{2,1,0:T(8,128)(2,1)} %gate_hbm.1, bf16[1,3584,128]{2,1,0:T(8,128)(2,1)} %up_hbm.1, bf16[1,128,3584]{2,1,0:T(8,128)(2,1)} %down_hbm.1), custom_call_target="tpu_custom_call" | custom-call | bytes 5505024 | tf_op jit(solution)/shard_map/pallas_call | solution.py:34
  19.5 4.7 %collective-permute-start = (bf16[3,448,256]{2,1,0:T(8,128)(2,1)}, bf16[3,448,256]{2,1,0:T(8,128)(2,1)S(1)}, u32[]{:S(2)}, u32[]{:S(2)}) collective-permute-start(bf16[3,448,256]{2,1,0:T(8,128)(2,1)} %get-tuple-element.9), channel_id=1, source_target_pairs={{0,2},{1,3},{2,0},{3,1},{4,6},{5,7},{6,4},{7,5},{8,10},{9,11},{10,... | collective-permute-start | bytes 2064392 | tf_op jit(solution)/shard_map/ppermute | solution.py:291
  24.2 2.2 %collective-permute-start.1 = (bf16[3,448,256]{2,1,0:T(8,128)(2,1)}, bf16[3,448,256]{2,1,0:T(8,128)(2,1)S(1)}, u32[]{:S(2)}, u32[]{:S(2)}) collective-permute-start(bf16[3,448,256]{2,1,0:T(8,128)(2,1)} %get-tuple-element.10), channel_id=1, source_target_pairs={{0,1},{1,2},{2,3},{3,0},{4,5},{5,6},{6,7},{7,4},{8,9},{9,10},{10,1... | collective-permute-start | bytes 2064392 | tf_op jit(solution)/shard_map/ppermute | solution.py:291
  26.4 4.3 %collective-permute-start.2 = (bf16[3,448,256]{2,1,0:T(8,128)(2,1)}, bf16[3,448,256]{2,1,0:T(8,128)(2,1)S(1)}, u32[]{:S(2)}, u32[]{:S(2)}) collective-permute-start(bf16[3,448,256]{2,1,0:T(8,128)(2,1)} %get-tuple-element.11), channel_id=1, source_target_pairs={{0,3},{1,0},{2,1},{3,2},{4,7},{5,4},{6,5},{7,6},{8,11},{9,8},{10,9... | collective-permute-start | bytes 2064392 | tf_op jit(solution)/shard_map/ppermute | solution.py:291
  30.7 3.5 %all-to-all-done.rows_ref = bf16[8,32,512]{2,1,0:T(8,128)(2,1)S(1)} async-done(((bf16[8,32,512]{2,1,0:T(8,128)(2,1)}), bf16[8,32,512]{2,1,0:T(8,128)(2,1)S(1)}, u32[]{:S(2)}, u32[]{:S(2)}) %all-to-all-start) | async-done | bytes 262176 | tf_op jit(solution)/shard_map/all_to_all | solution.py:48
  34.1 0.0 copy-start
  34.1 1.7 %shard_map.65._ = bf16[16,32,896]{2,1,0:T(8,128)(2,1)} custom-call(bf16[8,32,512]{2,1,0:T(8,128)(2,1)S(1)} %all-to-all-done.rows_ref), custom_call_target="tpu_custom_call" | custom-call | flops 117440512 | bytes 1179648 | tf_op jit(solution)/shard_map/pallas_call | solution.py:34
  35.8 0.0 copy-done
  35.8 0.0 copy-start.2
  35.8 7.6 %all-to-all-start.1 = ((bf16[16,32,896]{2,1,0:T(8,128)(2,1)}), bf16[16,32,896]{2,1,0:T(8,128)(2,1)}, u32[]{:S(2)}, u32[]{:S(2)}) async-start(bf16[16,32,896]{2,1,0:T(8,128)(2,1)} %shard_map.65._), calls=%async_computation.1 | async-start | bytes 1835008 | tf_op jit(solution)/shard_map/all_to_all | solution.py:48
  43.4 0.0 copy-done.2
  43.4 0.3 shard_map.67.refs_3_.rest_3_
  43.7 0.0 collective-permute-done.refs_0_.rest_0_
  43.7 11.6 %collective-permute-done.1.refs_1_.rest_1_ = bf16[3,448,256]{2,1,0:T(8,128)(2,1)S(1)} collective-permute-done((bf16[3,448,256]{2,1,0:T(8,128)(2,1)}, bf16[3,448,256]{2,1,0:T(8,128)(2,1)S(1)}, u32[]{:S(2)}, u32[]{:S(2)}) %collective-permute-start.1) | collective-permute-done | bytes 688160 | tf_op jit(solution)/shard_map/ppermute | solution.py:291
  55.3 0.0 collective-permute-done.2.refs_2_.rest_2_
  55.3 1.6 %all-to-all-done.1.rows_ref = bf16[16,32,896]{2,1,0:T(8,128)(2,1)} async-done(((bf16[16,32,896]{2,1,0:T(8,128)(2,1)}), bf16[16,32,896]{2,1,0:T(8,128)(2,1)}, u32[]{:S(2)}, u32[]{:S(2)}) %all-to-all-start.1) | async-done | bytes 917536 | tf_op jit(solution)/shard_map/all_to_all | solution.py:48
  56.9 2.4 %shard_map.69 = bf16[4,512,256]{2,1,0:T(8,128)(2,1)S(1)} custom-call(bf16[16,32,896]{2,1,0:T(8,128)(2,1)} %all-to-all-done.1.rows_ref, bf16[3,448,256]{2,1,0:T(8,128)(2,1)S(1)} %collective-permute-done.refs_0_.rest_0_, bf16[3,448,256]{2,1,0:T(8,128)(2,1)S(1)} %collective-permute-done.1.refs_1_.rest_1_, ...), custom_call_target="tpu_custom_call" | custom-call | flops 939524096 | bytes 4722688 | tf_op jit(solution)/shard_map/pallas_call | solution.py:34
  59.3 17.9 %all_to_all.30.acts_ref = bf16[4,512,256]{2,1,0:T(8,128)(2,1)S(1)} all-to-all(bf16[4,512,256]{2,1,0:T(8,128)(2,1)S(1)} %shard_map.69), channel_id=1, replica_groups={{0,1,3,2},{4,5,7,6},{8,9,11,10},{12,13,15,14},{16,17,19,18},{20,21,23,2..., dimensions={0} | all-to-all | bytes 2097152 | tf_op jit(solution)/shard_map/all_to_all | solution.py:48
  77.3 0.2 shard_map.70
  77.4 10.0 %all_to_all.31.inner_ref = bf16[4,512,128]{2,1,0:T(8,128)(2,1)S(1)} all-to-all(bf16[4,512,128]{2,1,0:T(8,128)(2,1)S(1)} %shard_map.70), channel_id=1, replica_groups={{0,1,3,2},{4,5,7,6},{8,9,11,10},{12,13,15,14},{16,17,19,18},{20,21,23,2..., dimensions={0} | all-to-all | bytes 1048576 | tf_op jit(solution)/shard_map/all_to_all | solution.py:48
  87.4 1.7 %shard_map.71 = bf16[16,32,896]{2,1,0:T(8,128)(2,1)} custom-call(bf16[4,512,128]{2,1,0:T(8,128)(2,1)S(1)} %all_to_all.31.inner_ref, bf16[3,448,256]{2,1,0:T(8,128)(2,1)S(1)} %collective-permute-done.refs_0_.rest_0_, bf16[3,448,256]{2,1,0:T(8,128)(2,1)S(1)} %collective-permute-done.1.refs_1_.rest_1_, ...), custom_call_target="tpu_custom_call" | custom-call | flops 469762048 | bytes 4194304 | tf_op jit(solution)/shard_map/pallas_call | solution.py:34
  89.2 0.0 copy-start.1
  89.2 6.5 %all-to-all-start.4 = ((bf16[16,32,896]{2,1,0:T(8,128)(2,1)}), bf16[16,32,896]{2,1,0:T(8,128)(2,1)S(1)}, u32[]{:S(2)}, u32[]{:S(2)}) async-start(bf16[16,32,896]{2,1,0:T(8,128)(2,1)} %shard_map.71), calls=%async_computation.4 | async-start | bytes 1835008 | tf_op jit(solution)/shard_map/all_to_all | solution.py:48
  95.7 0.0 copy-done.1
  95.7 0.5 shard_map.72.weight_ref
  96.2 12.9 %all-to-all-done.4.rows_ref = bf16[16,32,896]{2,1,0:T(8,128)(2,1)S(1)} async-done(((bf16[16,32,896]{2,1,0:T(8,128)(2,1)}), bf16[16,32,896]{2,1,0:T(8,128)(2,1)S(1)}, u32[]{:S(2)}, u32[]{:S(2)}) %all-to-all-start.4) | async-done | bytes 917536 | tf_op jit(solution)/shard_map/all_to_all | solution.py:48
  109.1 0.9 shard_map.73
  110.0 30.0 %all_to_all.32.sums_ref = bf16[8,16,896]{2,1,0:T(8,128)(2,1)S(1)} all-to-all(bf16[8,16,896]{2,1,0:T(8,128)(2,1)S(1)} %shard_map.73), channel_id=1, replica_groups={{0,96,48,16,112,64,32,80},{1,97,49,17,113,65,33,81},{2,98,50,18,114,66,..., dimensions={0} | all-to-all | bytes 458752 | tf_op jit(solution)/shard_map/all_to_all | solution.py:48
  139.9 0.7 shard_map.74
  (1 shorter events, 0.0 us)
Async XLA Ops:
  1.7 32.4 %all-to-all-start = ((bf16[8,32,512]{2,1,0:T(8,128)(2,1)}), bf16[8,32,512]{2,1,0:T(8,128)(2,1)S(1)}, u32[]{:S(2)}, u32[]{:S(2)}) async-start(bf16[8,32,512]{2,1,0:T(8,128)(2,1)} %shard_map.64), calls=%async_computation | async-start | bytes 524288 | tf_op jit(solution)/shard_map/all_to_all | solution.py:48
  19.5 24.2 %collective-permute-start = (bf16[3,448,256]{2,1,0:T(8,128)(2,1)}, bf16[3,448,256]{2,1,0:T(8,128)(2,1)S(1)}, u32[]{:S(2)}, u32[]{:S(2)}) collective-permute-start(bf16[3,448,256]{2,1,0:T(8,128)(2,1)} %get-tuple-element.9), channel_id=1, source_target_pairs={{0,2},{1,3},{2,0},{3,1},{4,6},{5,7},{6,4},{7,5},{8,10},{9,11},{10,... | collective-permute-start | bytes 2064392 | tf_op jit(solution)/shard_map/ppermute | solution.py:291
  24.2 31.2 %collective-permute-start.1 = (bf16[3,448,256]{2,1,0:T(8,128)(2,1)}, bf16[3,448,256]{2,1,0:T(8,128)(2,1)S(1)}, u32[]{:S(2)}, u32[]{:S(2)}) collective-permute-start(bf16[3,448,256]{2,1,0:T(8,128)(2,1)} %get-tuple-element.10), channel_id=1, source_target_pairs={{0,1},{1,2},{2,3},{3,0},{4,5},{5,6},{6,7},{7,4},{8,9},{9,10},{10,1... | collective-permute-start | bytes 2064392 | tf_op jit(solution)/shard_map/ppermute | solution.py:291
  26.4 28.9 %collective-permute-start.2 = (bf16[3,448,256]{2,1,0:T(8,128)(2,1)}, bf16[3,448,256]{2,1,0:T(8,128)(2,1)S(1)}, u32[]{:S(2)}, u32[]{:S(2)}) collective-permute-start(bf16[3,448,256]{2,1,0:T(8,128)(2,1)} %get-tuple-element.11), channel_id=1, source_target_pairs={{0,3},{1,0},{2,1},{3,2},{4,7},{5,4},{6,5},{7,6},{8,11},{9,8},{10,9... | collective-permute-start | bytes 2064392 | tf_op jit(solution)/shard_map/ppermute | solution.py:291
  34.1 1.7 %copy-start = (bf16[8,32,512]{2,1,0:T(8,128)(2,1)}, bf16[8,32,512]{2,1,0:T(8,128)(2,1)S(1)}, u32[]{:S(2)}) copy-start(bf16[8,32,512]{2,1,0:T(8,128)(2,1)S(1)} %all-to-all-done.rows_ref) | copy-start | bytes 786436
  35.8 7.6 %copy-start.2 = (bf16[3,448,256]{2,1,0:T(8,128)(2,1)S(1)}, bf16[3,448,256]{2,1,0:T(8,128)(2,1)}, u32[]{:S(2)}) copy-start(bf16[3,448,256]{2,1,0:T(8,128)(2,1)} %get-tuple-element.12.part_hbm) | copy-start | bytes 2064388
  35.8 21.1 %all-to-all-start.1 = ((bf16[16,32,896]{2,1,0:T(8,128)(2,1)}), bf16[16,32,896]{2,1,0:T(8,128)(2,1)}, u32[]{:S(2)}, u32[]{:S(2)}) async-start(bf16[16,32,896]{2,1,0:T(8,128)(2,1)} %shard_map.65._), calls=%async_computation.1 | async-start | bytes 1835008 | tf_op jit(solution)/shard_map/all_to_all | solution.py:48
  89.2 6.5 %copy-start.1 = (bf16[8,32,512]{2,1,0:T(8,128)(2,1)S(1)}, bf16[8,32,512]{2,1,0:T(8,128)(2,1)}, u32[]{:S(2)}) copy-start(bf16[8,32,512]{2,1,0:T(8,128)(2,1)} %copy-done) | copy-start | bytes 786436
  89.2 19.9 %all-to-all-start.4 = ((bf16[16,32,896]{2,1,0:T(8,128)(2,1)}), bf16[16,32,896]{2,1,0:T(8,128)(2,1)S(1)}, u32[]{:S(2)}, u32[]{:S(2)}) async-start(bf16[16,32,896]{2,1,0:T(8,128)(2,1)} %shard_map.71), calls=%async_computation.4 | async-start | bytes 1835008 | tf_op jit(solution)/shard_map/all_to_all | solution.py:48
